TPU v7x, 32 devices: a whole 2x2x4 slice. The times are simulated.
32 devices in a mesh: dp: 4 (over y, x), expert: 8 (over z, core).
Axes of the slice: x: 2, y: 2, z: 4, core: 2. Of those that a mesh axis runs over, the one named last changes fastest.
Arguments:
- tokens: bfloat16 [4096, 1024], P(('dp', 'expert')), may hold values from -6 to 6
- cotangent: bfloat16 [4096, 1024], P(('dp', 'expert')), may hold values from -6 to 6
- gain_attention: float32 [1024], replicated, may hold values from 0.5 to 1.5
- gain_feedforward: float32 [1024], replicated, may hold values from 0.5 to 1.5
- query_weight: bfloat16 [1024, 512], replicated, may hold values from -0.1875 to 0.1875
- key_weight: bfloat16 [1024, 512], replicated, may hold values from -0.1875 to 0.1875
- value_weight: bfloat16 [1024, 2560], replicated, may hold values from -0.1875 to 0.1875
- output_weight: bfloat16 [2560, 1024], replicated, may hold values from -2 to 2
- value_router: bfloat16 [1024, 20], replicated, may hold values from -0.125 to 0.125
- output_router: bfloat16 [1024, 20], replicated, may hold values from -0.125 to 0.125
- expert_router: bfloat16 [1024, 96], replicated, may hold values from -0.09375 to 0.09375
- expert_first: bfloat16 [96, 1024, 128], P(('dp', 'expert')), may hold values from -0.1875 to 0.1875
- expert_second: bfloat16 [96, 128, 1024], P(('dp', 'expert')), may hold values from -0.5 to 0.5
- segments: int32 [32, 128], P(('dp', 'expert')), may hold values from 0 to 3, never falling along the last dimension, each value on 1 to 64 neighbouring positions
- value_ids: int32 [1, 4096, 4, 2], P(None, ('dp', 'expert')), may hold values from 0 to 4, all different within a row
- output_ids: int32 [1, 4096, 4, 2], P(None, ('dp', 'expert')), may hold values from 0 to 4, all different within a row
- ffn_ids: int32 [1, 4096, 16], P(None, ('dp', 'expert')), may hold values from 0 to 95, all different within a row; in each aligned block of 128 rows (0 to 127, 128 to 255, ..., all dimensions but the last counted through in order) at most 32 rows name the same one
Outputs:
- block_output: bfloat16 [4096, 1024], P(('dp', 'expert'))
- input_gradient: float32 [4096, 1024], P(('dp', 'expert'))
- gain_attention_gradient: float32 [1024], replicated
- gain_feedforward_gradient: float32 [1024], replicated
- query_gradient: float32 [1024, 512], replicated
- key_gradient: float32 [1024, 512], replicated
- value_gradient: float32 [1024, 2560], replicated
- output_gradient: float32 [2560, 1024], replicated
- value_router_gradient: float32 [1024, 20], replicated
- output_router_gradient: float32 [1024, 20], replicated
- expert_router_gradient: float32 [1024, 96], replicated
- first_gradient: float32 [96, 1024, 128], P(('dp', 'expert'))
- second_gradient: float32 [96, 128, 1024], P(('dp', 'expert'))
Inputs may be any that keep to these rules, and one draw needn't show every extreme that they name: `ffn_ids`: in each repeat, among the 128 rows of one device no expert is named by more than 32 rows, a bound that some block reaches; the 16 experts of a row differ. `value_ids`: the 2 experts of one token and head differ. `output_ids`: the 2 experts of one token and head differ. `segments`: along a sequence the numbers never fall; every document has 1 to 64 tokens, one exactly that many.
All inputs are finite; a program needn't handle non-finite values.
Results may differ from a plain program's by a relative error of at most 0.015.
The roundings to bfloat16 on the way count: a program that leaves them out, or rounds other values in their place, can miss the bound.
Values may be sent and summed in bfloat16 or wider, within the bound.
A program may use at most 192 MiB of HBM per device.

v0:
```python
import math

import jax
import jax.numpy as jnp
from jax import lax
from jax.sharding import PartitionSpec as P

HEADS = 4
HEAD = 128
ATT_EXP = 5
TOPK = 16


NEG_FILL = -1000000000.0


def layer_norm(stream, norm_gain):
    average = jnp.mean(stream, axis=-1, keepdims=True)
    centred = stream - average
    variance = jnp.mean(centred * centred, axis=-1, keepdims=True)
    return centred * lax.rsqrt(variance + 1e-05) * norm_gain


def expert_mask(picked_ids, expert_count):
    matches = picked_ids[..., None] == jnp.arange(expert_count, dtype=jnp.int32)
    return jnp.sum(matches.astype(jnp.float32), axis=-2)


def slot_tables(picked_ids, expert_count, capacity):
    flat_ids = picked_ids.reshape(-1)
    onehot = (flat_ids[:, None] == jnp.arange(expert_count, dtype=jnp.int32)[None, :]).astype(
        jnp.int32
    )
    before = jnp.cumsum(onehot, axis=0) - onehot
    within = jnp.sum(before * onehot, axis=1)
    target = flat_ids * capacity + within
    owners = (
        jnp.full((expert_count * capacity,), -1, jnp.int32)
        .at[target]
        .set(jnp.arange(flat_ids.shape[0], dtype=jnp.int32))
    )
    return (target, owners)


def float_zeros(array):
    return jnp.zeros(array.shape, jnp.float32)


def send_tokens(packet):
    return lax.all_to_all(packet, ("dp", "expert"), split_axis=0, concat_axis=0, tiled=True)


def return_results(result):
    return lax.all_to_all(result, ("dp", "expert"), split_axis=0, concat_axis=0, tiled=True)


def send_grad_only(grad_packet, gate_packet):
    return (
        lax.all_to_all(grad_packet, ("dp", "expert"), split_axis=0, concat_axis=0, tiled=True),
        lax.all_to_all(gate_packet, ("dp", "expert"), split_axis=0, concat_axis=0, tiled=True),
    )


def return_gradients(row_grad, gate_grad):
    return (
        lax.all_to_all(row_grad, ("dp", "expert"), split_axis=0, concat_axis=0, tiled=True),
        lax.all_to_all(gate_grad, ("dp", "expert"), split_axis=0, concat_axis=0, tiled=True),
    )


def expert_forward(received, expert_first, expert_second):
    owner_count, slot_count, model_width = received.shape
    local_count = expert_first.shape[0]
    shaped = received.reshape(owner_count, local_count, slot_count // local_count, model_width)
    hidden_pre = jnp.einsum(
        "secd,edf->secf", shaped, expert_first, preferred_element_type=jnp.float32
    )
    hidden = jax.nn.gelu(hidden_pre).astype(jnp.bfloat16)
    result = jnp.einsum(
        "secf,efd->secd", hidden, expert_second, preferred_element_type=jnp.float32
    ).astype(jnp.bfloat16)
    return (shaped, hidden_pre, hidden, result)


def attention_forward(stream, document_ids, value_picks, output_picks, shared):
    (
        gain_attention,
        query_weight,
        key_weight,
        value_weight,
        output_weight,
        value_router,
        output_router,
    ) = shared
    length = stream.shape[0]
    normed_low = layer_norm(stream, gain_attention).astype(jnp.bfloat16)
    queries = (
        jnp.dot(normed_low, query_weight, preferred_element_type=jnp.float32)
        .astype(jnp.bfloat16)
        .reshape(length, HEADS, HEAD)
    )
    key_rows = (
        jnp.dot(normed_low, key_weight, preferred_element_type=jnp.float32)
        .astype(jnp.bfloat16)
        .reshape(length, HEADS, HEAD)
    )
    value_sig = jax.nn.sigmoid(
        jnp.dot(normed_low, value_router, preferred_element_type=jnp.float32)
    ).reshape(length, HEADS, ATT_EXP)
    output_sig = jax.nn.sigmoid(
        jnp.dot(normed_low, output_router, preferred_element_type=jnp.float32)
    ).reshape(length, HEADS, ATT_EXP)
    value_mask = expert_mask(value_picks, ATT_EXP)
    output_mask = expert_mask(output_picks, ATT_EXP)
    value_gates = value_mask * value_sig
    output_gates = output_mask * output_sig
    stream_low = stream.astype(jnp.bfloat16)
    projected = jnp.dot(stream_low, value_weight, preferred_element_type=jnp.float32).reshape(
        length, HEADS, ATT_EXP, HEAD
    )
    values = jnp.sum(value_gates[..., None] * projected, axis=2).astype(jnp.bfloat16)
    scores = jnp.einsum("qhd,khd->hqk", queries, key_rows, preferred_element_type=jnp.float32) * (
        1.0 / math.sqrt(HEAD)
    )
    positions = jnp.arange(length, dtype=jnp.int32)
    allowed = (document_ids[:, None] == document_ids[None, :]) & (
        positions[:, None] >= positions[None, :]
    )
    scores = jnp.where(allowed[None], scores, NEG_FILL)
    row_max = jnp.max(scores, axis=-1, keepdims=True)
    exponent = jnp.exp(scores - row_max)
    row_total = jnp.sum(exponent, axis=-1, keepdims=True)
    probability = exponent / row_total
    weights_low = probability.astype(jnp.bfloat16)
    mixed = jnp.einsum("hqk,khd->qhd", weights_low, values, preferred_element_type=jnp.float32)
    gated_rows = (
        (output_gates[..., None] * mixed[:, :, None, :])
        .reshape(length, HEADS * ATT_EXP * HEAD)
        .astype(jnp.bfloat16)
    )
    after_attention = stream + jnp.dot(
        gated_rows, output_weight, preferred_element_type=jnp.float32
    )
    saved_parts = (
        normed_low,
        queries,
        key_rows,
        value_sig,
        output_sig,
        value_mask,
        output_mask,
        value_gates,
        output_gates,
        stream_low,
        projected,
        values,
        probability,
        weights_low,
        mixed,
        gated_rows,
    )
    return (after_attention, saved_parts)


def attention_backward(after_grad, saved_parts, stream, shared):
    (
        gain_attention,
        query_weight,
        key_weight,
        value_weight,
        output_weight,
        value_router,
        output_router,
    ) = shared
    (
        normed_low,
        queries,
        key_rows,
        value_sig,
        output_sig,
        value_mask,
        output_mask,
        value_gates,
        output_gates,
        stream_low,
        projected,
        values,
        probability,
        weights_low,
        mixed,
        gated_rows,
    ) = saved_parts
    length = after_grad.shape[0]
    scale = 1.0 / math.sqrt(HEAD)
    after_low = after_grad.astype(jnp.bfloat16)
    output_part = jnp.einsum("sa,sb->ab", gated_rows, after_low, preferred_element_type=jnp.float32)
    gated_grad = jnp.einsum(
        "sb,ab->sa", after_low, output_weight, preferred_element_type=jnp.float32
    ).astype(jnp.bfloat16)
    gated_grad = gated_grad.reshape(length, HEADS, ATT_EXP, HEAD).astype(jnp.float32)
    mixed_grad = jnp.sum(output_gates[..., None] * gated_grad, axis=2).astype(jnp.bfloat16)
    output_gate_grad = jnp.sum(gated_grad * mixed[:, :, None, :], axis=3)
    prob_grad = jnp.einsum("qhd,khd->hqk", mixed_grad, values, preferred_element_type=jnp.float32)
    values_grad = jnp.einsum(
        "hqk,qhd->khd", weights_low, mixed_grad, preferred_element_type=jnp.float32
    ).astype(jnp.bfloat16)
    values_grad = values_grad.astype(jnp.float32)
    score_grad = (
        probability * (prob_grad - jnp.sum(probability * prob_grad, axis=-1, keepdims=True))
    ).astype(jnp.bfloat16)
    query_grad = (
        (
            jnp.einsum("hqk,khd->qhd", score_grad, key_rows, preferred_element_type=jnp.float32)
            * scale
        )
        .astype(jnp.bfloat16)
        .reshape(length, HEADS * HEAD)
    )
    key_grad = (
        (
            jnp.einsum("hqk,qhd->khd", score_grad, queries, preferred_element_type=jnp.float32)
            * scale
        )
        .astype(jnp.bfloat16)
        .reshape(length, HEADS * HEAD)
    )
    projected_grad = (
        (value_gates[..., None] * values_grad[:, :, None, :])
        .astype(jnp.bfloat16)
        .reshape(length, HEADS * ATT_EXP * HEAD)
    )
    value_gate_grad = jnp.sum(values_grad[:, :, None, :] * projected, axis=3)
    value_logit_grad = (
        (value_gate_grad * value_mask * value_sig * (1.0 - value_sig))
        .astype(jnp.bfloat16)
        .reshape(length, HEADS * ATT_EXP)
    )
    output_logit_grad = (
        (output_gate_grad * output_mask * output_sig * (1.0 - output_sig))
        .astype(jnp.bfloat16)
        .reshape(length, HEADS * ATT_EXP)
    )
    value_part = jnp.einsum(
        "sa,sb->ab", stream_low, projected_grad, preferred_element_type=jnp.float32
    )
    query_part = jnp.einsum("sa,sb->ab", normed_low, query_grad, preferred_element_type=jnp.float32)
    key_part = jnp.einsum("sa,sb->ab", normed_low, key_grad, preferred_element_type=jnp.float32)
    value_router_part = jnp.einsum(
        "sa,sb->ab", normed_low, value_logit_grad, preferred_element_type=jnp.float32
    )
    output_router_part = jnp.einsum(
        "sa,sb->ab", normed_low, output_logit_grad, preferred_element_type=jnp.float32
    )
    normed_grad = jnp.einsum(
        "sb,ab->sa", query_grad, query_weight, preferred_element_type=jnp.float32
    )
    normed_grad = normed_grad + jnp.einsum(
        "sb,ab->sa", key_grad, key_weight, preferred_element_type=jnp.float32
    )
    normed_grad = normed_grad + jnp.einsum(
        "sb,ab->sa", value_logit_grad, value_router, preferred_element_type=jnp.float32
    )
    normed_grad = normed_grad + jnp.einsum(
        "sb,ab->sa", output_logit_grad, output_router, preferred_element_type=jnp.float32
    )
    norm_value, norm_pull = jax.vjp(layer_norm, stream, gain_attention)
    stream_extra, gain_part = norm_pull(normed_grad)
    value_input = jnp.einsum(
        "sb,ab->sa", projected_grad, value_weight, preferred_element_type=jnp.float32
    )
    stream_grad = after_grad + stream_extra + value_input
    return (
        stream_grad,
        (
            gain_part,
            query_part,
            key_part,
            value_part,
            output_part,
            value_router_part,
            output_router_part,
        ),
    )


def ffn_prepare(
    after_attention, gain_feedforward, expert_router, expert_picks, expert_count, capacity
):
    normed_low = layer_norm(after_attention, gain_feedforward).astype(jnp.bfloat16)
    logits = jnp.dot(normed_low, expert_router, preferred_element_type=jnp.float32)
    chosen = jnp.take_along_axis(logits, expert_picks, axis=1)
    sigmoid_out = jax.nn.sigmoid(chosen)
    gate_values = sigmoid_out.astype(jnp.bfloat16)
    target, owners = slot_tables(expert_picks, expert_count, capacity)
    present = owners >= 0
    safe_index = jnp.where(present, owners, 0)
    after_low = after_attention.astype(jnp.bfloat16)
    packet = jnp.where(present[:, None], after_low[safe_index // TOPK], jnp.zeros((), jnp.bfloat16))
    return (normed_low, sigmoid_out, gate_values, target, present, safe_index, packet)


def body(
    tokens,
    cotangent,
    gain_attention,
    gain_feedforward,
    query_weight,
    key_weight,
    value_weight,
    output_weight,
    value_router,
    output_router,
    expert_router,
    expert_first,
    expert_second,
    segments,
    value_ids,
    output_ids,
    ffn_ids,
):
    owner_total = lax.axis_size("dp") * lax.axis_size("expert")
    expert_count = expert_first.shape[0] * owner_total
    length, model_width = tokens.shape
    capacity = max(2, 3 * length * TOPK // (2 * expert_count))
    document_ids = segments[0]
    shared = (
        gain_attention,
        query_weight,
        key_weight,
        value_weight,
        output_weight,
        value_router,
        output_router,
    )
    stream = tokens.astype(jnp.float32)
    repeat_index = 0
    saved_inputs = [stream]
    after_attention, saved_parts = attention_forward(
        stream, document_ids, value_ids[repeat_index], output_ids[repeat_index], shared
    )
    normed_low, sigmoid_out, gate_values, target, present, safe_index, packet = ffn_prepare(
        after_attention,
        gain_feedforward,
        expert_router,
        ffn_ids[repeat_index],
        expert_count,
        capacity,
    )
    received = send_tokens(packet.reshape(owner_total, -1, model_width))
    shaped, hidden_pre, hidden, result = expert_forward(received, expert_first, expert_second)
    returned = return_results(result.reshape(received.shape))
    picked_rows = returned.reshape(-1, model_width)[target].reshape(length, TOPK, model_width)
    stream = after_attention + jnp.einsum(
        "sk,skd->sd", gate_values, picked_rows, preferred_element_type=jnp.float32
    )
    block_output = stream.astype(jnp.bfloat16)
    upstream = cotangent.astype(jnp.float32)
    attention_sums = jax.tree.map(float_zeros, shared)
    expert_axis = jnp.arange(expert_count, dtype=jnp.int32)
    repeat_index = 0
    stream = saved_inputs[repeat_index]
    after_attention, saved_parts = attention_forward(
        stream, document_ids, value_ids[repeat_index], output_ids[repeat_index], shared
    )
    normed_low, sigmoid_out, gate_values, target, present, safe_index, packet = ffn_prepare(
        after_attention,
        gain_feedforward,
        expert_router,
        ffn_ids[repeat_index],
        expert_count,
        capacity,
    )
    upstream_low = upstream.astype(jnp.bfloat16)
    grad_packet = jnp.where(
        present[:, None], upstream_low[safe_index // TOPK], jnp.zeros((), jnp.bfloat16)
    )
    gate_packet = jnp.where(
        present, gate_values.reshape(-1)[safe_index], jnp.zeros((), jnp.bfloat16)
    )
    grads_in, gates_in = send_grad_only(
        grad_packet.reshape(owner_total, -1, model_width), gate_packet.reshape(owner_total, -1)
    )
    received = lax.all_to_all(
        packet.reshape(owner_total, -1, model_width),
        ("dp", "expert"),
        split_axis=0,
        concat_axis=0,
        tiled=True,
    )
    shaped, hidden_pre, hidden, result = expert_forward(received, expert_first, expert_second)
    grads_shaped = grads_in.reshape(shaped.shape)
    gate_grad = jnp.einsum(
        "secd,secd->sec", grads_shaped, result, preferred_element_type=jnp.float32
    ).astype(jnp.bfloat16)
    gates_shaped = gates_in.reshape(shaped.shape[:3]).astype(jnp.float32)
    result_grad = (gates_shaped[..., None] * grads_shaped.astype(jnp.float32)).astype(jnp.bfloat16)
    second_sum = jnp.einsum(
        "secf,secd->efd", hidden, result_grad, preferred_element_type=jnp.float32
    )
    hidden_grad = jnp.einsum(
        "secd,efd->secf", result_grad, expert_second, preferred_element_type=jnp.float32
    )
    gelu_value, gelu_pull = jax.vjp(jax.nn.gelu, hidden_pre)
    pre_grad = gelu_pull(hidden_grad)[0].astype(jnp.bfloat16)
    first_sum = jnp.einsum("secd,secf->edf", shaped, pre_grad, preferred_element_type=jnp.float32)
    row_grad = jnp.einsum(
        "secf,edf->secd", pre_grad, expert_first, preferred_element_type=jnp.float32
    ).astype(jnp.bfloat16)
    rows_back, gates_back = return_gradients(
        row_grad.reshape(received.shape), gate_grad.reshape(gates_in.shape)
    )
    token_rows = rows_back.reshape(-1, model_width)[target].reshape(length, TOPK, model_width)
    token_grad = jnp.sum(token_rows.astype(jnp.float32), axis=1)
    chosen_grad = (
        gates_back.reshape(-1)[target].reshape(length, TOPK).astype(jnp.float32)
        * sigmoid_out
        * (1.0 - sigmoid_out)
    )
    selected = (ffn_ids[repeat_index][:, :, None] == expert_axis[None, None, :]).astype(jnp.float32)
    logit_grad = jnp.sum(selected * chosen_grad[:, :, None], axis=1).astype(jnp.bfloat16)
    router_sum = jnp.einsum("sa,sb->ab", normed_low, logit_grad, preferred_element_type=jnp.float32)
    normed_grad = jnp.einsum(
        "sb,ab->sa", logit_grad, expert_router, preferred_element_type=jnp.float32
    )
    norm_value, norm_pull = jax.vjp(layer_norm, after_attention, gain_feedforward)
    after_extra, feed_gain_part = norm_pull(normed_grad)
    after_grad = upstream + token_grad + after_extra
    upstream, attention_parts = attention_backward(after_grad, saved_parts, stream, shared)
    attention_sums = jax.tree.map(jnp.add, attention_sums, attention_parts)
    summed = lax.psum(
        (
            attention_sums[0],
            feed_gain_part,
            attention_sums[1],
            attention_sums[2],
            attention_sums[3],
            attention_sums[4],
            attention_sums[5],
            attention_sums[6],
            router_sum,
        ),
        ("dp", "expert"),
    )
    return (
        block_output,
        upstream,
        summed[0],
        summed[1],
        summed[2],
        summed[3],
        summed[4],
        summed[5],
        summed[6],
        summed[7],
        summed[8],
        first_sum,
        second_sum,
    )


def solution(mesh):
    placed = (
        P(("dp", "expert"), None),
        P(("dp", "expert"), None),
        P(),
        P(),
        P(),
        P(),
        P(),
        P(),
        P(),
        P(),
        P(),
        P(("dp", "expert"), None, None),
        P(("dp", "expert"), None, None),
        P(("dp", "expert"), None),
        P(None, ("dp", "expert"), None, None),
        P(None, ("dp", "expert"), None, None),
        P(None, ("dp", "expert"), None),
    )
    return jax.shard_map(
        body,
        mesh=mesh,
        in_specs=placed,
        out_specs=(
            P(("dp", "expert"), None),
            P(("dp", "expert"), None),
            P(),
            P(),
            P(),
            P(),
            P(),
            P(),
            P(),
            P(),
            P(),
            P(("dp", "expert"), None, None),
            P(("dp", "expert"), None, None),
        ),
        check_vma=False,
    )
```

profile of v0, /device:TPU:1, one launch (start us, length us, event | category | flops | bytes accessed | tf_op | source)
XLA Modules:
  0.0 1262.4 jit_solution(15129272999610501925)
XLA Ops:
  9.2 27.2 %reduce-window.6 = s32[96,16,128]{2,1,0:T(8,128)S(1)} reduce-window(s32[96,16,128]{2,1,0:T(8,128)S(1)} %fusion.47, s32[]{:T(128)} %constant.74.clone.1), window={size=1x1x128 pad=0_0x0_0x127_0}, to_apply=%region_9.0 | reduce-window | flops 24969216 | bytes 1572868 | tf_op jit(solution)/shard_map/reduce-window
  38.9 8.1 scatter_custom_fusion
  50.4 1.6 convolution_convert_fusion.3
  53.2 4.6 fusion.89
  59.7 3.4 fusion.88
  64.5 13.9 %gather_fusion = bf16[3072,1024]{1,0:T(8,128)(2,1)} fusion(bf16[128,1024]{1,0:T(8,128)(2,1)S(1)} %get-tuple-element.138, s32[3072]{0:T(1024)S(1)} %fusion.68), kind=kCustom, calls=%fused_computation.1 | custom fusion | bytes 12595200 | tf_op jit(solution)/shard_map/gather | solution.py:298
  78.3 13.9 %gather_fusion.3 = bf16[3072,1024]{1,0:T(8,128)(2,1)} fusion(bf16[128,1024]{1,0:T(8,128)(2,1)S(1)} %copy-done.1, s32[3072]{0:T(1024)S(1)} %fusion.68), kind=kCustom, calls=%fused_computation.4 | custom fusion | bytes 12595200 | tf_op jit(solution)/shard_map/gather | solution.py:375
  92.2 8.2 broadcast_select_fusion
  100.4 146.4 %all_to_all.41 = bf16[32,96,1024]{2,1,0:T(8,128)(2,1)} all-to-all(bf16[32,96,1024]{2,1,0:T(8,128)(2,1)S(1)} %get-tuple-element.145), channel_id=1, replica_groups=mesh['dp'=4,'expert'=8] {'dp','expert'}, dimensions={0} | all-to-all | bytes 12582912 | tf_op jit(solution)/shard_map/all_to_all | solution.py:50
  246.8 4.6 all-to-all-start.3
  251.6 5.9 fusion.1
  257.5 133.3 %all-to-all-done.3 = bf16[32,96,1024]{2,1,0:T(8,128)(2,1)} async-done(((bf16[32,96,1024]{2,1,0:T(8,128)(2,1)}), bf16[32,96,1024]{2,1,0:T(8,128)(2,1)}, u32[]{:S(2)}, u32[]{:S(2)}) %all-to-all-start.3) | async-done | bytes 6291488 | tf_op jit(solution)/shard_map/all_to_all | solution.py:59
  390.8 8.4 multiply_reduce_fusion
  399.8 1.5 all_to_all.34
  401.3 3.6 all-to-all-start.5
  406.6 13.5 %gather_fusion.6 = f32[2048]{0:T(1024)S(1)} fusion(f32[128,96]{0,1:T(8,128)S(1)} %fusion.90, s32[2048]{0:T(1024)S(1)} %reshape.408), kind=kCustom, calls=%fused_computation.clone | custom fusion | bytes 32768 | tf_op jit(solution)/shard_map/jit(take_along_axis)/gather | solution.py:291
  422.6 13.1 %gather_fusion.5 = bf16[2048]{0:T(1024)(128)(2,1)S(1)} fusion(bf16[3072]{0:T(1024)(128)(2,1)S(1)} %reshape.330, s32[2048]{0:T(1024)S(1)} %broadcast_clamp_fusion), kind=kCustom, calls=%fused_computation.6 | custom fusion | bytes 16384 | tf_op jit(solution)/shard_map/gather | solution.py:415
  437.6 19.4 %gather_fusion.2 = bf16[3072]{0:T(1024)(128)(2,1)S(1)} fusion(bf16[2048]{0:T(1024)(128)(2,1)S(1)} %reshape.326, s32[3072]{0:T(1024)S(1)} %copy-done.51), kind=kCustom, calls=%fused_computation.3 | custom fusion | bytes 24576 | tf_op jit(solution)/shard_map/gather | solution.py:378
  457.7 6.0 all-to-all-start.2
  463.6 6.8 copy.291
  470.5 5.9 all-to-all-start.1
  478.0 6.0 fusion.12
  484.0 1.8 convert_bitcast_fusion
  485.8 3.4 copy.296
  489.2 126.6 %all-to-all-done.1 = bf16[32,96,1024]{2,1,0:T(8,128)(2,1)} async-done(((bf16[32,96,1024]{2,1,0:T(8,128)(2,1)}), bf16[32,96,1024]{2,1,0:T(8,128)(2,1)}, u32[]{:S(2)}, u32[]{:S(2)}) %all-to-all-start.1) | async-done | bytes 6291488 | tf_op jit(solution)/shard_map/all_to_all | solution.py:54
  615.8 4.1 all-to-all-start.4
  620.9 1.7 multiply_reduce_fusion.5
  623.5 14.6 %gather_fusion.1 = bf16[2048,1024]{1,0:T(8,128)(2,1)} fusion(bf16[3072,1024]{1,0:T(8,128)(2,1)} %bitcast.23, s32[2048]{0:T(1024)S(1)} %broadcast_clamp_fusion), kind=kCustom, calls=%fused_computation.2 | custom fusion | bytes 8396800 | tf_op jit(solution)/shard_map/gather | solution.py:352
  638.1 3.0 fusion.91
  642.3 117.3 %all-to-all-done.4 = bf16[32,96,1024]{2,1,0:T(8,128)(2,1)} async-done(((bf16[32,96,1024]{2,1,0:T(8,128)(2,1)}), bf16[32,96,1024]{2,1,0:T(8,128)(2,1)}, u32[]{:S(2)}, u32[]{:S(2)}) %all-to-all-start.4) | async-done | bytes 6291488 | tf_op jit(solution)/shard_map/all_to_all | solution.py:66
  759.6 23.0 %gather_fusion.4 = bf16[2048,1024]{1,0:T(8,128)(2,1)} fusion(bf16[3072,1024]{1,0:T(8,128)(2,1)} %bitcast.33, s32[2048]{0:T(1024)S(1)} %broadcast_clamp_fusion), kind=kCustom, calls=%fused_computation.5 | custom fusion | bytes 8396800 | tf_op jit(solution)/shard_map/gather | solution.py:412
  782.6 4.3 convert_reduce_fusion
  787.1 5.4 fusion.5
  792.5 2.8 copy.299
  795.4 2.3 multiply_reduce_fusion.1
  797.6 1.4 fusion.26
  801.5 5.6 fusion.55
  809.4 1.8 fusion.96
  811.2 1.8 fusion.95
  812.9 5.6 convolution_bitcast_fusion
  819.3 6.5 fusion.17
  825.9 6.7 convolution_bitcast_fusion.1
  834.6 40.1 %all-reduce = (f32[1024]{0:T(1024)}, f32[1024]{0:T(1024)}) all-reduce(f32[1024]{0:T(1024)S(1)} %get-tuple-element.122, f32[1024]{0:T(1024)S(1)} %copy-done.56), channel_id=1, replica_groups=mesh['dp'=4,'expert'=8] {'dp','expert'}, use_global_device_ids=true, to_apply=%region_24.26 | all-reduce | flops 2048 | bytes 16384 | tf_op jit(solution)/shard_map/psum | solution.py:430
  874.7 5.2 convolution_add_fusion.1
  880.0 347.7 %all-reduce.4.cloned.1.call-done = (f32[1024,512]{1,0:T(8,128)}, f32[1024,512]{1,0:T(8,128)}, f32[1024,2560]{0,1:T(8,128)}, f32[2560,1024]{1,0:T(8,128)}, f32[10...) async-done(((f32[1024,512]{1,0:T(8,128)}, f32[1024,512]{1,0:T(8,128)}, f32[1024,2560]{0,1:T(8,128)}, f32[2560,1024]{1,0:T(8,128)}, f32[1024,20]{0,1:T(8,128)}, ...) | async-done | bytes 25722896 | tf_op jit(solution)/shard_map/psum | solution.py:430
  1227.7 11.5 copy.316
  1239.3 1.3 copy.366
  1242.9 10.3 copy.368
  (256 shorter events, 35.9 us)
Async XLA Ops:
  7.2 42.8 %copy-start = (bf16[1024,512]{1,0:T(8,128)(2,1)S(1)}, bf16[1024,512]{1,0:T(8,128)(2,1)}, u32[]{:S(2)}) copy-start(bf16[1024,512]{1,0:T(8,128)(2,1)} %param.24) | copy-start | bytes 3145732
  9.2 38.5 %copy-start.2 = (bf16[128,1024]{1,0:T(8,128)(2,1)S(1)}, bf16[128,1024]{1,0:T(8,128)(2,1)}, u32[]{:S(2)}) copy-start(bf16[128,1024]{1,0:T(8,128)(2,1)} %param.19) | copy-start | bytes 786436
  36.4 11.6 copy-start.68
  36.4 11.6 copy-start.69
  36.4 12.2 copy-start.70
  36.4 12.2 copy-start.44
  36.4 12.5 copy-start.25
  36.5 12.7 %copy-start.27 = (bf16[1024,20]{0,1:T(8,128)(2,1)S(1)}, bf16[1024,20]{0,1:T(8,128)(2,1)}, u32[]{:S(2)}) copy-start(bf16[1024,20]{0,1:T(8,128)(2,1)} %param.28) | copy-start | bytes 122884
  49.4 9.9 copy-start.31
  50.0 7.9 copy-start.29
  50.4 7.4 copy-start.10
  52.1 5.7 copy-start.12
  52.4 6.7 copy-start.15
  53.2 5.8 copy-start.59
  64.5 13.9 %copy-start.1 = (bf16[128,1024]{1,0:T(8,128)(2,1)S(1)}, bf16[128,1024]{1,0:T(8,128)(2,1)}, u32[]{:S(2)}) copy-start(bf16[128,1024]{1,0:T(8,128)(2,1)} %param.20) | copy-start | bytes 786436
  246.8 144.0 %all-to-all-start.3 = ((bf16[32,96,1024]{2,1,0:T(8,128)(2,1)}), bf16[32,96,1024]{2,1,0:T(8,128)(2,1)}, u32[]{:S(2)}, u32[]{:S(2)}) async-start(bf16[32,96,1024]{2,1,0:T(8,128)(2,1)} %get-tuple-element.144), calls=%async_computation.3 | async-start | bytes 12582912 | tf_op jit(solution)/shard_map/all_to_all | solution.py:59
  390.8 14.1 %copy-start.55 = (s32[2048,1]{0,1:T(1,128)S(1)}, s32[2048,1]{0,1:T(1,128)}, u32[]{:S(2)}) copy-start(s32[2048,1]{0,1:T(1,128)} %copy-done.54) | copy-start | bytes 24580
  401.3 20.5 %all-to-all-start.5 = ((bf16[32,1,96]{2,1,0:T(2,128)(2,1)}), bf16[32,1,96]{2,1,0:T(2,128)(2,1)}, u32[]{:S(2)}, u32[]{:S(2)}) async-start(bf16[32,1,96]{2,1,0:T(2,128)(2,1)} %all_to_all.34), calls=%async_computation.5 | async-start | bytes 32768 | tf_op jit(solution)/shard_map/all_to_all | solution.py:67
  420.1 17.4 %copy-start.51 = (s32[3072]{0:T(1024)S(1)}, s32[3072]{0:T(1024)}, u32[]{:S(2)}) copy-start(s32[3072]{0:T(1024)} %get-tuple-element.135) | copy-start | bytes 36868
  437.6 19.4 %copy-start.50 = (pred[3072]{0:T(1024)(128)(4,1)S(1)}, pred[3072]{0:T(1024)(128)(4,1)}, u32[]{:S(2)}) copy-start(pred[3072]{0:T(1024)(128)(4,1)} %copy-done.49) | copy-start | bytes 9220
  457.7 12.8 %all-to-all-start.2 = ((bf16[32,1,96]{2,1,0:T(2,128)(2,1)}), bf16[32,1,96]{2,1,0:T(2,128)(2,1)S(1)}, u32[]{:S(2)}, u32[]{:S(2)}) async-start(bf16[32,1,96]{2,1,0:T(2,128)(2,1)} %all_to_all.33), calls=%async_computation.2 | async-start | bytes 32768 | tf_op jit(solution)/shard_map/all_to_all | solution.py:60
  470.5 145.3 %all-to-all-start.1 = ((bf16[32,96,1024]{2,1,0:T(8,128)(2,1)}), bf16[32,96,1024]{2,1,0:T(8,128)(2,1)}, u32[]{:S(2)}, u32[]{:S(2)}) async-start(bf16[32,96,1024]{2,1,0:T(8,128)(2,1)} %bitcast.193), calls=%async_computation.1 | async-start | bytes 12582912 | tf_op jit(solution)/shard_map/all_to_all | solution.py:54
  478.0 6.0 copy-start.47
  478.0 6.0 copy-start.19
  615.8 6.7 copy-start.74
  615.8 143.7 %all-to-all-start.4 = ((bf16[32,96,1024]{2,1,0:T(8,128)(2,1)}), bf16[32,96,1024]{2,1,0:T(8,128)(2,1)}, u32[]{:S(2)}, u32[]{:S(2)}) async-start(bf16[32,96,1024]{2,1,0:T(8,128)(2,1)} %bitcast.192), calls=%async_computation.4 | async-start | bytes 12582912 | tf_op jit(solution)/shard_map/all_to_all | solution.py:66
  620.0 607.8 %all-reduce.4.cloned.1.call-start = ((), (), s32[]{:S(2)}) async-start(), calls=%async_computation.6 | async-start | bytes 51511296 | tf_op jit(solution)/shard_map/psum | solution.py:430
  623.5 14.6 %copy-start.23 = (bf16[128,16,1]{1,2,0:T(2,128)(2,1)S(1)}, bf16[128,16,1]{1,2,0:T(2,128)(2,1)}, u32[]{:S(2)}) copy-start(bf16[128,16,1]{1,2,0:T(2,128)(2,1)} %copy.321) | copy-start | bytes 12292
  787.1 8.3 copy-start.17
  787.1 8.3 copy-start.32
  792.5 6.4 copy-start.14
  792.5 8.4 copy-start.13
  795.4 5.8 copy-start.11
  801.4 5.7 copy-start.43
  801.5 5.7 copy-start.46
  801.5 5.9 copy-start.41
  801.5 6.2 copy-start.37
  801.5 6.2 copy-start.35
  819.3 6.5 copy-start.21
  825.8 6.7 copy-start.26
  825.8 7.0 copy-start.28
  825.8 7.3 copy-start.5
  825.9 7.8 copy-start.45
  825.9 7.8 copy-start.58
  1227.7 11.5 copy-start.7
  1242.9 10.3 copy-start.39
  1242.9 11.0 copy-start.38
  1242.9 11.6 copy-start.22
  (33 other events, 80.4 us)
Sparse Core Ops, SparseCore 0:
  818.7 408.9 all-reduce.3
where the time goes:
time: 1270 us; the launch traced here: 1260 us
  waiting for transfers between devices  725 us (57%)
  blocking collectives  186 us (15%)
  local copies, waits for them, and re-layouts  178 us (14%)
  matrix products  83.6 us (7%)
  other arithmetic  50.1 us (4%)
  starting transfers between devices  24.2 us (2%)
  between operations  15.5 us (1%)
    psum x1, waiting for transfers between devices, body(): lax.psum((attention_sums[0], feed_gain_part, attention_sums[1], attention...  348 us
    all_to_all x1, blocking collectives, send_tokens(): lax.all_to_all(packet, ('dp', 'expert'), split_axis=0, concat_axis=0, til...  146 us
    all_to_all x1, waiting for transfers between devices, send_grad_only(): lax.all_to_all(grad_packet, ('dp', 'expert'), split_axis=0, concat_axis=0...  133 us
    all_to_all x1, waiting for transfers between devices, return_results(): lax.all_to_all(result, ('dp', 'expert'), split_axis=0, concat_axis=0, til...  127 us
    all_to_all x1, waiting for transfers between devices, return_gradients(): lax.all_to_all(row_grad, ('dp', 'expert'), split_axis=0, concat_axis=0, t...  117 us
    psum x1, blocking collectives, body(): lax.psum((attention_sums[0], feed_gain_part, attention_sums[1], attention...  40.1 us
    unnamed x159, local copies, waits for them, and re-layouts  33.7 us
    another operation x3, other arithmetic  27.7 us
  transfers between devices with their start and end apart: 6, of which 4 were waited for; matrix products, arithmetic and copies ran while one was open for 7% of the time, Pallas kernels for 0%

commit v1 on v0

--- a/solution.py
+++ b/solution.py
@@ -8,7 +8,6 @@
 HEADS = 4
 HEAD = 128
 ATT_EXP = 5
-TOPK = 16
 
 
 NEG_FILL = -1000000000.0
@@ -24,62 +23,6 @@
 def expert_mask(picked_ids, expert_count):
     matches = picked_ids[..., None] == jnp.arange(expert_count, dtype=jnp.int32)
     return jnp.sum(matches.astype(jnp.float32), axis=-2)
-
-
-def slot_tables(picked_ids, expert_count, capacity):
-    flat_ids = picked_ids.reshape(-1)
-    onehot = (flat_ids[:, None] == jnp.arange(expert_count, dtype=jnp.int32)[None, :]).astype(
-        jnp.int32
-    )
-    before = jnp.cumsum(onehot, axis=0) - onehot
-    within = jnp.sum(before * onehot, axis=1)
-    target = flat_ids * capacity + within
-    owners = (
-        jnp.full((expert_count * capacity,), -1, jnp.int32)
-        .at[target]
-        .set(jnp.arange(flat_ids.shape[0], dtype=jnp.int32))
-    )
-    return (target, owners)
-
-
-def float_zeros(array):
-    return jnp.zeros(array.shape, jnp.float32)
-
-
-def send_tokens(packet):
-    return lax.all_to_all(packet, ("dp", "expert"), split_axis=0, concat_axis=0, tiled=True)
-
-
-def return_results(result):
-    return lax.all_to_all(result, ("dp", "expert"), split_axis=0, concat_axis=0, tiled=True)
-
-
-def send_grad_only(grad_packet, gate_packet):
-    return (
-        lax.all_to_all(grad_packet, ("dp", "expert"), split_axis=0, concat_axis=0, tiled=True),
-        lax.all_to_all(gate_packet, ("dp", "expert"), split_axis=0, concat_axis=0, tiled=True),
-    )
-
-
-def return_gradients(row_grad, gate_grad):
-    return (
-        lax.all_to_all(row_grad, ("dp", "expert"), split_axis=0, concat_axis=0, tiled=True),
-        lax.all_to_all(gate_grad, ("dp", "expert"), split_axis=0, concat_axis=0, tiled=True),
-    )
-
-
-def expert_forward(received, expert_first, expert_second):
-    owner_count, slot_count, model_width = received.shape
-    local_count = expert_first.shape[0]
-    shaped = received.reshape(owner_count, local_count, slot_count // local_count, model_width)
-    hidden_pre = jnp.einsum(
-        "secd,edf->secf", shaped, expert_first, preferred_element_type=jnp.float32
-    )
-    hidden = jax.nn.gelu(hidden_pre).astype(jnp.bfloat16)
-    result = jnp.einsum(
-        "secf,efd->secd", hidden, expert_second, preferred_element_type=jnp.float32
-    ).astype(jnp.bfloat16)
-    return (shaped, hidden_pre, hidden, result)
 
 
 def attention_forward(stream, document_ids, value_picks, output_picks, shared):
@@ -283,20 +226,72 @@
     )
 
 
-def ffn_prepare(
-    after_attention, gain_feedforward, expert_router, expert_picks, expert_count, capacity
-):
-    normed_low = layer_norm(after_attention, gain_feedforward).astype(jnp.bfloat16)
-    logits = jnp.dot(normed_low, expert_router, preferred_element_type=jnp.float32)
-    chosen = jnp.take_along_axis(logits, expert_picks, axis=1)
-    sigmoid_out = jax.nn.sigmoid(chosen)
-    gate_values = sigmoid_out.astype(jnp.bfloat16)
-    target, owners = slot_tables(expert_picks, expert_count, capacity)
-    present = owners >= 0
-    safe_index = jnp.where(present, owners, 0)
-    after_low = after_attention.astype(jnp.bfloat16)
-    packet = jnp.where(present[:, None], after_low[safe_index // TOPK], jnp.zeros((), jnp.bfloat16))
-    return (normed_low, sigmoid_out, gate_values, target, present, safe_index, packet)
+def expert_pass(rows, upstream_rows, gates, expert_first, expert_second):
+    local_count, model_width, hidden_width = expert_first.shape
+    wide = local_count * hidden_width
+    first = expert_first.transpose(1, 0, 2).reshape(model_width, wide)
+    second = expert_second.reshape(wide, model_width)
+    gates_wide = jnp.repeat(gates.astype(jnp.float32), hidden_width, axis=1)
+    hidden_pre = jnp.dot(rows, first, preferred_element_type=jnp.float32)
+    hidden, gelu_pull = jax.vjp(jax.nn.gelu, hidden_pre)
+    hidden = hidden.astype(jnp.bfloat16).astype(jnp.float32)
+    gated_hidden = (gates_wide * hidden).astype(jnp.bfloat16)
+    back = jnp.einsum("sd,fd->sf", upstream_rows, second, preferred_element_type=jnp.float32)
+    gate_grad = jnp.sum((back * hidden).reshape(-1, local_count, hidden_width), axis=2)
+    pre_grad = gelu_pull(gates_wide * back)[0].astype(jnp.bfloat16)
+    result = jnp.dot(gated_hidden, second, preferred_element_type=jnp.float32)
+    row_grad = jnp.einsum("sf,df->sd", pre_grad, first, preferred_element_type=jnp.float32)
+    second_sum = jnp.einsum(
+        "sf,sd->fd", gated_hidden, upstream_rows, preferred_element_type=jnp.float32
+    )
+    first_sum = jnp.einsum("sd,sf->df", rows, pre_grad, preferred_element_type=jnp.float32)
+    first_sum = first_sum.reshape(model_width, local_count, hidden_width).transpose(1, 0, 2)
+    return (
+        result.astype(jnp.bfloat16),
+        row_grad.astype(jnp.bfloat16),
+        gate_grad.astype(jnp.bfloat16),
+        first_sum,
+        second_sum.reshape(expert_second.shape),
+    )
+
+
+BOTH = ("dp", "expert")
+
+
+def expert_piece(after_low, upstream_low, dense_gates, expert_first, expert_second):
+    local_count = expert_first.shape[0]
+    me = lax.axis_index("dp") * lax.axis_size("expert") + lax.axis_index("expert")
+    upstream_rows = lax.all_gather(upstream_low, BOTH, axis=0, tiled=True)
+    rows = lax.all_gather(after_low, BOTH, axis=0, tiled=True)
+    gates = lax.all_gather(dense_gates, BOTH, axis=0, tiled=True)
+    gates = lax.dynamic_slice_in_dim(gates, me * local_count, local_count, axis=1)
+    result, row_grad, gate_grad, first_sum, second_sum = expert_pass(
+        rows, upstream_rows, gates, expert_first, expert_second
+    )
+    gate_back = lax.all_to_all(gate_grad, BOTH, split_axis=0, concat_axis=1, tiled=True)
+    token_grad = lax.psum_scatter(row_grad, BOTH, scatter_dimension=0, tiled=True)
+    result = lax.psum_scatter(result, BOTH, scatter_dimension=0, tiled=True)
+    return (result, token_grad, gate_back), (first_sum, second_sum)
+
+
+def expert_exchange(after_low, upstream_low, dense_gates, expert_first, expert_second, pieces):
+    if pieces == 1:
+        back, sums = expert_piece(
+            after_low, upstream_low, dense_gates, expert_first, expert_second
+        )
+        return (*back, *sums)
+
+    def step(totals, piece):
+        back, sums = expert_piece(*piece, expert_first, expert_second)
+        return (totals[0] + sums[0], totals[1] + sums[1]), back
+
+    cut = lambda array: array.reshape(pieces, -1, array.shape[1])
+    start = (
+        jnp.zeros(expert_first.shape, jnp.float32),
+        jnp.zeros(expert_second.shape, jnp.float32),
+    )
+    sums, back = lax.scan(step, start, (cut(after_low), cut(upstream_low), cut(dense_gates)))
+    return (*(part.reshape(-1, part.shape[2]) for part in back), *sums)
 
 
 def body(
@@ -319,10 +314,8 @@
     ffn_ids,
 ):
     owner_total = lax.axis_size("dp") * lax.axis_size("expert")
-    expert_count = expert_first.shape[0] * owner_total
-    length, model_width = tokens.shape
-    capacity = max(2, 3 * length * TOPK // (2 * expert_count))
-    document_ids = segments[0]
+    local_count = expert_first.shape[0]
+    expert_count = local_count * owner_total
     shared = (
         gain_attention,
         query_weight,
@@ -333,126 +326,55 @@
         output_router,
     )
     stream = tokens.astype(jnp.float32)
-    repeat_index = 0
-    saved_inputs = [stream]
+    upstream = cotangent.astype(jnp.float32)
     after_attention, saved_parts = attention_forward(
-        stream, document_ids, value_ids[repeat_index], output_ids[repeat_index], shared
-    )
-    normed_low, sigmoid_out, gate_values, target, present, safe_index, packet = ffn_prepare(
-        after_attention,
-        gain_feedforward,
-        expert_router,
-        ffn_ids[repeat_index],
-        expert_count,
-        capacity,
-    )
-    received = send_tokens(packet.reshape(owner_total, -1, model_width))
-    shaped, hidden_pre, hidden, result = expert_forward(received, expert_first, expert_second)
-    returned = return_results(result.reshape(received.shape))
-    picked_rows = returned.reshape(-1, model_width)[target].reshape(length, TOPK, model_width)
-    stream = after_attention + jnp.einsum(
-        "sk,skd->sd", gate_values, picked_rows, preferred_element_type=jnp.float32
-    )
-    block_output = stream.astype(jnp.bfloat16)
-    upstream = cotangent.astype(jnp.float32)
-    attention_sums = jax.tree.map(float_zeros, shared)
-    expert_axis = jnp.arange(expert_count, dtype=jnp.int32)
-    repeat_index = 0
-    stream = saved_inputs[repeat_index]
-    after_attention, saved_parts = attention_forward(
-        stream, document_ids, value_ids[repeat_index], output_ids[repeat_index], shared
-    )
-    normed_low, sigmoid_out, gate_values, target, present, safe_index, packet = ffn_prepare(
-        after_attention,
-        gain_feedforward,
-        expert_router,
-        ffn_ids[repeat_index],
-        expert_count,
-        capacity,
-    )
-    upstream_low = upstream.astype(jnp.bfloat16)
-    grad_packet = jnp.where(
-        present[:, None], upstream_low[safe_index // TOPK], jnp.zeros((), jnp.bfloat16)
-    )
-    gate_packet = jnp.where(
-        present, gate_values.reshape(-1)[safe_index], jnp.zeros((), jnp.bfloat16)
-    )
-    grads_in, gates_in = send_grad_only(
-        grad_packet.reshape(owner_total, -1, model_width), gate_packet.reshape(owner_total, -1)
-    )
-    received = lax.all_to_all(
-        packet.reshape(owner_total, -1, model_width),
-        ("dp", "expert"),
-        split_axis=0,
-        concat_axis=0,
-        tiled=True,
-    )
-    shaped, hidden_pre, hidden, result = expert_forward(received, expert_first, expert_second)
-    grads_shaped = grads_in.reshape(shaped.shape)
-    gate_grad = jnp.einsum(
-        "secd,secd->sec", grads_shaped, result, preferred_element_type=jnp.float32
+        stream, segments[0], value_ids[0], output_ids[0], shared
+    )
+    normed_low = layer_norm(after_attention, gain_feedforward).astype(jnp.bfloat16)
+    logits = jnp.dot(normed_low, expert_router, preferred_element_type=jnp.float32)
+    sigmoid_out = jax.nn.sigmoid(logits)
+    mask = expert_mask(ffn_ids[0], expert_count)
+    dense_gates = (sigmoid_out * mask).astype(jnp.bfloat16)
+    result, token_grad, gate_back, first_sum, second_sum = expert_exchange(
+        after_attention.astype(jnp.bfloat16),
+        cotangent,
+        dense_gates,
+        expert_first,
+        expert_second,
+        max(1, owner_total // 32),
+    )
+    block_output = (after_attention + result.astype(jnp.float32)).astype(jnp.bfloat16)
+    logit_grad = (
+        gate_back.astype(jnp.float32) * mask * sigmoid_out * (1.0 - sigmoid_out)
     ).astype(jnp.bfloat16)
-    gates_shaped = gates_in.reshape(shaped.shape[:3]).astype(jnp.float32)
-    result_grad = (gates_shaped[..., None] * grads_shaped.astype(jnp.float32)).astype(jnp.bfloat16)
-    second_sum = jnp.einsum(
-        "secf,secd->efd", hidden, result_grad, preferred_element_type=jnp.float32
-    )
-    hidden_grad = jnp.einsum(
-        "secd,efd->secf", result_grad, expert_second, preferred_element_type=jnp.float32
-    )
-    gelu_value, gelu_pull = jax.vjp(jax.nn.gelu, hidden_pre)
-    pre_grad = gelu_pull(hidden_grad)[0].astype(jnp.bfloat16)
-    first_sum = jnp.einsum("secd,secf->edf", shaped, pre_grad, preferred_element_type=jnp.float32)
-    row_grad = jnp.einsum(
-        "secf,edf->secd", pre_grad, expert_first, preferred_element_type=jnp.float32
-    ).astype(jnp.bfloat16)
-    rows_back, gates_back = return_gradients(
-        row_grad.reshape(received.shape), gate_grad.reshape(gates_in.shape)
-    )
-    token_rows = rows_back.reshape(-1, model_width)[target].reshape(length, TOPK, model_width)
-    token_grad = jnp.sum(token_rows.astype(jnp.float32), axis=1)
-    chosen_grad = (
-        gates_back.reshape(-1)[target].reshape(length, TOPK).astype(jnp.float32)
-        * sigmoid_out
-        * (1.0 - sigmoid_out)
-    )
-    selected = (ffn_ids[repeat_index][:, :, None] == expert_axis[None, None, :]).astype(jnp.float32)
-    logit_grad = jnp.sum(selected * chosen_grad[:, :, None], axis=1).astype(jnp.bfloat16)
     router_sum = jnp.einsum("sa,sb->ab", normed_low, logit_grad, preferred_element_type=jnp.float32)
     normed_grad = jnp.einsum(
         "sb,ab->sa", logit_grad, expert_router, preferred_element_type=jnp.float32
     )
     norm_value, norm_pull = jax.vjp(layer_norm, after_attention, gain_feedforward)
     after_extra, feed_gain_part = norm_pull(normed_grad)
-    after_grad = upstream + token_grad + after_extra
-    upstream, attention_parts = attention_backward(after_grad, saved_parts, stream, shared)
-    attention_sums = jax.tree.map(jnp.add, attention_sums, attention_parts)
+    after_grad = upstream + token_grad.astype(jnp.float32) + after_extra
+    stream_grad, attention_parts = attention_backward(after_grad, saved_parts, stream, shared)
+    gain_part, query_part, key_part, value_part, output_part, value_router_part, output_router_part = attention_parts
+    low = lambda part: part.astype(jnp.bfloat16)
     summed = lax.psum(
         (
-            attention_sums[0],
+            gain_part,
             feed_gain_part,
-            attention_sums[1],
-            attention_sums[2],
-            attention_sums[3],
-            attention_sums[4],
-            attention_sums[5],
-            attention_sums[6],
+            low(query_part),
+            low(key_part),
+            low(value_part),
+            low(output_part),
+            value_router_part,
+            output_router_part,
             router_sum,
         ),
-        ("dp", "expert"),
+        BOTH,
     )
     return (
         block_output,
-        upstream,
-        summed[0],
-        summed[1],
-        summed[2],
-        summed[3],
-        summed[4],
-        summed[5],
-        summed[6],
-        summed[7],
-        summed[8],
+        stream_grad,
+        *(part.astype(jnp.float32) for part in summed),
         first_sum,
         second_sum,
     )

time: 1270 us -> 919 us (0.72)
  local copies, waits for them, and re-layouts: 178 us -> 30.8 us
  waiting for transfers between devices: 725 us -> 612 us
  blocking collectives: 186 us -> 105 us
  matrix products: 83.6 us -> 113 us
  starting transfers between devices: 24.2 us -> 0.71 us
  other arithmetic: 50.1 us -> 35 us
    all_to_all x5 -> x0, waiting for transfers between devices: 377 us -> none  [the longest x1 133 us: send_grad_only(): lax.all_to_all(grad_packet, ('dp', 'expert'), split_axis=0, concat_axis=0...]
    reduce_scatter x0 -> x2, waiting for transfers between devices: none -> 267 us  [the longest x1 150 us: expert_piece(): lax.psum_scatter(row_grad, BOTH, scatter_dimension=0, tiled=True)]
    all_to_all x1, blocking collectives: 146 us -> 10.9 us  [expert_piece(): lax.all_to_all(gate_grad, BOTH, split_axis=0, concat_axis=1, tiled=True)]
    gather x11 -> x0, local copies, waits for them, and re-layouts: 115 us -> none  [the longest x1 23 us: body(): rows_back.reshape(-1, model_width)[target]]
    psum x1 -> x2, waiting for transfers between devices: 348 us -> 269 us  [body(): lax.psum((gain_part, feed_gain_part, low(query_part), low(key_part), low(...]
    all_gather x0 -> x2, waiting for transfers between devices: none -> 75.8 us  [the longest x1 71.4 us: expert_piece(): rows = lax.all_gather(after_low, BOTH, axis=0, tiled=True)]
    all_gather x0 -> x1, blocking collectives: none -> 50.4 us  [expert_piece(): gates = lax.all_gather(dense_gates, BOTH, axis=0, tiled=True)]
    another operation x3 -> x0, other arithmetic: 27.7 us -> none
  transfers between devices with their start and end apart: 6 -> 6, of which waited for: 4 -> 6; matrix products, arithmetic and copies ran while one was open for 7% -> 12% of each run, Pallas kernels for 0% -> 0%
where the time goes in v1:
time: 919 us; the launch traced here: 912 us
  waiting for transfers between devices  612 us (67%)
  matrix products  113 us (12%)
  blocking collectives  105 us (11%)
  other arithmetic  35 us (4%)
  local copies, waits for them, and re-layouts  30.8 us (3%)
  between operations  15.2 us (2%)
    psum x2, waiting for transfers between devices, body(): lax.psum((gain_part, feed_gain_part, low(query_part), low(key_part), low(...  269 us
    reduce_scatter x1, waiting for transfers between devices, expert_piece(): lax.psum_scatter(row_grad, BOTH, scatter_dimension=0, tiled=True)  150 us
    reduce_scatter x1, waiting for transfers between devices, expert_piece(): result = lax.psum_scatter(result, BOTH, scatter_dimension=0, tiled=True)  116 us
    all_gather x1, waiting for transfers between devices, expert_piece(): rows = lax.all_gather(after_low, BOTH, axis=0, tiled=True)  71.4 us
    all_gather x1, blocking collectives, expert_piece(): gates = lax.all_gather(dense_gates, BOTH, axis=0, tiled=True)  50.4 us
    psum x1, blocking collectives, body(): lax.psum((gain_part, feed_gain_part, low(query_part), low(key_part), low(...  43.7 us
    unnamed x87, local copies, waits for them, and re-layouts  20.7 us
  transfers between devices with their start and end apart: 6, of which 6 were waited for; matrix products, arithmetic and copies ran while one was open for 12% of the time, Pallas kernels for 0%

profile of v1, /device:TPU:1, one launch (start us, length us, event | category | flops | bytes accessed | tf_op | source)
XLA Modules:
  0.0 912.0 jit_solution(10678073523756943204)
XLA Ops:
  16.6 1.6 convolution_convert_fusion.9
  18.3 4.7 fusion.58
  24.9 1.8 convolution_bitcast_fusion
  28.7 3.5 fusion.57
  33.5 2.3 copy.135
  35.9 1.9 multiply_convert_fusion.6
  37.8 50.4 %all_gather.9 = bf16[4096,96]{0,1:T(8,128)(2,1)S(1)} all-gather(bf16[128,96]{0,1:T(8,128)(2,1)S(1)} %get-tuple-element.107), channel_id=1, replica_groups=mesh['dp'=4,'expert'=8] {'dp','expert'}, dimensions={0}, use_global_device_ids=true | all-gather | bytes 811008 | tf_op jit(solution)/shard_map/all_gather | solution.py:266
  88.2 4.5 all-gather.5.cloned.1.call-done
  92.6 9.7 %fusion.59 = f32[4096,384]{0,1:T(8,128)} fusion(bf16[4096,1024]{1,0:T(8,128)(2,1)} %all-gather.5.cloned.1.call-done, bf16[384,1024]{1,0:T(8,128)(2,1)} %bitcast.142), kind=kOutput, calls=%fused_computation.130 | convolution fusion | flops 3221225472 | bytes 15466496 | tf_op jit(solution)/shard_map/sd,fd->sf/dot_general | solution.py:239
  102.3 71.4 %all-gather.3.cloned.1.call-done = bf16[4096,1024]{1,0:T(8,128)(2,1)} async-done(((bf16[128,1024]{1,0:T(8,128)(2,1)}), bf16[4096,1024]{1,0:T(8,128)(2,1)}) %all-gather.3.cloned.1.call-update) | async-done | bytes 8388624 | tf_op jit(solution)/shard_map/all_gather | solution.py:265
  173.7 13.8 %fusion.7 = (bf16[4096,384]{0,1:T(8,128)(2,1)}, f32[4096,384]{0,1:T(8,128)}, bf16[4096,384]{0,1:T(8,128)(2,1)S(1)}) fusion(f32[4096,384]{0,1:T(8,128)} %fusion.59, f32[4096,3]{0,1:T(4,128)S(1)} %dynamic-slice_convert_fusion, bf16[4096,1024]{1,0:T(8,128)(2,1)} %all-gather.3.cloned.1.call-done, bf16[1024,384]{0,1:T(8,128)(2,1)} %bitcast.125), kind=kOutput, calls=%fused_computation.14 | convolution fusion | flops 3263692800 | bytes 28098560 | tf_op jit(solution)/shard_map/dot_general | solution.py:235
  187.5 1.7 copy-done.6
  189.2 6.8 convolution_convert_fusion.1
  196.3 10.0 %convolution_convert_fusion = bf16[4096,1024]{1,0:T(8,128)(2,1)} fusion(bf16[4096,384]{0,1:T(8,128)(2,1)} %get-tuple-element.95, bf16[1024,384]{0,1:T(8,128)(2,1)} %bitcast.126), kind=kOutput, calls=%fused_computation.6 | convolution fusion | flops 3225419776 | bytes 12320768 | tf_op jit(solution)/shard_map/sf,df->sd/dot_general | solution.py:243
  206.5 3.2 reduce_sum.190
  209.6 10.9 %all_to_all.10 = bf16[32,128,3]{1,2,0:T(4,128)(2,1)S(1)} all-to-all(bf16[32,128,3]{1,2,0:T(4,128)(2,1)S(1)} %bitcast.137), channel_id=1, replica_groups=mesh['dp'=4,'expert'=8] {'dp','expert'}, dimensions={0} | all-to-all | bytes 49152 | tf_op jit(solution)/shard_map/all_to_all | solution.py:271
  222.7 2.6 multiply_reduce_fusion.4
  226.0 116.3 %reduce-scatter.3.cloned.1.call-done = bf16[128,1024]{1,0:T(8,128)(2,1)} async-done(((bf16[4096,1024]{1,0:T(8,128)(2,1)}), bf16[128,1024]{1,0:T(8,128)(2,1)}) %reduce-scatter.3.cloned.1.call-update) | async-done | bytes 262160 | tf_op jit(solution)/shard_map/reduce_scatter | solution.py:273
  342.2 2.2 fusion.54
  344.4 150.5 %reduce-scatter.5.cloned.1.call-done = bf16[128,1024]{1,0:T(8,128)(2,1)} async-done(((bf16[4096,1024]{1,0:T(8,128)(2,1)}), bf16[128,1024]{1,0:T(8,128)(2,1)}) %reduce-scatter.5.cloned.1.call-update) | async-done | bytes 262160 | tf_op jit(solution)/shard_map/reduce_scatter | solution.py:272
  494.9 1.3 add_add_fusion.2
  497.0 5.4 fusion.10
  502.4 2.8 copy.137
  505.2 2.3 multiply_reduce_fusion
  507.5 2.1 fusion.19
  509.6 1.3 multiply_reduce_fusion.7
  511.9 1.8 fusion.20
  513.7 1.8 fusion.21
  515.5 5.0 convolution_convert_fusion.2
  523.4 1.4 convolution_convert_fusion.5
  524.8 1.4 convolution_convert_fusion.6
  526.2 3.9 fusion.9
  530.4 8.9 fusion.67
  539.3 3.0 copy.153
  542.4 9.3 %fusion.65 = f32[384,1024]{1,0:T(8,128)} fusion(bf16[4096,384]{0,1:T(8,128)(2,1)} %copy-done.6, bf16[4096,1024]{1,0:T(8,128)(2,1)} %all-gather.5.cloned.1.call-done), kind=kOutput, calls=%fused_computation.136 | convolution fusion | flops 3221225472 | bytes 13107200 | tf_op jit(solution)/shard_map/sf,sd->fd/dot_general | solution.py:244
  553.4 1.7 fusion.60
  558.1 43.7 %all-reduce = (f32[1024]{0:T(1024)}, f32[1024]{0:T(1024)}) all-reduce(f32[1024]{0:T(1024)S(1)} %get-tuple-element.82, f32[1024]{0:T(1024)S(1)} %copy-done.30), channel_id=1, replica_groups=mesh['dp'=4,'expert'=8] {'dp','expert'}, use_global_device_ids=true, to_apply=%region_22.23 | all-reduce | flops 2048 | bytes 16384 | tf_op jit(solution)/shard_map/psum | solution.py:360
  601.8 1.5 fusion.64
  604.1 5.2 convolution_add_fusion.1
  609.3 155.2 %all-reduce.8.cloned.1.call-done = (bf16[1024,512]{1,0:T(8,128)(2,1)}, bf16[1024,512]{1,0:T(8,128)(2,1)}, bf16[1024,2560]{0,1:T(8,128)(2,1)}, bf16[2560,1024]{1,0:T(8,128)(2,1)}) async-done(((bf16[1024,512]{1,0:T(8,128)(2,1)}, bf16[1024,512]{1,0:T(8,128)(2,1)}, bf16[1024,2560]{0,1:T(8,128)(2,1)}, bf16[2560,1024]{1,0:T(8,128)(2,1)}), (bf16[1024,512]{1,0:T(8,128)(2,1)}, bf16[1024,512]{1,0:T(8,128)(2,1)}, ...) | async-done | bytes 12582928 | tf_op jit(solution)/shard_map/psum | solution.py:360
  764.5 2.8 convert_element_type.226
  767.3 2.8 convert_element_type.228
  770.2 8.2 copy.154
  778.4 7.9 convert_element_type.233
  786.3 113.6 %all-reduce.6.cloned.1.call-done = (f32[1024,20]{0,1:T(8,128)}, f32[1024,20]{0,1:T(8,128)}, f32[1024,96]{0,1:T(8,128)}) async-done(((f32[1024,20]{0,1:T(8,128)}, f32[1024,20]{0,1:T(8,128)}, f32[1024,96]{0,1:T(8,128)}), (f32[1024,20]{0,1:T(8,128)}, f32[1024,20]{0,1:T(8,128)}, f32[1024,96]{0,1:T(8,128)})) %all-reduce.6.cloned.1.call-update) | async-done | bytes 557072 | tf_op jit(solution)/shard_map/psum | solution.py:360
  899.9 1.5 copy.177
  901.4 1.5 copy.178
  902.9 1.8 copy.179
  (149 shorter events, 27.9 us)
Async XLA Ops:
  7.2 9.0 copy-start
  7.2 11.1 %copy-start.1 = (bf16[128,1024]{1,0:T(8,128)(2,1)S(1)}, bf16[128,1024]{1,0:T(8,128)(2,1)}, u32[]{:S(2)}) copy-start(bf16[128,1024]{1,0:T(8,128)(2,1)} %param.17) | copy-start | bytes 786436
  7.2 85.4 %all-gather.5.cloned.1.call-start = ((), (), s32[]{:S(2)}) async-start(), calls=%async_computation.5 | async-start | bytes 8650752 | tf_op jit(solution)/shard_map/all_gather | solution.py:264
  7.9 165.7 %all-gather.3.cloned.1.call-start = ((), (), s32[]{:S(2)}) async-start(), calls=%async_computation.3 | async-start | bytes 8650752 | tf_op jit(solution)/shard_map/all_gather | solution.py:265
  10.4 3.4 copy-start.31
  11.6 2.9 copy-start.38
  11.6 2.2 copy-start.36
  13.8 1.7 copy-start.17
  13.9 0.6 copy-start.21
  14.5 12.3 %copy-start.16 = (f32[128,4,5]{0,2,1:T(8,128)}, f32[128,4,5]{0,2,1:T(8,128)S(1)}, u32[]{:S(2)}) copy-start(f32[128,4,5]{0,2,1:T(8,128)S(1)} %copy.127) | copy-start | bytes 30724
  15.5 0.6 copy-start.19
  15.5 0.6 copy-start.23
  16.5 7.3 copy-start.37
  16.6 7.5 copy-start.8
  18.3 8.4 copy-start.9
  23.8 8.7 copy-start.29
  24.1 3.7 copy-start.10
  24.9 7.3 copy-start.32
  27.9 0.8 copy-start.2
  27.9 7.9 copy-start.33
  32.4 3.4 copy-start.39
  32.4 3.4 copy-start.34
  33.4 308.8 %reduce-scatter.3.cloned.1.call-start = ((), (), s32[]{:S(2)}) async-start(), calls=%async_computation.4 | async-start | bytes 8650752 | tf_op jit(solution)/shard_map/reduce_scatter | solution.py:273
  173.7 15.6 %copy-start.40 = (bf16[3,128,1024]{2,1,0:T(8,128)(2,1)S(1)}, bf16[3,128,1024]{2,1,0:T(8,128)(2,1)}, u32[]{:S(2)}) copy-start(bf16[3,128,1024]{2,1,0:T(8,128)(2,1)} %param.29) | copy-start | bytes 2359300
  187.5 1.8 copy-start.6
  196.1 298.8 %reduce-scatter.5.cloned.1.call-start = ((), (), s32[]{:S(2)}) async-start(), calls=%async_computation.6 | async-start | bytes 8650752 | tf_op jit(solution)/shard_map/reduce_scatter | solution.py:272
  206.4 16.3 %copy-start.35 = (f32[128]{0:T(128)S(1)}, f32[128]{0:T(128)}, u32[]{:S(2)}) copy-start(f32[128]{0:T(128)} %copy-done.34) | copy-start | bytes 1540
  206.4 558.1 %all-reduce.8.cloned.1.call-start = ((), (), s32[]{:S(2)}) async-start(), calls=%async_computation.8 | async-start | bytes 25165824 | tf_op jit(solution)/shard_map/psum | solution.py:360
  222.1 0.6 copy-start.12
  496.2 0.8 copy-start.4
  502.4 13.1 %copy-start.3 = (bf16[128,4,5,128]{0,3,2,1:T(8,128)(2,1)S(1)}, bf16[128,4,5,128]{0,3,2,1:T(8,128)(2,1)}, u32[]{:S(2)}) copy-start(bf16[128,4,5,128]{0,3,2,1:T(8,128)(2,1)} %copy-done.2) | copy-start | bytes 1966084
  515.5 5.0 copy-start.11
  530.1 369.7 %all-reduce.6.cloned.1.call-start = ((), (), s32[]{:S(2)}) async-start(), calls=%async_computation.7 | async-start | bytes 1179648 | tf_op jit(solution)/shard_map/psum | solution.py:360
  542.3 9.4 %copy-start.7 = (bf16[128,1024]{1,0:T(8,128)(2,1)S(1)}, bf16[128,1024]{1,0:T(8,128)(2,1)}, u32[]{:S(2)}) copy-start(bf16[128,1024]{1,0:T(8,128)(2,1)} %get-tuple-element.100) | copy-start | bytes 786436
  542.3 9.4 %copy-start.13 = (bf16[128,96]{0,1:T(8,128)(2,1)S(1)}, bf16[128,96]{0,1:T(8,128)(2,1)}, u32[]{:S(2)}) copy-start(bf16[128,96]{0,1:T(8,128)(2,1)} %copy-done.12) | copy-start | bytes 73732
  542.3 10.4 %copy-start.24 = (f32[128,4,5]{0,1,2:T(4,128)S(1)}, f32[128,4,5]{0,1,2:T(4,128)}, u32[]{:S(2)}) copy-start(f32[128,4,5]{0,1,2:T(4,128)} %copy-done.23) | copy-start | bytes 30724
  542.3 10.4 %copy-start.27 = (f32[128,4,5]{0,2,1:T(8,128)S(1)}, f32[128,4,5]{0,2,1:T(8,128)}, u32[]{:S(2)}) copy-start(f32[128,4,5]{0,2,1:T(8,128)} %get-tuple-element.101) | copy-start | bytes 30724
  542.3 10.4 %copy-start.22 = (f32[128,4,5]{0,1,2:T(4,128)S(1)}, f32[128,4,5]{0,1,2:T(4,128)}, u32[]{:S(2)}) copy-start(f32[128,4,5]{0,1,2:T(4,128)} %copy-done.21) | copy-start | bytes 30724
  542.4 10.4 %copy-start.26 = (f32[128,4,5]{0,2,1:T(8,128)S(1)}, f32[128,4,5]{0,2,1:T(8,128)}, u32[]{:S(2)}) copy-start(f32[128,4,5]{0,2,1:T(8,128)} %get-tuple-element.78) | copy-start | bytes 30724
  542.4 10.4 %copy-start.20 = (f32[128,20]{0,1:T(8,128)S(1)}, f32[128,20]{0,1:T(8,128)}, u32[]{:S(2)}) copy-start(f32[128,20]{0,1:T(8,128)} %copy-done.19) | copy-start | bytes 30724
  542.4 10.4 %copy-start.18 = (f32[128,20]{0,1:T(8,128)S(1)}, f32[128,20]{0,1:T(8,128)}, u32[]{:S(2)}) copy-start(f32[128,20]{0,1:T(8,128)} %copy-done.17) | copy-start | bytes 30724
  542.4 10.4 %copy-start.14 = (bf16[1024,20]{0,1:T(8,128)(2,1)S(1)}, bf16[1024,20]{0,1:T(8,128)(2,1)}, u32[]{:S(2)}) copy-start(bf16[1024,20]{0,1:T(8,128)(2,1)} %param.25) | copy-start | bytes 122884
  542.4 10.7 %copy-start.15 = (bf16[1024,20]{0,1:T(8,128)(2,1)S(1)}, bf16[1024,20]{0,1:T(8,128)(2,1)}, u32[]{:S(2)}) copy-start(bf16[1024,20]{0,1:T(8,128)(2,1)} %param.26) | copy-start | bytes 122884
  542.4 12.7 %copy-start.25 = (f32[1024]{0:T(1024)S(1)}, f32[1024]{0:T(1024)}, u32[]{:S(2)}) copy-start(f32[1024]{0:T(1024)} %param.19) | copy-start | bytes 12292
  551.7 6.3 copy-start.30
  551.7 52.4 %copy-start.5 = (f32[128,1024]{1,0:T(8,128)S(1)}, f32[128,1024]{1,0:T(8,128)}, u32[]{:S(2)}) copy-start(f32[128,1024]{1,0:T(8,128)} %copy-done.4) | copy-start | bytes 1572868
  552.8 0.6 copy-start.28
Sparse Core Ops, SparseCore 0:
  11.0 81.5 all-gather.4
  96.2 77.4 all-gather.2
  196.2 146.0 reduce-scatter.2
  345.0 149.8 reduce-scatter.4
  530.2 234.1 all-reduce.7
  770.6 129.2 all-reduce.5

commit v2 on v1

--- a/solution.py
+++ b/solution.py
@@ -1,8 +1,11 @@
+import functools
 import math
 
 import jax
 import jax.numpy as jnp
 from jax import lax
+from jax.experimental import pallas as pl
+from jax.experimental.pallas import tpu as pltpu
 from jax.sharding import PartitionSpec as P
 
 HEADS = 4
@@ -294,6 +297,663 @@
     return (*(part.reshape(-1, part.shape[2]) for part in back), *sums)
 
 
+MESH = pl.DeviceIdType.MESH
+GRID = (4, 8)
+
+
+class Place:
+    def __init__(self):
+        dp, expert = lax.axis_index("dp"), lax.axis_index("expert")
+        self.y, self.x = dp // 2, dp % 2
+        self.z, self.core = expert // 2, expert % 2
+        self.dp, self.expert = dp, expert
+        self.me = dp * GRID[1] + expert
+        self.x_peer = (2 * self.y + 1 - self.x, expert)
+        self.y_peer = (2 * (1 - self.y) + self.x, expert)
+        self.core_peer = (dp, 2 * self.z + 1 - self.core)
+
+    def z_at(self, j):
+        return 2 * ((self.z // 2 + j // 2) % 2) + (self.z % 2 + j % 2) % 2
+
+    def z_peer(self, j):
+        return (self.dp, 2 * self.z_at(j) + self.core)
+
+    def peers(self):
+        return [self.x_peer, self.y_peer, self.core_peer] + [self.z_peer(j) for j in (1, 2, 3)]
+
+    def chip(self, q, j):
+        return ((self.y + q // 2) % 2 * 2 + (self.x + q % 2) % 2) * 4 + self.z_at(j)
+
+
+def enter(place):
+    barrier = pltpu.get_barrier_semaphore()
+    peers = place.peers()
+    for peer in peers:
+        pl.semaphore_signal(barrier, inc=1, device_id=peer, device_id_type=MESH)
+    pl.semaphore_wait(barrier, len(peers))
+
+
+def remote(src, dst, send, recv, peer):
+    return pltpu.make_async_remote_copy(
+        src_ref=src,
+        dst_ref=dst,
+        send_sem=send,
+        recv_sem=recv,
+        device_id=peer,
+        device_id_type=MESH,
+    )
+
+
+N_SEM = 35
+
+
+class Gather:
+    def __init__(self, place, buf, rows, split, sems):
+        self.place, self.buf, self.rows, self.split = place, buf, rows, split
+        self.send, self.recv = sems.at[0], sems.at[1]
+
+    def block(self, q, j, part=None):
+        start = (2 * self.place.chip(q, j) + self.place.core) * self.rows
+        rows = pl.ds(pl.multiple_of(start, self.rows), self.rows)
+        if part == "b":
+            return self.buf.at[rows, : self.split]
+        if part == "a":
+            return self.buf.at[rows, self.split :]
+        return self.buf.at[rows]
+
+    def copy(self, kind, j, q=0):
+        place = self.place
+        if kind == "z":
+            ref, number, peer = self.block(0, 0), j - 1, place.z_peer(j)
+        elif kind == "x":
+            ref, number, peer = self.block(0, j), 3 + j, place.x_peer
+        elif kind == "y":
+            ref, number, peer = self.block(0, j), 7 + j, place.y_peer
+        elif kind == "a":
+            ref, number, peer = self.block(1, j, "a"), 11 + j, place.y_peer
+        elif kind == "b":
+            ref, number, peer = self.block(2, j, "b"), 15 + j, place.x_peer
+        else:
+            ref, number, peer = self.block(q, j), 19 + 4 * q + j, place.core_peer
+        return remote(ref, ref, self.send.at[number], self.recv.at[number], peer)
+
+    def line(self, j, first):
+        if not first:
+            self.copy("z", j).wait_recv()
+        self.copy("x", j).start()
+        self.copy("y", j).start()
+        self.copy("core", j, 0).start()
+
+    def side_x(self, j):
+        self.copy("x", j).wait_recv()
+        self.copy("a", j).start()
+        self.copy("core", j, 1).start()
+
+    def side_y(self, j):
+        self.copy("y", j).wait_recv()
+        self.copy("b", j).start()
+        self.copy("core", j, 2).start()
+
+    def corner(self, j):
+        self.copy("a", j).wait_recv()
+        self.copy("b", j).wait_recv()
+        self.copy("core", j, 3).start()
+
+    def whole(self, q, j):
+        self.copy("core", j, q).wait_recv()
+
+    def finish(self):
+        for j in (1, 2, 3):
+            self.copy("z", j).wait_send()
+
+        def step(j, carry):
+            for kind in ("x", "y", "a", "b"):
+                self.copy(kind, j).wait_send()
+            for q in range(4):
+                self.copy("core", j, q).wait_send()
+            return carry
+
+        lax.fori_loop(0, 4, step, 0)
+
+
+class Reduce:
+    def __init__(self, place, own, other, other_in, a_in, b_in, x_in, y_in, z_in, split, sems):
+        self.place, self.own, self.other, self.other_in = place, own, other, other_in
+        self.a_in, self.b_in, self.x_in, self.y_in, self.z_in = a_in, b_in, x_in, y_in, z_in
+        self.split = split
+        self.send, self.recv = sems.at[0], sems.at[1]
+
+    def copy(self, kind, k):
+        place, split = self.place, self.split
+        j = k % 4
+        if kind == "core":
+            src, dst, number, peer = self.other(k), self.other_in.at[k], k, place.core_peer
+        elif kind == "a":
+            src, dst, number, peer = self.own(k).at[:, split:], self.a_in.at[j], 16 + j, place.y_peer
+        elif kind == "b":
+            src, dst, number, peer = self.own(k).at[:, :split], self.b_in.at[j], 20 + j, place.x_peer
+        elif kind == "x":
+            src, dst, number, peer = self.own(k), self.x_in.at[j], 24 + j, place.x_peer
+        elif kind == "y":
+            src, dst, number, peer = self.own(k), self.y_in.at[j], 28 + j, place.y_peer
+        else:
+            src, dst, number, peer = self.own(k), self.z_in.at[j - 1], 31 + j, place.z_peer(j)
+        return remote(src, dst, self.send.at[number], self.recv.at[number], peer)
+
+    def add(self, k, columns, terms):
+        own = self.own(k)
+        rows = own.shape[0]
+
+        def step(number, carry):
+            at = pl.ds(pl.multiple_of(number * 16, 16), 16)
+            total = own[at, columns].astype(jnp.float32)
+            for term in terms:
+                total = total + term(at).astype(jnp.float32)
+            own[at, columns] = total.astype(own.dtype)
+            return carry
+
+        lax.fori_loop(0, rows // 16, step, 0)
+
+    def corner(self, j):
+        k = 12 + j
+        self.copy("core", k).wait_recv()
+        self.add(k, slice(None), [lambda at: self.other_in[k, at, :]])
+        self.copy("a", k).start()
+        self.copy("b", k).start()
+
+    def side_x(self, j):
+        k, split = 4 + j, self.split
+        self.copy("core", k).wait_recv()
+        self.add(k, slice(0, split), [lambda at: self.other_in[k, at, :split]])
+        self.copy("a", k).wait_recv()
+        self.add(
+            k,
+            slice(split, None),
+            [lambda at: self.other_in[k, at, split:], lambda at: self.a_in[j, at, :]],
+        )
+        self.copy("x", k).start()
+
+    def side_y(self, j):
+        k, split = 8 + j, self.split
+        self.copy("core", k).wait_recv()
+        self.add(k, slice(split, None), [lambda at: self.other_in[k, at, split:]])
+        self.copy("b", k).wait_recv()
+        self.add(
+            k,
+            slice(0, split),
+            [lambda at: self.other_in[k, at, :split], lambda at: self.b_in[j, at, :]],
+        )
+        self.copy("y", k).start()
+
+    def line(self, j):
+        self.copy("core", j).wait_recv()
+        self.copy("x", j).wait_recv()
+        self.copy("y", j).wait_recv()
+        boxes = (self.other_in, self.x_in, self.y_in)
+        self.add(j, slice(None), [lambda at, box=box: box[j, at, :] for box in boxes])
+        self.copy("z", j).start()
+
+    def last(self, put):
+        self.copy("core", 0).wait_recv()
+        self.copy("x", 0).wait_recv()
+        self.copy("y", 0).wait_recv()
+        for j in (1, 2, 3):
+            self.copy("z", j).wait_recv()
+        own = self.own(0)
+
+        def step(number, carry):
+            at = pl.ds(pl.multiple_of(number * 16, 16), 16)
+            total = own[at, :].astype(jnp.float32)
+            for box in (self.other_in, self.x_in, self.y_in):
+                total = total + box[0, at, :].astype(jnp.float32)
+            for j in range(3):
+                total = total + self.z_in[j, at, :].astype(jnp.float32)
+            put(at, total)
+            return carry
+
+        lax.fori_loop(0, own.shape[0] // 16, step, 0)
+
+    def finish(self):
+        def step(j, carry):
+            for kind, q in (("a", 3), ("b", 3), ("x", 1), ("y", 2)):
+                self.copy(kind, 4 * q + j).wait_send()
+            for q in range(4):
+                self.copy("core", 4 * q + j).wait_send()
+            return carry
+
+        lax.fori_loop(0, 4, step, 0)
+        for j in (1, 2, 3):
+            self.copy("z", j).wait_send()
+
+
+def reduce_scratch(rows, width, split):
+    low = jnp.bfloat16
+    return [
+        pltpu.VMEM((16, rows, width), low),
+        pltpu.VMEM((4, rows, width - split), low),
+        pltpu.VMEM((4, rows, split), low),
+        pltpu.VMEM((4, rows, width), low),
+        pltpu.VMEM((4, rows, width), low),
+        pltpu.VMEM((3, rows, width), low),
+    ]
+
+
+GELU_C = math.sqrt(2.0 / math.pi)
+GELU_K = 0.044715
+
+
+def mm(left, right):
+    return jnp.dot(left, right, preferred_element_type=jnp.float32)
+
+
+def mm_tn(left, right):
+    return lax.dot_general(left, right, (((0,), (0,)), ((), ())), preferred_element_type=jnp.float32)
+
+
+def expert_kernel(
+    model_width,
+    local_count,
+    packed_ref,
+    first_ref,
+    first_t_ref,
+    second_ref,
+    second_t_ref,
+    pick_ref,
+    rows_out,
+    result_out,
+    first_out,
+    second_out,
+    gathered,
+    gated_hidden,
+    pre_grads,
+    partial,
+    other_in,
+    a_in,
+    b_in,
+    x_in,
+    y_in,
+    z_in,
+    result_stage,
+    gather_sems,
+    reduce_sems,
+    result_sems,
+):
+    place = Place()
+    length = packed_ref.shape[0]
+    pair = 2 * length
+    half = model_width // 2
+    gate_width = pick_ref.shape[0]
+    hidden_width = first_ref.shape[1] // local_count
+    split = model_width
+    enter(place)
+    gather = Gather(place, gathered, length, split, gather_sems)
+    gathered[pl.ds(pl.multiple_of(place.me * length, length), length), :] = packed_ref[...]
+
+    def own(k):
+        return partial.at[k, pl.ds(pl.multiple_of(place.core * length, length), length)]
+
+    def other(k):
+        return partial.at[k, pl.ds(pl.multiple_of((1 - place.core) * length, length), length)]
+
+    reduce = Reduce(
+        place,
+        own,
+        other,
+        other_in,
+        a_in,
+        b_in,
+        x_in,
+        y_in,
+        z_in,
+        model_width // 2,
+        reduce_sems,
+    )
+
+    def result_copy(slot, chip):
+        return pltpu.make_async_copy(
+            result_stage.at[slot],
+            result_out.at[pl.ds(pl.multiple_of(chip * pair, pair), pair)],
+            result_sems.at[slot],
+        )
+
+    def compute(step, q, j):
+        chip = place.chip(q, j)
+        rows = pl.ds(pl.multiple_of(chip * pair, pair), pair)
+        hidden_pre = mm(gathered[rows, half : half + model_width], first_ref[...])
+        back = mm(gathered[rows, :half], second_t_ref[:half])
+        back = back + mm(gathered[rows, 3 * half + gate_width :], second_t_ref[half:])
+        gates = mm(gathered[rows, 3 * half : 3 * half + gate_width], pick_ref[...])
+        square = hidden_pre * hidden_pre
+        bent = jnp.tanh(GELU_C * hidden_pre * (1.0 + GELU_K * square))
+        grow = 0.5 * (1.0 + bent)
+        slope = grow + 0.5 * hidden_pre * (1.0 - bent * bent) * (
+            GELU_C * (1.0 + 3.0 * GELU_K * square)
+        )
+        hidden = (hidden_pre * grow).astype(jnp.bfloat16).astype(jnp.float32)
+        gated = (gates * hidden).astype(jnp.bfloat16)
+        pre_grad = (gates * back * slope).astype(jnp.bfloat16)
+        gated_hidden[rows, :] = gated
+        pre_grads[rows, :] = pre_grad
+        k = 4 * q + j
+        partial[k, :, :model_width] = mm(pre_grad, first_t_ref[...]).astype(jnp.bfloat16)
+        product = hidden * back
+        column = lax.broadcasted_iota(jnp.int32, (pair, gate_width), 1) - place.me * local_count
+        gate_grad = jnp.zeros((pair, gate_width), jnp.float32)
+        for e in range(local_count):
+            own_sum = jnp.sum(
+                product[:, e * hidden_width : (e + 1) * hidden_width], axis=1, keepdims=True
+            )
+            gate_grad = jnp.where(column == e, own_sum, gate_grad)
+        partial[k, :, model_width:] = gate_grad.astype(jnp.bfloat16)
+        reduce.copy("core", k).start()
+        slot = step % 2
+
+        @pl.when(step >= 2)
+        def _():
+            result_copy(slot, chip).wait()
+
+        result_stage[slot] = mm(gated, second_ref[...]).astype(jnp.bfloat16)
+        result_copy(slot, chip).start()
+
+    gather.copy("z", 1).start()
+    gather.line(0, True)
+    gather.copy("z", 2).start()
+    gather.copy("z", 3).start()
+
+    def arrive(actions):
+        for kind, j in actions:
+            if kind == "line":
+                gather.line(j, False)
+            else:
+                getattr(gather, kind)(j)
+
+    before = {
+        1: [("side_x", 0), ("side_y", 0), ("line", 1)],
+        4: [("corner", 0), ("side_x", 1), ("side_y", 1), ("line", 2)],
+        8: [("corner", 1), ("side_x", 2), ("side_y", 2), ("line", 3)],
+        12: [("corner", 2), ("side_x", 3), ("side_y", 3)],
+        15: [("corner", 3)],
+    }
+    order = [(0, 0), (1, 0), (2, 0), (0, 1), (3, 0), (1, 1), (2, 1), (0, 2)]
+    order += [(3, 1), (1, 2), (2, 2), (0, 3), (3, 2), (1, 3), (2, 3), (3, 3)]
+
+    def pick(step, values):
+        total = 0
+        for number, value in enumerate(values):
+            total = total + value * jnp.where(step == number, 1, 0)
+        return total
+
+    def walk(step, carry):
+        for number, actions in before.items():
+            pl.when(step == number)(functools.partial(arrive, actions))
+        q = pick(step, [pair_[0] for pair_ in order])
+        j = pick(step, [pair_[1] for pair_ in order])
+        gather.whole(q, j)
+        compute(step, q, j)
+        return carry
+
+    lax.fori_loop(0, 16, walk, 0)
+    piece = 512
+    pieces = gathered.shape[0] // piece
+
+    def weight_piece(number):
+        rows = pl.ds(pl.multiple_of(number * piece, piece), piece)
+        left = mm_tn(gated_hidden[rows, :], gathered[rows, :half])
+        right = mm_tn(gated_hidden[rows, :], gathered[rows, 3 * half + gate_width :])
+        first = mm_tn(pre_grads[rows, :], gathered[rows, half : half + model_width])
+
+        @pl.when(number == 0)
+        def _():
+            second_out[:, :half] = left
+            second_out[:, half:] = right
+            first_out[...] = first
+
+        @pl.when(number > 0)
+        def _():
+            second_out[:, :half] += left
+            second_out[:, half:] += right
+            first_out[...] += first
+
+    def give(step, carry):
+        j = 3 - step % 4
+
+        @pl.when(step < 4)
+        def _():
+            reduce.corner(j)
+
+        @pl.when(step >= 4)
+        def _():
+            reduce.side_x(j)
+            reduce.side_y(j)
+
+        weight_piece(step)
+        return carry
+
+    lax.fori_loop(0, pieces, give, 0)
+    lax.fori_loop(0, 3, lambda step, carry: (reduce.line(3 - step), carry)[1], 0)
+
+    def put(at, total):
+        rows_out[at, :] = total
+
+    reduce.last(put)
+    for slot in range(2):
+        result_copy(slot, 0).wait()
+    gather.finish()
+    reduce.finish()
+
+
+def call_experts(packed, expert_first, expert_second, pick):
+    local_count, model_width, hidden_width = expert_first.shape
+    wide = local_count * hidden_width
+    length, width = packed.shape
+    total = GRID[0] * GRID[1] * length
+    gate_width = pick.shape[0]
+    first = expert_first.transpose(1, 0, 2).reshape(model_width, wide)
+    first_t = expert_first.transpose(0, 2, 1).reshape(wide, model_width)
+    second = expert_second.reshape(wide, model_width)
+    second_t = expert_second.transpose(2, 0, 1).reshape(model_width, wide)
+    out_width = model_width + gate_width
+    split = model_width // 2
+    vmem = pl.BlockSpec(memory_space=pltpu.VMEM)
+    flops = 12 * total * model_width * wide
+    rows_sum, result, first_sum, second_sum = pl.pallas_call(
+        functools.partial(expert_kernel, model_width, local_count),
+        out_shape=(
+            jax.ShapeDtypeStruct((length, out_width), jnp.float32),
+            jax.ShapeDtypeStruct((total, model_width), jnp.bfloat16),
+            jax.ShapeDtypeStruct((wide, model_width), jnp.float32),
+            jax.ShapeDtypeStruct((wide, model_width), jnp.float32),
+        ),
+        in_specs=[vmem] * 6,
+        out_specs=(vmem, pl.BlockSpec(memory_space=pl.ANY), vmem, vmem),
+        scratch_shapes=[
+            pltpu.VMEM((total, width), jnp.bfloat16),
+            pltpu.VMEM((total, wide), jnp.bfloat16),
+            pltpu.VMEM((total, wide), jnp.bfloat16),
+            pltpu.VMEM((16, 2 * length, out_width), jnp.bfloat16),
+            *reduce_scratch(length, out_width, split),
+            pltpu.VMEM((2, 2 * length, model_width), jnp.bfloat16),
+            pltpu.SemaphoreType.DMA((2, N_SEM)),
+            pltpu.SemaphoreType.DMA((2, N_SEM)),
+            pltpu.SemaphoreType.DMA((2,)),
+        ],
+        compiler_params=pltpu.CompilerParams(
+            collective_id=0, has_side_effects=True, vmem_limit_bytes=62 * 2**20
+        ),
+        cost_estimate=pl.CostEstimate(
+            flops=flops, bytes_accessed=4 * total * model_width, transcendentals=total * wide
+        ),
+        name="experts",
+    )(packed, first, first_t, second, second_t, pick)
+    first_sum = first_sum.reshape(local_count, hidden_width, model_width).transpose(0, 2, 1)
+    return rows_sum, result, first_sum, second_sum.reshape(expert_second.shape)
+
+
+def sums_kernel(shapes, *refs):
+    count = len(shapes)
+    ins, refs = refs[:count], refs[count:]
+    first_out, outs, refs = refs[0], refs[1:count], refs[count:]
+    place = Place()
+    enter(place)
+    reduces, gathers, loads = [], [], []
+    for number, (rows, width, split) in enumerate(shapes):
+        held, refs = refs[0], refs[1:]
+        boxes, refs = refs[:6], refs[6:]
+        sems, load_sem, refs = refs[0], refs[1], refs[2:]
+
+        def source(k, core, rows=rows, ref=ins[number]):
+            start = (2 * place.chip(k // 4, k % 4) + core) * rows
+            return ref.at[pl.ds(pl.multiple_of(start, rows), rows)]
+
+        reduces.append(
+            Reduce(
+                place,
+                lambda k, held=held: held.at[k],
+                lambda k, source=source: source(k, 1 - place.core),
+                *boxes,
+                split,
+                sems,
+            )
+        )
+        loads.append(
+            lambda k, source=source, held=held, sem=load_sem: pltpu.make_async_copy(
+                source(k, place.core), held.at[k], sem.at[k]
+            )
+        )
+        if number:
+            buf, gather_sems, out_sem, refs = refs[0], refs[1], refs[2], refs[3:]
+            gathers.append((Gather(place, buf, rows, split, gather_sems), outs[number - 1], out_sem))
+
+    def begin(step, carry):
+        k = 15 - step
+        for reduce, load in zip(reduces, loads):
+            load(k).start()
+            reduce.copy("core", k).start()
+        return carry
+
+    lax.fori_loop(0, 16, begin, 0)
+
+    def corner(step, carry):
+        for reduce, load in zip(reduces, loads):
+            load(15 - step).wait()
+            reduce.corner(3 - step)
+        return carry
+
+    def side(step, carry):
+        for reduce, load in zip(reduces, loads):
+            load(7 - step).wait()
+            load(11 - step).wait()
+            reduce.side_x(3 - step)
+            reduce.side_y(3 - step)
+        return carry
+
+    def line(step, carry):
+        for reduce, load in zip(reduces, loads):
+            load(3 - step).wait()
+            reduce.line(3 - step)
+        return carry
+
+    lax.fori_loop(0, 4, corner, 0)
+    lax.fori_loop(0, 4, side, 0)
+    lax.fori_loop(0, 3, line, 0)
+    for number in reversed(range(count)):
+        reduce, load = reduces[number], loads[number]
+        load(0).wait()
+        mine = first_out if number == 0 else gathers[number - 1][0].block(0, 0)
+
+        def put(at, total, mine=mine):
+            mine[at, :] = total.astype(mine.dtype)
+
+        reduce.last(put)
+        if number == 0:
+            continue
+        gather = gathers[number - 1][0]
+        gather.copy("z", 1).start()
+        gather.line(0, True)
+        gather.copy("z", 2).start()
+        gather.copy("z", 3).start()
+
+    def pair_copy(number, q, j):
+        gather, out, sem = gathers[number]
+        rows = 2 * gather.rows
+        at = pl.ds(pl.multiple_of(place.chip(q, j) * rows, rows), rows)
+        return pltpu.make_async_copy(gather.buf.at[at], out.at[at], sem.at[4 * q + j])
+
+    def store(q, j):
+        for number in range(count - 1):
+            gathers[number][0].whole(q, j)
+            pair_copy(number, q, j).start()
+
+    def spread(j, carry):
+        for gather, _, _ in gathers:
+            gather.side_x(j)
+            gather.side_y(j)
+
+        @pl.when(j < 3)
+        def _():
+            for gather, _, _ in gathers:
+                gather.line(j + 1, False)
+
+        store(0, j)
+        store(1, j)
+        store(2, j)
+        for gather, _, _ in gathers:
+            gather.corner(j)
+        store(3, j)
+        return carry
+
+    lax.fori_loop(0, 4, spread, 0)
+
+    def drain(k, carry):
+        for number in range(count - 1):
+            pair_copy(number, k // 4, k % 4).wait()
+        return carry
+
+    lax.fori_loop(0, 16, drain, 0)
+    for reduce in reduces:
+        reduce.finish()
+    for gather, _, _ in gathers:
+        gather.finish()
+
+
+def call_sums(parts):
+    total = GRID[0] * GRID[1]
+    shapes = []
+    for part in parts:
+        width = part.shape[1]
+        shapes.append((part.shape[0] // total, width, width // 256 * 128))
+    scratch = []
+    for number, (rows, width, split) in enumerate(shapes):
+        scratch += [
+            pltpu.VMEM((16, rows, width), jnp.bfloat16),
+            *reduce_scratch(rows, width, split),
+            pltpu.SemaphoreType.DMA((2, N_SEM)),
+            pltpu.SemaphoreType.DMA((16,)),
+        ]
+        if number:
+            scratch += [
+                pltpu.VMEM((total * rows, width), jnp.bfloat16),
+                pltpu.SemaphoreType.DMA((2, N_SEM)),
+                pltpu.SemaphoreType.DMA((16,)),
+            ]
+    hbm = pl.BlockSpec(memory_space=pl.ANY)
+    rows, width, _ = shapes[0]
+    return pl.pallas_call(
+        functools.partial(sums_kernel, shapes),
+        out_shape=(
+            jax.ShapeDtypeStruct((rows, width), jnp.float32),
+            *(jax.ShapeDtypeStruct(part.shape, jnp.bfloat16) for part in parts[1:]),
+        ),
+        in_specs=[hbm] * len(parts),
+        out_specs=(pl.BlockSpec(memory_space=pltpu.VMEM), *([hbm] * (len(parts) - 1))),
+        scratch_shapes=scratch,
+        compiler_params=pltpu.CompilerParams(
+            collective_id=1, has_side_effects=True, vmem_limit_bytes=62 * 2**20
+        ),
+        name="sums",
+    )(*parts)
+
+
 def body(
     tokens,
     cotangent,
@@ -335,15 +995,33 @@
     sigmoid_out = jax.nn.sigmoid(logits)
     mask = expert_mask(ffn_ids[0], expert_count)
     dense_gates = (sigmoid_out * mask).astype(jnp.bfloat16)
-    result, token_grad, gate_back, first_sum, second_sum = expert_exchange(
-        after_attention.astype(jnp.bfloat16),
-        cotangent,
-        dense_gates,
-        expert_first,
-        expert_second,
-        max(1, owner_total // 32),
-    )
-    block_output = (after_attention + result.astype(jnp.float32)).astype(jnp.bfloat16)
+    after_low = after_attention.astype(jnp.bfloat16)
+    own_kernels = (lax.axis_size("dp"), lax.axis_size("expert")) == GRID
+    if own_kernels:
+        model_width = tokens.shape[1]
+        gate_width = -(-expert_count // 128) * 128
+        me = lax.axis_index("dp") * lax.axis_size("expert") + lax.axis_index("expert")
+        owner = me * local_count + jnp.arange(local_count * expert_first.shape[2]) // expert_first.shape[2]
+        pick = (jnp.arange(gate_width)[:, None] == owner[None, :]).astype(jnp.bfloat16)
+        padded = jnp.pad(dense_gates, ((0, 0), (0, gate_width - expert_count)))
+        half = model_width // 2
+        packed = jnp.concatenate(
+            [cotangent[:, :half], after_low, padded, cotangent[:, half:]], axis=1
+        )
+        rows_sum, result, first_sum, second_sum = call_experts(
+            packed, expert_first, expert_second, pick
+        )
+        token_grad = rows_sum[:, :model_width]
+        gate_back = rows_sum[:, model_width : model_width + expert_count]
+    else:
+        result, token_grad, gate_back, first_sum, second_sum = expert_exchange(
+            after_low,
+            cotangent,
+            dense_gates,
+            expert_first,
+            expert_second,
+            max(1, owner_total // 32),
+        )
     logit_grad = (
         gate_back.astype(jnp.float32) * mask * sigmoid_out * (1.0 - sigmoid_out)
     ).astype(jnp.bfloat16)
@@ -356,25 +1034,44 @@
     after_grad = upstream + token_grad.astype(jnp.float32) + after_extra
     stream_grad, attention_parts = attention_backward(after_grad, saved_parts, stream, shared)
     gain_part, query_part, key_part, value_part, output_part, value_router_part, output_router_part = attention_parts
-    low = lambda part: part.astype(jnp.bfloat16)
-    summed = lax.psum(
-        (
-            gain_part,
-            feed_gain_part,
-            low(query_part),
-            low(key_part),
-            low(value_part),
-            low(output_part),
-            value_router_part,
-            output_router_part,
-            router_sum,
-        ),
-        BOTH,
+    parts = (
+        query_part,
+        key_part,
+        value_part,
+        value_router_part,
+        output_router_part,
+        router_sum,
+        gain_part[:, None],
+        feed_gain_part[:, None],
+    )
+    low = jnp.concatenate([part.astype(jnp.bfloat16) for part in parts], axis=1)
+    low = jnp.pad(low, ((0, 0), (0, -low.shape[1] % 256)))
+    output_low = output_part.astype(jnp.bfloat16)
+    if own_kernels:
+        result, low, output_low = call_sums([result, low, output_low])
+    else:
+        low, output_low = lax.psum((low, output_low), BOTH)
+    block_output = (after_attention + result.astype(jnp.float32)).astype(jnp.bfloat16)
+    summed, start = [], 0
+    for part in parts:
+        summed.append(low[:, start : start + part.shape[1]].astype(jnp.float32))
+        start += part.shape[1]
+    query_sum, key_sum, value_sum, value_router_sum, output_router_sum, router_sum, *gains = summed
+    summed = (
+        gains[0][:, 0],
+        gains[1][:, 0],
+        query_sum,
+        key_sum,
+        value_sum,
+        output_low.astype(jnp.float32),
+        value_router_sum,
+        output_router_sum,
+        router_sum,
     )
     return (
         block_output,
         stream_grad,
-        *(part.astype(jnp.float32) for part in summed),
+        *summed,
         first_sum,
         second_sum,
     )

time: 919 us -> 433 us (0.47)
  waiting for transfers between devices: 612 us -> 0 us
  Pallas kernels: 0 us -> 308 us
  blocking collectives: 105 us -> 0 us
  matrix products: 113 us -> 39.5 us
  between operations: 15.2 us -> 1.66 us
  local copies, waits for them, and re-layouts: 30.8 us -> 43.5 us
    pallas_call x0 -> x2, Pallas kernels: none -> 308 us  [the longest x1 170 us: call_sums(): pl.pallas_call(functools.partial(sums_kernel, shapes), out_shape=(jax.Sha...]
    psum x2 -> x0, waiting for transfers between devices: 269 us -> none  [body(): lax.psum((gain_part, feed_gain_part, low(query_part), low(key_part), low(...]
    reduce_scatter x2 -> x0, waiting for transfers between devices: 267 us -> none  [the longest x1 150 us: expert_piece(): lax.psum_scatter(row_grad, BOTH, scatter_dimension=0, tiled=True)]
    all_gather x2 -> x0, waiting for transfers between devices: 75.8 us -> none  [the longest x1 71.4 us: expert_piece(): rows = lax.all_gather(after_low, BOTH, axis=0, tiled=True)]
    dot_general x6 -> x0, matrix products: 58.5 us -> none  [the longest x1 13.8 us: expert_pass(): hidden_pre = jnp.dot(rows, first, preferred_element_type=jnp.float32)]
    all_gather x1 -> x0, blocking collectives: 50.4 us -> none  [expert_piece(): gates = lax.all_gather(dense_gates, BOTH, axis=0, tiled=True)]
    psum x1 -> x0, blocking collectives: 43.7 us -> none  [body(): lax.psum((gain_part, feed_gain_part, low(query_part), low(key_part), low(...]
    unnamed x87 -> x133, local copies, waits for them, and re-layouts: 20.7 us -> 8.78 us
  transfers between devices with their start and end apart: 6 -> 0, of which waited for: 6 -> 0; matrix products, arithmetic and copies ran while one was open for 12% -> 0% of each run, Pallas kernels for 0% -> 0%
where the time goes in v2:
time: 433 us; the launch traced here: 432 us
  Pallas kernels  308 us (71%)
  local copies, waits for them, and re-layouts  43.5 us (10%)
  matrix products  39.5 us (9%)
  other arithmetic  38.7 us (9%)
    pallas_call x1, Pallas kernels, call_sums(): pl.pallas_call(functools.partial(sums_kernel, shapes), out_shape=(jax.Sha...  170 us
    pallas_call x1, Pallas kernels, call_experts(): pl.pallas_call(functools.partial(expert_kernel, model_width, local_count)...  139 us
    convert_element_type x4, other arithmetic, body(): summed.append(low[:, start:start + part.shape[1]].astype(jnp.float32))  14.8 us
    concatenate x1, local copies, waits for them, and re-layouts, body(): low = jnp.concatenate([part.astype(jnp.bfloat16) for part in parts], axis=1)  11.7 us
    unnamed x133, local copies, waits for them, and re-layouts  8.78 us

profile of v2, /device:TPU:1, one launch (start us, length us, event | category | flops | bytes accessed | tf_op | source)
XLA Modules:
  0.0 431.8 jit_solution(8007547991375211184)
XLA Ops:
  0.7 1.2 convert_reduce_fusion.1
  1.9 1.2 fusion.35
  7.5 1.2 fusion.33
  8.7 1.0 fusion.21
  9.7 1.0 fusion.24
  13.3 2.3 copy.238.second_t_ref
  15.6 1.2 copy.236
  16.8 1.2 copy.235
  17.9 2.3 copy.237.first_ref
  20.2 4.6 %fusion.60 = f32[128,2560]{0,1:T(8,128)S(1)} fusion(bf16[128,1024]{1,0:T(8,128)(2,1)S(1)} %copy-done.2, bf16[1024,2560]{1,0:T(8,128)(2,1)} %param.23), kind=kOutput, calls=%fused_computation.138 | convolution fusion | flops 671088640 | bytes 6815744 | tf_op jit(solution)/shard_map/dot_general | solution.py:64
  24.9 1.0 copy-done.6
  26.5 3.7 fusion.59
  31.9 0.9 multiply_convert_fusion.5
  32.8 0.8 fusion.32.packed_ref
  33.7 138.9 %experts.1 = (f32[128,1152]{1,0:T(8,128)}, bf16[4096,1024]{1,0:T(8,128)(2,1)}, f32[384,1024]{1,0:T(8,128)}, f32[384,1024]{1,0:T(8,128)}) custom-call(bf16[128,2176]{1,0:T(8,128)(2,1)} %fusion.32.packed_ref, bf16[1024,384]{1,0:T(8,128)(2,1)} %copy.237.first_ref, bf16[384,1024]{1,0:T(8,128)(2,1)} %bitcast.119, bf16[384,1024]{1,0:T(8,128)(2,1)} %bitcast.118, ...), custom_call_target="tpu_custom_call" | custom-call | flops 19327352832 | bytes 16777216 | tf_op jit(solution)/shard_map/experts/pallas_call | solution.py:759
  172.5 0.9 multiply_convert_fusion.4
  173.4 1.2 convolution_convert_fusion.5
  174.7 3.0 copy.264
  177.7 0.8 copy.261
  178.6 1.3 multiply_reduce_fusion.4
  180.1 1.2 add_add_fusion.2
  181.3 0.9 convert_element_type.246
  182.2 4.3 %fusion.2 = f32[128,2560]{1,0:T(8,128)S(1)} fusion(bf16[2560,1024]{1,0:T(8,128)(2,1)} %param.24, f32[128,1024]{1,0:T(8,128)S(1)} %add_add_fusion.2), kind=kOutput, calls=%fused_computation.6 | convolution fusion | flops 671875072 | bytes 7077888 | tf_op jit(solution)/shard_map/sb,ab->sa/dot_general | solution.py:143
  186.6 1.5 copy.240
  188.1 1.7 multiply_reduce_fusion
  189.8 2.0 fusion.11
  191.8 2.0 multiply_reduce_fusion.1
  193.9 1.3 multiply_reduce_fusion.7
  196.6 0.9 copy.260
  199.8 5.2 %convolution_add_fusion.1 = f32[128,1024]{1,0:T(8,128)} fusion(bf16[128,2560]{0,1:T(8,128)(2,1)S(1)} %bitcast.99, bf16[1024,2560]{1,0:T(8,128)(2,1)} %param.23, f32[128,1024]{1,0:T(8,128)S(1)} %copy-done.12, f32[128]{0:T(128)S(1)} %negate_multiply_fusion, f32[128]{0:T(128)S(1)} %multiply_multiply_fusion, f32[128]{0:T(128)S(1)} %copy-done.49, ...), kind=kOutput, calls=%fused_computation.20 | convolution fusion | flops 672399360 | bytes 7739392 | tf_op jit(solution)/shard_map/sb,ab->sa/dot_general | solution.py:214
  205.0 0.9 convert_element_type.245
  206.3 1.4 convolution_convert_fusion.4
  207.8 3.8 convolution_convert_fusion.refs_2_
  211.6 3.9 fusion.1
  215.5 11.7 %concatenate.7 = bf16[1024,3722]{1,0:T(8,128)(2,1)} concatenate(bf16[1024,512]{1,0:T(8,128)(2,1)S(1)} %copy-done.13, bf16[1024,512]{1,0:T(8,128)(2,1)S(1)} %convolution_convert_fusion.3, bf16[1024,2560]{1,0:T(8,128)(2,1)} %fusion.1, bf16[1024,20]{1,0:T(8,128)(2,1)S(1)} %copy.259, bf16[1024,20]{1,0:T(8,128)(2,1)} %copy.260, bf16[1024,96]{1,0:T(8,128)(2,1)S(1)} %copy-done.18, ...), dimensions={1} | concatenate | bytes 15245312 | tf_op jit(solution)/shard_map/concatenate | solution.py:1047
  227.2 7.0 %pad.9.refs_1_ = bf16[1024,3840]{1,0:T(8,128)(2,1)} pad(bf16[1024,3722]{1,0:T(8,128)(2,1)} %concatenate.7, bf16[]{:T(256)} %constant.49.clone.1), padding=0_0x0_118 | pad | bytes 15486978 | tf_op jit(solution)/shard_map/jit(_pad)/pad | solution.py:1048
  234.3 169.6 %sums.1 = (f32[128,1024]{1,0:T(8,128)}, bf16[1024,3840]{1,0:T(8,128)(2,1)}, bf16[2560,1024]{1,0:T(8,128)(2,1)}) custom-call(bf16[4096,1024]{1,0:T(8,128)(2,1)} %get-tuple-element.20.refs_0_, bf16[1024,3840]{1,0:T(8,128)(2,1)} %pad.9.refs_1_, bf16[2560,1024]{1,0:T(8,128)(2,1)} %convolution_convert_fusion.refs_2_), custom_call_target="tpu_custom_call" | custom-call | tf_op jit(solution)/shard_map/sums/pallas_call | solution.py:941
  403.9 1.8 add_convert_fusion
  405.7 2.1 convert_reduce_fusion.2
  407.8 1.2 slice_convert_fusion.3
  409.0 0.9 copy.267
  409.9 1.2 slice_convert_fusion.4
  411.1 0.8 copy.266
  411.9 0.8 copy.265
  412.8 4.3 slice_convert_fusion.1
  417.1 8.1 %slice_convert_fusion = f32[1024,2560]{1,0:T(8,128)} fusion(bf16[1024,3840]{1,0:T(8,128)(2,1)} %get-tuple-element.23), kind=kLoop, calls=%fused_computation.3 | loop fusion | flops 2621440 | bytes 15728640 | tf_op jit(solution)/shard_map/convert_element_type | solution.py:1057
  425.2 5.4 %convert_element_type.239 = f32[2560,1024]{1,0:T(8,128)} convert(bf16[2560,1024]{1,0:T(8,128)(2,1)S(1)} %bitcast.103) | non-fusion elementwise | flops 2621440 | bytes 15728640 | tf_op jit(solution)/shard_map/convert_element_type | solution.py:1066
  430.6 1.1 copy.288
  (186 shorter events, 13.3 us)
Async XLA Ops:
  0.6 10.7 %copy-start = (bf16[1024,512]{1,0:T(8,128)(2,1)S(1)}, bf16[1024,512]{1,0:T(8,128)(2,1)}, u32[]{:S(2)}) copy-start(bf16[1024,512]{1,0:T(8,128)(2,1)} %param.22) | copy-start | bytes 3145732
  0.7 11.1 %copy-start.14 = (bf16[1024,512]{1,0:T(8,128)(2,1)S(1)}, bf16[1024,512]{1,0:T(8,128)(2,1)}, u32[]{:S(2)}) copy-start(bf16[1024,512]{1,0:T(8,128)(2,1)} %param.21) | copy-start | bytes 3145732
  1.9 7.8 %copy-start.48 = (f32[128]{0:T(128)}, f32[128]{0:T(128)S(1)}, u32[]{:S(2)}) copy-start(f32[128]{0:T(128)S(1)} %broadcast_multiply_fusion.1) | copy-start | bytes 1540
  3.7 6.0 %copy-start.56 = (f32[128]{0:T(128)}, f32[128]{0:T(128)S(1)}, u32[]{:S(2)}) copy-start(f32[128]{0:T(128)S(1)} %fusion.52) | copy-start | bytes 1540
  5.1 5.7 %copy-start.42 = (f32[128,4,5]{0,1,2:T(4,128)}, f32[128,4,5]{0,1,2:T(4,128)S(1)}, u32[]{:S(2)}) copy-start(f32[128,4,5]{0,1,2:T(4,128)S(1)} %convert_reduce_fusion.5) | copy-start | bytes 30724
  5.1 5.7 %copy-start.40 = (f32[128,4,5]{0,1,2:T(4,128)}, f32[128,4,5]{0,1,2:T(4,128)S(1)}, u32[]{:S(2)}) copy-start(f32[128,4,5]{0,1,2:T(4,128)S(1)} %convert_reduce_fusion.4) | copy-start | bytes 30724
  10.8 15.5 %copy-start.31 = (f32[128,4,5]{0,2,1:T(8,128)}, f32[128,4,5]{0,2,1:T(8,128)S(1)}, u32[]{:S(2)}) copy-start(f32[128,4,5]{0,2,1:T(8,128)S(1)} %copy.225) | copy-start | bytes 30724
  11.3 13.6 %copy-start.29 = (f32[128,4,5]{0,2,1:T(8,128)}, f32[128,4,5]{0,2,1:T(8,128)S(1)}, u32[]{:S(2)}) copy-start(f32[128,4,5]{0,2,1:T(8,128)S(1)} %copy.228) | copy-start | bytes 30724
  12.1 3.5 copy-start.16
  12.5 13.6 %copy-start.22 = (f32[4,128,128]{1,2,0:T(8,128)}, f32[4,128,128]{1,2,0:T(8,128)S(1)}, u32[]{:S(2)}) copy-start(f32[4,128,128]{1,2,0:T(8,128)S(1)} %fusion.6) | copy-start | bytes 786436
  13.3 12.7 %copy-start.52 = (f32[4,128]{1,0:T(4,128)}, f32[4,128]{1,0:T(4,128)S(1)}, u32[]{:S(2)}) copy-start(f32[4,128]{1,0:T(4,128)S(1)} %get-tuple-element.125) | copy-start | bytes 6148
  15.6 4.6 %copy-start.2 = (bf16[128,1024]{1,0:T(8,128)(2,1)S(1)}, bf16[128,1024]{1,0:T(8,128)(2,1)}, u32[]{:S(2)}) copy-start(bf16[128,1024]{1,0:T(8,128)(2,1)} %param.17) | copy-start | bytes 786436
  26.0 4.2 copy-start.33
  26.3 4.0 copy-start.23
  26.5 3.8 copy-start.8
  26.5 4.6 %copy-start.46 = (f32[1024]{0:T(1024)S(1)}, f32[1024]{0:T(1024)}, u32[]{:S(2)}) copy-start(f32[1024]{0:T(1024)} %param.20) | copy-start | bytes 12292
  26.5 5.5 %copy-start.28 = (bf16[1024,96]{0,1:T(8,128)(2,1)S(1)}, bf16[1024,96]{0,1:T(8,128)(2,1)}, u32[]{:S(2)}) copy-start(bf16[1024,96]{0,1:T(8,128)(2,1)} %param.27) | copy-start | bytes 589828
  33.6 138.9 %copy-start.45 = (f32[128,96]{1,0:T(8,128)S(1)}, f32[128,96]{1,0:T(8,128)}, u32[]{:S(2)}) copy-start(f32[128,96]{1,0:T(8,128)} %get-tuple-element.130) | copy-start | bytes 147460
  173.4 5.2 %copy-start.4 = (f32[128,1024]{1,0:T(8,128)S(1)}, f32[128,1024]{1,0:T(8,128)}, u32[]{:S(2)}) copy-start(f32[128,1024]{1,0:T(8,128)} %copy-done.3) | copy-start | bytes 1572868
  173.4 5.2 %copy-start.47 = (f32[1024]{0:T(1024)S(1)}, f32[1024]{0:T(1024)}, u32[]{:S(2)}) copy-start(f32[1024]{0:T(1024)} %param.20) | copy-start | bytes 12292
  173.4 5.2 %copy-start.51 = (f32[128]{0:T(128)S(1)}, f32[128]{0:T(128)}, u32[]{:S(2)}) copy-start(f32[128]{0:T(128)} %copy-done.50) | copy-start | bytes 1540
  173.4 5.2 %copy-start.55 = (f32[128]{0:T(128)S(1)}, f32[128]{0:T(128)}, u32[]{:S(2)}) copy-start(f32[128]{0:T(128)} %copy-done.54) | copy-start | bytes 1540
  174.7 5.2 %copy-start.61 = (f32[128]{0:T(128)S(1)}, f32[128]{0:T(128)}, u32[]{:S(2)}) copy-start(f32[128]{0:T(128)} %copy-done.60) | copy-start | bytes 1540
  177.7 2.4 copy-start.25
  186.6 3.2 copy-start.43
  186.6 3.2 copy-start.53
  188.1 3.8 copy-start.7
  188.1 3.8 copy-start.30
  189.7 4.1 copy-start.35
  189.7 4.1 copy-start.41
  189.8 4.1 copy-start.34
  191.8 3.4 copy-start.21
  193.9 2.2 copy-start.39
  193.9 2.2 copy-start.37
  193.9 3.6 copy-start.26
  195.2 2.6 copy-start.27
  195.3 2.8 copy-start.15
  196.1 2.5 copy-start.44
  196.1 2.5 copy-start.49
  205.0 2.8 copy-start.9
  211.6 3.9 copy-start.13
  211.6 3.9 copy-start.18
  211.6 3.9 copy-start.19
  234.3 169.6 %copy-start.5 = (f32[128,1024]{1,0:T(8,128)S(1)}, f32[128,1024]{1,0:T(8,128)}, u32[]{:S(2)}) copy-start(f32[128,1024]{1,0:T(8,128)} %copy-done.3) | copy-start | bytes 1572868
  412.8 12.4 %slice-start = ((s8[5242880]{0:T(1024)(128)(4,1)}), s8[4194304]{0:T(1024)(128)(4,1)S(1)}, s32[]{:S(2)}) async-start(s8[5242880]{0:T(1024)(128)(4,1)} %bitcast.102), calls=%async_computation | async-start | bytes 8388608
  417.1 8.1 %slice-start.1 = ((s8[5242880]{0:T(1024)(128)(4,1)}), s8[1048576]{0:T(1024)(128)(4,1)S(1)}, s32[]{:S(2)}) async-start(s8[5242880]{0:T(1024)(128)(4,1)} %bitcast.102), calls=%async_computation.1 | async-start | bytes 2097152
  425.2 5.5 %copy-start.17 = (f32[384,1024]{1,0:T(8,128)S(1)}, f32[384,1024]{1,0:T(8,128)}, u32[]{:S(2)}) copy-start(f32[384,1024]{1,0:T(8,128)} %get-tuple-element.26) | copy-start | bytes 4718596
  425.2 6.6 %copy-start.1 = (bf16[1024,512]{1,0:T(8,128)(2,1)S(1)}, bf16[1024,512]{1,0:T(8,128)(2,1)}, u32[]{:S(2)}) copy-start(bf16[1024,512]{1,0:T(8,128)(2,1)} %param.22) | copy-start | bytes 3145732
  (16 other events, 15.0 us)

commit v3 on v2

--- a/solution.py
+++ b/solution.py
@@ -91,10 +91,8 @@
         normed_low,
         queries,
         key_rows,
-        value_sig,
-        output_sig,
-        value_mask,
-        output_mask,
+        value_gates * (1.0 - value_sig),
+        output_gates * (1.0 - output_sig),
         value_gates,
         output_gates,
         stream_low,
@@ -122,10 +120,8 @@
         normed_low,
         queries,
         key_rows,
-        value_sig,
-        output_sig,
-        value_mask,
-        output_mask,
+        value_slope,
+        output_slope,
         value_gates,
         output_gates,
         stream_low,
@@ -177,12 +173,12 @@
     )
     value_gate_grad = jnp.sum(values_grad[:, :, None, :] * projected, axis=3)
     value_logit_grad = (
-        (value_gate_grad * value_mask * value_sig * (1.0 - value_sig))
+        (value_gate_grad * value_slope)
         .astype(jnp.bfloat16)
         .reshape(length, HEADS * ATT_EXP)
     )
     output_logit_grad = (
-        (output_gate_grad * output_mask * output_sig * (1.0 - output_sig))
+        (output_gate_grad * output_slope)
         .astype(jnp.bfloat16)
         .reshape(length, HEADS * ATT_EXP)
     )
@@ -299,6 +295,7 @@
 
 MESH = pl.DeviceIdType.MESH
 GRID = (4, 8)
+N_SEM = 47
 
 
 class Place:
@@ -306,31 +303,40 @@
         dp, expert = lax.axis_index("dp"), lax.axis_index("expert")
         self.y, self.x = dp // 2, dp % 2
         self.z, self.core = expert // 2, expert % 2
-        self.dp, self.expert = dp, expert
+        self.dp = dp
         self.me = dp * GRID[1] + expert
         self.x_peer = (2 * self.y + 1 - self.x, expert)
         self.y_peer = (2 * (1 - self.y) + self.x, expert)
         self.core_peer = (dp, 2 * self.z + 1 - self.core)
+        self.middle = (self.z + self.z // 2) % 2
+        self.main = 1 + self.z % 2
+        self.minor = 3 * (self.z // 2)
+
+    def along_z(self, z):
+        return (self.dp, 2 * z + self.core)
 
     def z_at(self, j):
-        return 2 * ((self.z // 2 + j // 2) % 2) + (self.z % 2 + j % 2) % 2
-
-    def z_peer(self, j):
-        return (self.dp, 2 * self.z_at(j) + self.core)
-
-    def peers(self):
-        return [self.x_peer, self.y_peer, self.core_peer] + [self.z_peer(j) for j in (1, 2, 3)]
+        near = j + self.middle * (1 - 2 * j) * (1 - j // 2)
+        return near + self.z // 2 * (3 - 2 * near)
 
     def chip(self, q, j):
         return ((self.y + q // 2) % 2 * 2 + (self.x + q % 2) % 2) * 4 + self.z_at(j)
 
+    def if_middle(self, action):
+        pl.when(self.middle == 1)(action)
+
 
 def enter(place):
     barrier = pltpu.get_barrier_semaphore()
-    peers = place.peers()
-    for peer in peers:
+
+    def signal(peer):
         pl.semaphore_signal(barrier, inc=1, device_id=peer, device_id_type=MESH)
-    pl.semaphore_wait(barrier, len(peers))
+
+    for peer in (place.x_peer, place.y_peer, place.core_peer, place.along_z(place.main)):
+        signal(peer)
+    place.if_middle(lambda: signal(place.along_z(place.minor)))
+    pl.when(place.middle == 0)(lambda: pl.semaphore_wait(barrier, 4))
+    place.if_middle(lambda: pl.semaphore_wait(barrier, 5))
 
 
 def remote(src, dst, send, recv, peer):
@@ -344,52 +350,103 @@
     )
 
 
-N_SEM = 35
+def cut_columns(width):
+    tiles = width // 128
+    split = tiles // 2
+    outer = max(1, tiles * 3 // 10)
+    return outer * 128, split * 128, (tiles - outer) * 128
 
 
 class Gather:
-    def __init__(self, place, buf, rows, split, sems):
-        self.place, self.buf, self.rows, self.split = place, buf, rows, split
+    def __init__(self, place, buf, rows, sems):
+        self.place, self.buf, self.rows = place, buf, rows
+        self.width = buf.shape[1]
+        self.d_end, self.split, self.c_start = cut_columns(self.width)
         self.send, self.recv = sems.at[0], sems.at[1]
 
-    def block(self, q, j, part=None):
+    def block(self, q, j, columns=slice(None)):
         start = (2 * self.place.chip(q, j) + self.place.core) * self.rows
-        rows = pl.ds(pl.multiple_of(start, self.rows), self.rows)
-        if part == "b":
-            return self.buf.at[rows, : self.split]
-        if part == "a":
-            return self.buf.at[rows, self.split :]
-        return self.buf.at[rows]
+        return self.buf.at[pl.ds(pl.multiple_of(start, self.rows), self.rows), columns]
 
     def copy(self, kind, j, q=0):
         place = self.place
-        if kind == "z":
-            ref, number, peer = self.block(0, 0), j - 1, place.z_peer(j)
+        if kind == "x0":
+            ref, number, peer = self.block(0, 0), 15, place.x_peer
+        elif kind == "y0":
+            ref, number, peer = self.block(0, 0), 19, place.y_peer
         elif kind == "x":
-            ref, number, peer = self.block(0, j), 3 + j, place.x_peer
+            ref, number, peer = self.block(0, j, slice(0, self.c_start)), 15 + j, place.x_peer
         elif kind == "y":
-            ref, number, peer = self.block(0, j), 7 + j, place.y_peer
+            ref, number, peer = self.block(0, j, slice(self.d_end, None)), 19 + j, place.y_peer
         elif kind == "a":
-            ref, number, peer = self.block(1, j, "a"), 11 + j, place.y_peer
+            ref, number, peer = self.block(1, j, slice(self.split, None)), 23 + j, place.y_peer
         elif kind == "b":
-            ref, number, peer = self.block(2, j, "b"), 15 + j, place.x_peer
+            ref, number, peer = self.block(2, j, slice(0, self.split)), 27 + j, place.x_peer
         else:
-            ref, number, peer = self.block(q, j), 19 + 4 * q + j, place.core_peer
+            ref, number, peer = self.block(q, j), 31 + 4 * q + j, place.core_peer
         return remote(ref, ref, self.send.at[number], self.recv.at[number], peer)
 
-    def line(self, j, first):
-        if not first:
-            self.copy("z", j).wait_recv()
+    def z_copy(self, part, j, number, z, receiver_j):
+        columns = (slice(None), slice(self.c_start, None), slice(0, self.d_end))[part]
+        ref = self.block(part, j, columns)
+        return remote(
+            ref,
+            ref,
+            self.send.at[5 * part + number],
+            self.recv.at[3 * part + receiver_j - 1],
+            self.place.along_z(z),
+        )
+
+    def z_own(self, part):
+        place = self.place
+        self.z_copy(part, 0, 0, place.main, 1 + place.middle).start()
+        place.if_middle(lambda: self.z_copy(part, 0, 1, place.minor, 1).start())
+
+    def outer_own(self, middle):
+        @pl.when(self.place.middle == middle)
+        def _():
+            self.z_own(1)
+            self.z_own(2)
+
+    def z_pass(self, part, j):
+        place = self.place
+        first = 1 - (j + 2) // 4
+        z = place.minor + first * (place.main - place.minor)
+        return self.z_copy(part, j, 1 + j, z, j + 2 * first)
+
+    def z_arrive(self, part, j):
+        self.z_copy(part, j, 0, self.place.main, j).wait_recv()
+        self.place.if_middle(lambda: self.z_pass(part, j).start())
+
+    def begin(self):
+        self.z_own(0)
+        self.copy("x0", 0).start()
+        self.copy("y0", 0).start()
+        self.copy("core", 0, 0).start()
+
+    def line(self, j):
+        self.z_arrive(0, j)
         self.copy("x", j).start()
         self.copy("y", j).start()
         self.copy("core", j, 0).start()
-
-    def side_x(self, j):
+        if j == 3:
+            self.outer_own(1)
+
+    def sides_first(self):
+        self.copy("x0", 0).wait_recv()
+        self.copy("a", 0).start()
+        self.copy("core", 0, 1).start()
+        self.copy("y0", 0).wait_recv()
+        self.copy("b", 0).start()
+        self.copy("core", 0, 2).start()
+        self.outer_own(0)
+
+    def sides(self, j):
+        self.z_arrive(1, j)
+        self.z_arrive(2, j)
         self.copy("x", j).wait_recv()
         self.copy("a", j).start()
         self.copy("core", j, 1).start()
-
-    def side_y(self, j):
         self.copy("y", j).wait_recv()
         self.copy("b", j).start()
         self.copy("core", j, 2).start()
@@ -403,12 +460,34 @@
         self.copy("core", j, q).wait_recv()
 
     def finish(self):
-        for j in (1, 2, 3):
-            self.copy("z", j).wait_send()
+        place = self.place
+        for part in range(3):
+            self.z_copy(part, 0, 0, place.main, 1).wait_send()
+
+        def middle():
+            for part in range(3):
+                self.z_copy(part, 0, 1, place.minor, 1).wait_send()
+
+                def passed(j, carry):
+                    self.z_pass(part, j).wait_send()
+                    return carry
+
+                lax.fori_loop(1, 4, passed, 0)
+
+        place.if_middle(middle)
+        self.copy("x0", 0).wait_send()
+        self.copy("y0", 0).wait_send()
+
+        def line(j, carry):
+            self.copy("x", j).wait_send()
+            self.copy("y", j).wait_send()
+            return carry
+
+        lax.fori_loop(1, 4, line, 0)
 
         def step(j, carry):
-            for kind in ("x", "y", "a", "b"):
-                self.copy(kind, j).wait_send()
+            self.copy("a", j).wait_send()
+            self.copy("b", j).wait_send()
             for q in range(4):
                 self.copy("core", j, q).wait_send()
             return carry
@@ -417,32 +496,88 @@
 
 
 class Reduce:
-    def __init__(self, place, own, other, other_in, a_in, b_in, x_in, y_in, z_in, split, sems):
-        self.place, self.own, self.other, self.other_in = place, own, other, other_in
-        self.a_in, self.b_in, self.x_in, self.y_in, self.z_in = a_in, b_in, x_in, y_in, z_in
-        self.split = split
+    def __init__(self, place, own, other, boxes, sems):
+        self.place, self.own, self.other = place, own, other
+        self.other_in, self.a_in, self.b_in, self.x_in, self.y_in = boxes[:5]
+        self.z_in = boxes[5:]
+        self.rows, self.width = self.other_in.shape[1:]
+        self.d_end, self.split, self.c_start = cut_columns(self.width)
         self.send, self.recv = sems.at[0], sems.at[1]
 
     def copy(self, kind, k):
-        place, split = self.place, self.split
+        place = self.place
         j = k % 4
         if kind == "core":
             src, dst, number, peer = self.other(k), self.other_in.at[k], k, place.core_peer
         elif kind == "a":
-            src, dst, number, peer = self.own(k).at[:, split:], self.a_in.at[j], 16 + j, place.y_peer
+            src = self.own(k).at[:, self.split :]
+            dst, number, peer = self.a_in.at[j], 16 + j, place.y_peer
         elif kind == "b":
-            src, dst, number, peer = self.own(k).at[:, :split], self.b_in.at[j], 20 + j, place.x_peer
+            src = self.own(k).at[:, : self.split]
+            dst, number, peer = self.b_in.at[j], 20 + j, place.x_peer
+        elif kind == "x0":
+            src, dst, number, peer = self.own(k), self.x_in.at[0], 24, place.x_peer
+        elif kind == "y0":
+            src, dst, number, peer = self.own(k), self.y_in.at[0], 28, place.y_peer
         elif kind == "x":
-            src, dst, number, peer = self.own(k), self.x_in.at[j], 24 + j, place.x_peer
-        elif kind == "y":
-            src, dst, number, peer = self.own(k), self.y_in.at[j], 28 + j, place.y_peer
+            src = self.own(k).at[:, : self.c_start]
+            dst, number, peer = self.x_in.at[j, :, : self.c_start], 24 + j, place.x_peer
         else:
-            src, dst, number, peer = self.own(k), self.z_in.at[j - 1], 31 + j, place.z_peer(j)
+            src = self.own(k).at[:, self.d_end :]
+            dst, number, peer = self.y_in.at[j, :, self.d_end :], 28 + j, place.y_peer
         return remote(src, dst, self.send.at[number], self.recv.at[number], peer)
+
+    def z_columns(self, part):
+        return (slice(None), slice(self.c_start, None), slice(0, self.d_end))[part]
+
+    def z_copy(self, part, j):
+        place = self.place
+        first = 1 - (j + 2) // 4
+        box = place.middle * (j // 3) + (1 - place.middle) * (j + 1)
+        z = place.main + place.middle * first * (place.minor - place.main)
+        return remote(
+            self.own(4 * part + j).at[:, self.z_columns(part)],
+            self.z_in[part].at[box],
+            self.send.at[32 + 5 * part + j],
+            self.recv.at[32 + 5 * part + box],
+            place.along_z(z),
+        )
+
+    def z_wait(self, part, box):
+        self.copy_box(part, box).wait_recv()
+
+    def copy_box(self, part, box):
+        ref = self.z_in[part].at[box]
+        return remote(
+            ref,
+            ref,
+            self.send.at[32 + 5 * part],
+            self.recv.at[32 + 5 * part + box],
+            self.place.along_z(self.place.main),
+        )
+
+    def z_give(self, part, j):
+        def middle():
+            box = j + (j + 2) // 4
+            self.z_wait(part, box)
+            self.add(4 * part + j, self.z_columns(part), [lambda at: self.z_in[part][box, at, :]])
+
+        self.place.if_middle(middle)
+        self.z_copy(part, j).start()
+
+    def z_last(self, part):
+        columns = self.z_columns(part)
+        self.z_wait(part, 0)
+        self.add(4 * part, columns, [lambda at: self.z_in[part][0, at, :]])
+
+        def middle():
+            self.z_wait(part, 2)
+            self.add(4 * part, columns, [lambda at: self.z_in[part][2, at, :]])
+
+        self.place.if_middle(middle)
 
     def add(self, k, columns, terms):
         own = self.own(k)
-        rows = own.shape[0]
 
         def step(number, carry):
             at = pl.ds(pl.multiple_of(number * 16, 16), 16)
@@ -452,7 +587,7 @@
             own[at, columns] = total.astype(own.dtype)
             return carry
 
-        lax.fori_loop(0, rows // 16, step, 0)
+        lax.fori_loop(0, self.rows // 16, step, 0)
 
     def corner(self, j):
         k = 12 + j
@@ -471,7 +606,6 @@
             slice(split, None),
             [lambda at: self.other_in[k, at, split:], lambda at: self.a_in[j, at, :]],
         )
-        self.copy("x", k).start()
 
     def side_y(self, j):
         k, split = 8 + j, self.split
@@ -483,58 +617,126 @@
             slice(0, split),
             [lambda at: self.other_in[k, at, :split], lambda at: self.b_in[j, at, :]],
         )
-        self.copy("y", k).start()
+
+    def sides(self, j):
+        self.side_x(j)
+        self.copy("x", 4 + j).start()
+        self.z_give(1, j)
+        self.side_y(j)
+        self.copy("y", 8 + j).start()
+        self.z_give(2, j)
+
+    def sides_last(self):
+        self.side_x(0)
+        self.side_y(0)
+        self.z_last(1)
+        self.copy("x0", 4).start()
+        self.z_last(2)
+        self.copy("y0", 8).start()
 
     def line(self, j):
         self.copy("core", j).wait_recv()
         self.copy("x", j).wait_recv()
         self.copy("y", j).wait_recv()
+        d_end, c_start = self.d_end, self.c_start
         boxes = (self.other_in, self.x_in, self.y_in)
-        self.add(j, slice(None), [lambda at, box=box: box[j, at, :] for box in boxes])
-        self.copy("z", j).start()
+        for columns, used in (
+            (slice(0, d_end), boxes[:2]),
+            (slice(d_end, c_start), boxes),
+            (slice(c_start, None), (boxes[0], boxes[2])),
+        ):
+            self.add(j, columns, [lambda at, box=box: box[j, at, columns] for box in used])
+        self.z_give(0, j)
 
     def last(self, put):
         self.copy("core", 0).wait_recv()
-        self.copy("x", 0).wait_recv()
-        self.copy("y", 0).wait_recv()
-        for j in (1, 2, 3):
-            self.copy("z", j).wait_recv()
+        self.copy("x0", 0).wait_recv()
+        self.copy("y0", 0).wait_recv()
+        self.z_wait(0, 0)
         own = self.own(0)
 
-        def step(number, carry):
-            at = pl.ds(pl.multiple_of(number * 16, 16), 16)
-            total = own[at, :].astype(jnp.float32)
-            for box in (self.other_in, self.x_in, self.y_in):
-                total = total + box[0, at, :].astype(jnp.float32)
-            for j in range(3):
-                total = total + self.z_in[j, at, :].astype(jnp.float32)
-            put(at, total)
-            return carry
-
-        lax.fori_loop(0, own.shape[0] // 16, step, 0)
+        def sum_up(middle):
+            def step(number, carry):
+                at = pl.ds(pl.multiple_of(number * 16, 16), 16)
+                total = own[at, :].astype(jnp.float32)
+                for box in (self.other_in, self.x_in, self.y_in, self.z_in[0]):
+                    total = total + box[0, at, :].astype(jnp.float32)
+                if middle:
+                    total = total + self.z_in[0][2, at, :].astype(jnp.float32)
+                put(at, total)
+                return carry
+
+            lax.fori_loop(0, own.shape[0] // 16, step, 0)
+
+        @pl.when(self.place.middle == 1)
+        def _():
+            self.z_wait(0, 2)
+            sum_up(True)
+
+        pl.when(self.place.middle == 0)(lambda: sum_up(False))
 
     def finish(self):
         def step(j, carry):
-            for kind, q in (("a", 3), ("b", 3), ("x", 1), ("y", 2)):
-                self.copy(kind, 4 * q + j).wait_send()
+            self.copy("a", 12 + j).wait_send()
+            self.copy("b", 12 + j).wait_send()
             for q in range(4):
                 self.copy("core", 4 * q + j).wait_send()
             return carry
 
         lax.fori_loop(0, 4, step, 0)
-        for j in (1, 2, 3):
-            self.copy("z", j).wait_send()
-
-
-def reduce_scratch(rows, width, split):
+
+        def outer(j, carry):
+            self.copy("x", 4 + j).wait_send()
+            self.copy("y", 8 + j).wait_send()
+            for part in range(3):
+                self.z_copy(part, j).wait_send()
+            return carry
+
+        lax.fori_loop(1, 4, outer, 0)
+        self.copy("x0", 4).wait_send()
+        self.copy("y0", 8).wait_send()
+
+
+RETURN_ORDER = (
+    ("corner", (3,)),
+    ("corner", (2,)),
+    ("corner", (1,)),
+    ("sides", (3,)),
+    ("corner", (0,)),
+    ("sides", (2,)),
+    ("sides", (1,)),
+    ("line", (3,)),
+    ("sides_last", ()),
+    ("line", (2,)),
+    ("line", (1,)),
+)
+SPREAD_ORDER = (
+    ("line", (1,), [(0, 0)]),
+    ("sides_first", (), [(0, 1)]),
+    ("line", (2,), [(1, 0), (2, 0)]),
+    ("line", (3,), [(0, 2)]),
+    ("corner", (0,), [(0, 3)]),
+    ("sides", (1,), [(3, 0)]),
+    ("sides", (2,), [(1, 1), (2, 1)]),
+    ("sides", (3,), [(1, 2), (2, 2)]),
+    ("corner", (1,), [(1, 3), (2, 3)]),
+    ("corner", (2,), [(3, 1)]),
+    ("corner", (3,), [(3, 2), (3, 3)]),
+)
+
+
+def reduce_scratch(rows, width):
     low = jnp.bfloat16
+    d_end, split, c_start = cut_columns(width)
     return [
         pltpu.VMEM((16, rows, width), low),
         pltpu.VMEM((4, rows, width - split), low),
         pltpu.VMEM((4, rows, split), low),
         pltpu.VMEM((4, rows, width), low),
         pltpu.VMEM((4, rows, width), low),
-        pltpu.VMEM((3, rows, width), low),
+        pltpu.VMEM((5, rows, width), low),
+        pltpu.VMEM((5, rows, width - c_start), low),
+        pltpu.VMEM((5, rows, d_end), low),
     ]
 
 
@@ -548,46 +750,261 @@
 
 def mm_tn(left, right):
     return lax.dot_general(left, right, (((0,), (0,)), ((), ())), preferred_element_type=jnp.float32)
+
+
+def norm_parts(stream):
+    average = jnp.mean(stream, axis=-1, keepdims=True)
+    centred = stream - average
+    variance = jnp.mean(centred * centred, axis=-1, keepdims=True)
+    return centred, lax.rsqrt(variance + 1e-05)
+
+
+def mm_nt(left, right):
+    return lax.dot_general(left, right, (((1,), (1,)), ((), ())), preferred_element_type=jnp.float32)
+
+
+def picked_mask(ids, groups, per_group, group_size, width):
+    column = lax.broadcasted_iota(jnp.int32, (ids.shape[0], width), 1)
+    mask = jnp.zeros((ids.shape[0], width), jnp.float32)
+    for group in range(groups):
+        for number in range(per_group):
+            at = group * per_group + number
+            mask = jnp.where(column == ids[:, at : at + 1] + group * group_size, 1.0, mask)
+    return mask
+
+
+def attention_kernel(
+    tokens_ref,
+    cotangent_ref,
+    gain_attention_ref,
+    gain_feedforward_ref,
+    query_ref,
+    key_ref,
+    value_ref,
+    output_ref,
+    value_router_ref,
+    output_router_ref,
+    expert_router_ref,
+    segments_ref,
+    value_ids_ref,
+    output_ids_ref,
+    ffn_ids_ref,
+    upstream_out,
+    packed_out,
+    after_out,
+    normed_out,
+    normed_ffn_out,
+    queries_out,
+    keys_out,
+    projected_out,
+    values_out,
+    probability_out,
+    mixed_out,
+    gated_out,
+    value_gates_out,
+    value_slope_out,
+    output_gates_out,
+    output_slope_out,
+    expert_slope_out,
+    own_sem,
+    gather_sems,
+):
+    place = Place()
+    length, model_width = tokens_ref.shape
+    expert_count = expert_router_ref.shape[1]
+    router_width = value_router_ref.shape[1]
+    enter(place)
+    gather = Gather(place, upstream_out, length, gather_sems)
+    own_copy = pltpu.make_async_copy(cotangent_ref, gather.block(0, 0), own_sem)
+    own_copy.start()
+    own_copy.wait()
+    gather.begin()
+
+    stream_low = tokens_ref[...]
+    stream = stream_low.astype(jnp.float32)
+    centred, scale = norm_parts(stream)
+    normed = (centred * scale * gain_attention_ref[...]).astype(jnp.bfloat16)
+    normed_out[...] = normed
+    queries_out[...] = mm(normed, query_ref[...]).astype(jnp.bfloat16)
+    keys_out[...] = mm(normed, key_ref[...]).astype(jnp.bfloat16)
+    value_sig = jax.nn.sigmoid(mm(normed, value_router_ref[...]))
+    output_sig = jax.nn.sigmoid(mm(normed, output_router_ref[...]))
+    picks = value_ids_ref.shape[1] // HEADS
+    value_mask = picked_mask(value_ids_ref[...], HEADS, picks, ATT_EXP, router_width)
+    output_mask = picked_mask(output_ids_ref[...], HEADS, picks, ATT_EXP, router_width)
+    value_gates = value_mask * value_sig
+    output_gates = output_mask * output_sig
+    value_gates_out[...] = value_gates
+    output_gates_out[...] = output_gates
+    value_slope_out[...] = value_gates * (1.0 - value_sig)
+    output_slope_out[...] = output_gates * (1.0 - output_sig)
+    gather.line(1)
+    gather.sides_first()
+    gather.line(2)
+    head_width = ATT_EXP * HEAD
+    for head in range(HEADS):
+        columns = slice(head * head_width, (head + 1) * head_width)
+        projected_out[:, columns] = mm(stream_low, value_ref[:, columns])
+        total = jnp.zeros((length, HEAD), jnp.float32)
+        for e in range(ATT_EXP):
+            at = head * ATT_EXP + e
+            total = total + value_gates[:, at : at + 1] * projected_out[:, at * HEAD : (at + 1) * HEAD]
+        values_out[:, head * HEAD : (head + 1) * HEAD] = total.astype(jnp.bfloat16)
+    gather.line(3)
+    documents = jnp.broadcast_to(segments_ref[...].astype(jnp.float32), (length, length))
+    row = lax.broadcasted_iota(jnp.int32, (length, length), 0)
+    column = lax.broadcasted_iota(jnp.int32, (length, length), 1)
+    allowed = (documents == documents.T) & (row >= column)
+    for head in range(HEADS):
+        columns = slice(head * HEAD, (head + 1) * HEAD)
+        scores = mm_nt(queries_out[:, columns], keys_out[:, columns]) * (1.0 / math.sqrt(HEAD))
+        scores = jnp.where(allowed, scores, NEG_FILL)
+        exponent = jnp.exp(scores - jnp.max(scores, axis=-1, keepdims=True))
+        probability = exponent / jnp.sum(exponent, axis=-1, keepdims=True)
+        probability_out[head] = probability
+        mixed = mm(probability.astype(jnp.bfloat16), values_out[:, columns])
+        mixed_out[:, columns] = mixed
+        for e in range(ATT_EXP):
+            at = head * ATT_EXP + e
+            gated_out[:, at * HEAD : (at + 1) * HEAD] = (
+                output_gates[:, at : at + 1] * mixed
+            ).astype(jnp.bfloat16)
+    after = stream + mm(gated_out[...], output_ref[...])
+    after_out[...] = after
+    packed_out[:, :model_width] = after.astype(jnp.bfloat16)
+    centred, scale = norm_parts(after)
+    normed_ffn = (centred * scale * gain_feedforward_ref[...]).astype(jnp.bfloat16)
+    normed_ffn_out[...] = normed_ffn
+    expert_sig = jax.nn.sigmoid(mm(normed_ffn, expert_router_ref[...]))
+    expert_mask_ = picked_mask(ffn_ids_ref[...], 1, ffn_ids_ref.shape[1], 0, expert_count)
+    expert_gates = expert_mask_ * expert_sig
+    gate_width = packed_out.shape[1] - model_width
+    packed_out[:, model_width:] = jnp.zeros((length, gate_width), jnp.bfloat16)
+    packed_out[:, model_width : model_width + expert_count] = expert_gates.astype(jnp.bfloat16)
+    expert_slope_out[...] = expert_gates * (1.0 - expert_sig)
+    gather.corner(0)
+    for j in (1, 2, 3):
+        gather.sides(j)
+    for j in (1, 2, 3):
+        gather.corner(j)
+
+    def arrived(k, carry):
+        gather.whole(k // 4, k % 4)
+        return carry
+
+    lax.fori_loop(0, 16, arrived, 0)
+    gather.finish()
+
+
+def call_attention(
+    tokens,
+    cotangent,
+    gain_attention,
+    gain_feedforward,
+    shared_weights,
+    expert_router,
+    segments,
+    value_ids,
+    output_ids,
+    ffn_ids,
+    gate_width,
+):
+    length, model_width = tokens.shape
+    total = GRID[0] * GRID[1] * length
+    expert_count = expert_router.shape[1]
+    wide = shared_weights[3].shape[0]
+    narrow = HEADS * HEAD
+    router_width = HEADS * ATT_EXP
+    low, full = jnp.bfloat16, jnp.float32
+    shapes = (
+        ((total, model_width), low),
+        ((length, model_width + gate_width), low),
+        ((length, model_width), full),
+        ((length, model_width), low),
+        ((length, model_width), low),
+        ((length, narrow), low),
+        ((length, narrow), low),
+        ((length, wide), full),
+        ((length, narrow), low),
+        ((HEADS, length, length), full),
+        ((length, narrow), full),
+        ((length, wide), low),
+        ((length, router_width), full),
+        ((length, router_width), full),
+        ((length, router_width), full),
+        ((length, router_width), full),
+        ((length, expert_count), full),
+    )
+    vmem = pl.BlockSpec(memory_space=pltpu.VMEM)
+    hbm = pl.BlockSpec(memory_space=pl.ANY)
+    return pl.pallas_call(
+        attention_kernel,
+        out_shape=tuple(jax.ShapeDtypeStruct(*shape) for shape in shapes),
+        in_specs=[vmem] * 15,
+        out_specs=(hbm, *([vmem] * (len(shapes) - 1))),
+        scratch_shapes=[pltpu.SemaphoreType.DMA, pltpu.SemaphoreType.DMA((2, N_SEM))],
+        compiler_params=pltpu.CompilerParams(
+            collective_id=2, has_side_effects=True, vmem_limit_bytes=62 * 2**20
+        ),
+        name="attention",
+    )(
+        tokens,
+        cotangent,
+        gain_attention[None],
+        gain_feedforward[None],
+        *shared_weights,
+        expert_router,
+        segments,
+        value_ids.reshape(length, -1),
+        output_ids.reshape(length, -1),
+        ffn_ids,
+    )
 
 
 def expert_kernel(
     model_width,
     local_count,
     packed_ref,
-    first_ref,
-    first_t_ref,
-    second_ref,
-    second_t_ref,
-    pick_ref,
+    upstream_ref,
+    first_in,
+    second_in,
     rows_out,
     result_out,
     first_out,
     second_out,
     gathered,
+    upstream,
+    first_ref,
+    first_t_ref,
+    second_t_ref,
     gated_hidden,
     pre_grads,
     partial,
-    other_in,
-    a_in,
-    b_in,
-    x_in,
-    y_in,
-    z_in,
-    result_stage,
-    gather_sems,
-    reduce_sems,
-    result_sems,
+    *refs,
 ):
     place = Place()
     length = packed_ref.shape[0]
     pair = 2 * length
-    half = model_width // 2
-    gate_width = pick_ref.shape[0]
+    gate_width = packed_ref.shape[1] - model_width
     hidden_width = first_ref.shape[1] // local_count
-    split = model_width
+    boxes, (result_stage, gather_sems, reduce_sems, result_sems, upstream_sem) = refs[:8], refs[8:]
+    upstream_copy = pltpu.make_async_copy(upstream_ref, upstream, upstream_sem)
+    upstream_copy.start()
     enter(place)
-    gather = Gather(place, gathered, length, split, gather_sems)
+    gather = Gather(place, gathered, length, gather_sems)
     gathered[pl.ds(pl.multiple_of(place.me * length, length), length), :] = packed_ref[...]
+    gather.begin()
+    second_ref = second_in
+    for e in range(local_count):
+        columns = slice(e * hidden_width, (e + 1) * hidden_width)
+        first_ref[:, columns] = first_in[e]
+        first_t_ref[columns, :] = first_in[e].astype(jnp.float32).T.astype(jnp.bfloat16)
+        second_t_ref[:, columns] = second_in[columns, :].astype(jnp.float32).T.astype(jnp.bfloat16)
+    pick_row = lax.broadcasted_iota(jnp.int32, (gate_width, first_ref.shape[1]), 0)
+    pick_column = lax.broadcasted_iota(jnp.int32, (gate_width, first_ref.shape[1]), 1)
+    pick_gates = jnp.where(
+        pick_row == place.me * local_count + pick_column // hidden_width, 1.0, 0.0
+    ).astype(jnp.bfloat16)
 
     def own(k):
         return partial.at[k, pl.ds(pl.multiple_of(place.core * length, length), length)]
@@ -595,19 +1012,7 @@
     def other(k):
         return partial.at[k, pl.ds(pl.multiple_of((1 - place.core) * length, length), length)]
 
-    reduce = Reduce(
-        place,
-        own,
-        other,
-        other_in,
-        a_in,
-        b_in,
-        x_in,
-        y_in,
-        z_in,
-        model_width // 2,
-        reduce_sems,
-    )
+    reduce = Reduce(place, own, other, boxes, reduce_sems)
 
     def result_copy(slot, chip):
         return pltpu.make_async_copy(
@@ -619,10 +1024,9 @@
     def compute(step, q, j):
         chip = place.chip(q, j)
         rows = pl.ds(pl.multiple_of(chip * pair, pair), pair)
-        hidden_pre = mm(gathered[rows, half : half + model_width], first_ref[...])
-        back = mm(gathered[rows, :half], second_t_ref[:half])
-        back = back + mm(gathered[rows, 3 * half + gate_width :], second_t_ref[half:])
-        gates = mm(gathered[rows, 3 * half : 3 * half + gate_width], pick_ref[...])
+        hidden_pre = mm(gathered[rows, :model_width], first_ref[...])
+        back = mm(upstream[rows, :], second_t_ref[...])
+        gates = mm(gathered[rows, model_width:], pick_gates)
         square = hidden_pre * hidden_pre
         bent = jnp.tanh(GELU_C * hidden_pre * (1.0 + GELU_K * square))
         grow = 0.5 * (1.0 + bent)
@@ -655,27 +1059,29 @@
         result_stage[slot] = mm(gated, second_ref[...]).astype(jnp.bfloat16)
         result_copy(slot, chip).start()
 
-    gather.copy("z", 1).start()
-    gather.line(0, True)
-    gather.copy("z", 2).start()
-    gather.copy("z", 3).start()
+    upstream_copy.wait()
 
     def arrive(actions):
         for kind, j in actions:
-            if kind == "line":
-                gather.line(j, False)
+            if kind == "sides_first":
+                gather.sides_first()
+            elif kind == "line_middle":
+                place.if_middle(lambda: gather.line(j))
+            elif kind == "line_end":
+                pl.when(place.middle == 0)(lambda: gather.line(j))
             else:
                 getattr(gather, kind)(j)
 
     before = {
-        1: [("side_x", 0), ("side_y", 0), ("line", 1)],
-        4: [("corner", 0), ("side_x", 1), ("side_y", 1), ("line", 2)],
-        8: [("corner", 1), ("side_x", 2), ("side_y", 2), ("line", 3)],
-        12: [("corner", 2), ("side_x", 3), ("side_y", 3)],
+        1: [("line", 1), ("sides_first", 0), ("line_middle", 2)],
+        4: [("corner", 0), ("line_end", 2), ("line_middle", 3)],
+        6: [("line_end", 3), ("sides", 1)],
+        9: [("corner", 1), ("sides", 2)],
+        12: [("corner", 2), ("sides", 3)],
         15: [("corner", 3)],
     }
-    order = [(0, 0), (1, 0), (2, 0), (0, 1), (3, 0), (1, 1), (2, 1), (0, 2)]
-    order += [(3, 1), (1, 2), (2, 2), (0, 3), (3, 2), (1, 3), (2, 3), (3, 3)]
+    order = [(0, 0), (0, 1), (1, 0), (2, 0), (3, 0), (0, 2), (0, 3), (1, 1)]
+    order += [(2, 1), (3, 1), (1, 2), (2, 2), (3, 2), (1, 3), (2, 3), (3, 3)]
 
     def pick(step, values):
         total = 0
@@ -693,44 +1099,50 @@
         return carry
 
     lax.fori_loop(0, 16, walk, 0)
-    piece = 512
-    pieces = gathered.shape[0] // piece
+    piece = gathered.shape[0] // 8
 
     def weight_piece(number):
         rows = pl.ds(pl.multiple_of(number * piece, piece), piece)
-        left = mm_tn(gated_hidden[rows, :], gathered[rows, :half])
-        right = mm_tn(gated_hidden[rows, :], gathered[rows, 3 * half + gate_width :])
-        first = mm_tn(pre_grads[rows, :], gathered[rows, half : half + model_width])
+        second = mm_tn(gated_hidden[rows, :], upstream[rows, :])
+        first = mm_tn(pre_grads[rows, :], gathered[rows, :model_width])
 
         @pl.when(number == 0)
         def _():
-            second_out[:, :half] = left
-            second_out[:, half:] = right
+            second_out[...] = second
             first_out[...] = first
 
         @pl.when(number > 0)
         def _():
-            second_out[:, :half] += left
-            second_out[:, half:] += right
+            second_out[...] += second
             first_out[...] += first
 
+    give_back = [
+        [("corner", 3), ("corner", 2)],
+        [("corner", 1), ("sides", 3)],
+        [("corner", 0)],
+        [("sides", 2)],
+        [("sides", 1)],
+        [("line", 3)],
+        [("sides_last", 0)],
+        [("line", 2)],
+    ]
+
     def give(step, carry):
-        j = 3 - step % 4
-
-        @pl.when(step < 4)
-        def _():
-            reduce.corner(j)
-
-        @pl.when(step >= 4)
-        def _():
-            reduce.side_x(j)
-            reduce.side_y(j)
+        for number, actions in enumerate(give_back):
+
+            @pl.when(step == number)
+            def _(actions=actions):
+                for kind, j in actions:
+                    if kind == "sides_last":
+                        reduce.sides_last()
+                    else:
+                        getattr(reduce, kind)(j)
 
         weight_piece(step)
         return carry
 
-    lax.fori_loop(0, pieces, give, 0)
-    lax.fori_loop(0, 3, lambda step, carry: (reduce.line(3 - step), carry)[1], 0)
+    lax.fori_loop(0, len(give_back), give, 0)
+    reduce.line(1)
 
     def put(at, total):
         rows_out[at, :] = total
@@ -742,49 +1154,45 @@
     reduce.finish()
 
 
-def call_experts(packed, expert_first, expert_second, pick):
+def call_experts(packed, upstream, expert_first, expert_second):
     local_count, model_width, hidden_width = expert_first.shape
     wide = local_count * hidden_width
     length, width = packed.shape
-    total = GRID[0] * GRID[1] * length
-    gate_width = pick.shape[0]
-    first = expert_first.transpose(1, 0, 2).reshape(model_width, wide)
-    first_t = expert_first.transpose(0, 2, 1).reshape(wide, model_width)
-    second = expert_second.reshape(wide, model_width)
-    second_t = expert_second.transpose(2, 0, 1).reshape(model_width, wide)
-    out_width = model_width + gate_width
-    split = model_width // 2
+    total = upstream.shape[0]
     vmem = pl.BlockSpec(memory_space=pltpu.VMEM)
-    flops = 12 * total * model_width * wide
+    hbm = pl.BlockSpec(memory_space=pl.ANY)
+    low = jnp.bfloat16
     rows_sum, result, first_sum, second_sum = pl.pallas_call(
         functools.partial(expert_kernel, model_width, local_count),
         out_shape=(
-            jax.ShapeDtypeStruct((length, out_width), jnp.float32),
-            jax.ShapeDtypeStruct((total, model_width), jnp.bfloat16),
+            jax.ShapeDtypeStruct((length, width), jnp.float32),
+            jax.ShapeDtypeStruct((total, model_width), low),
             jax.ShapeDtypeStruct((wide, model_width), jnp.float32),
             jax.ShapeDtypeStruct((wide, model_width), jnp.float32),
         ),
-        in_specs=[vmem] * 6,
-        out_specs=(vmem, pl.BlockSpec(memory_space=pl.ANY), vmem, vmem),
+        in_specs=[vmem, hbm, vmem, vmem],
+        out_specs=(vmem, hbm, vmem, vmem),
         scratch_shapes=[
-            pltpu.VMEM((total, width), jnp.bfloat16),
-            pltpu.VMEM((total, wide), jnp.bfloat16),
-            pltpu.VMEM((total, wide), jnp.bfloat16),
-            pltpu.VMEM((16, 2 * length, out_width), jnp.bfloat16),
-            *reduce_scratch(length, out_width, split),
-            pltpu.VMEM((2, 2 * length, model_width), jnp.bfloat16),
+            pltpu.VMEM((total, width), low),
+            pltpu.VMEM((total, model_width), low),
+            pltpu.VMEM((model_width, wide), low),
+            pltpu.VMEM((wide, model_width), low),
+            pltpu.VMEM((model_width, wide), low),
+            pltpu.VMEM((total, wide), low),
+            pltpu.VMEM((total, wide), low),
+            pltpu.VMEM((16, 2 * length, width), low),
+            *reduce_scratch(length, width),
+            pltpu.VMEM((2, 2 * length, model_width), low),
             pltpu.SemaphoreType.DMA((2, N_SEM)),
             pltpu.SemaphoreType.DMA((2, N_SEM)),
             pltpu.SemaphoreType.DMA((2,)),
+            pltpu.SemaphoreType.DMA,
         ],
         compiler_params=pltpu.CompilerParams(
             collective_id=0, has_side_effects=True, vmem_limit_bytes=62 * 2**20
         ),
-        cost_estimate=pl.CostEstimate(
-            flops=flops, bytes_accessed=4 * total * model_width, transcendentals=total * wide
-        ),
         name="experts",
-    )(packed, first, first_t, second, second_t, pick)
+    )(packed, upstream, expert_first, expert_second.reshape(wide, model_width))
     first_sum = first_sum.reshape(local_count, hidden_width, model_width).transpose(0, 2, 1)
     return rows_sum, result, first_sum, second_sum.reshape(expert_second.shape)
 
@@ -796,9 +1204,9 @@
     place = Place()
     enter(place)
     reduces, gathers, loads = [], [], []
-    for number, (rows, width, split) in enumerate(shapes):
+    for number, (rows, width) in enumerate(shapes):
         held, refs = refs[0], refs[1:]
-        boxes, refs = refs[:6], refs[6:]
+        boxes, refs = refs[:8], refs[8:]
         sems, load_sem, refs = refs[0], refs[1], refs[2:]
 
         def source(k, core, rows=rows, ref=ins[number]):
@@ -810,8 +1218,7 @@
                 place,
                 lambda k, held=held: held.at[k],
                 lambda k, source=source: source(k, 1 - place.core),
-                *boxes,
-                split,
+                boxes,
                 sems,
             )
         )
@@ -822,7 +1229,7 @@
         )
         if number:
             buf, gather_sems, out_sem, refs = refs[0], refs[1], refs[2], refs[3:]
-            gathers.append((Gather(place, buf, rows, split, gather_sems), outs[number - 1], out_sem))
+            gathers.append((Gather(place, buf, rows, gather_sems), outs[number - 1], out_sem))
 
     def begin(step, carry):
         k = 15 - step
@@ -833,32 +1240,17 @@
 
     lax.fori_loop(0, 16, begin, 0)
 
-    def corner(step, carry):
-        for reduce, load in zip(reduces, loads):
-            load(15 - step).wait()
-            reduce.corner(3 - step)
+    def arrive(k, carry):
+        for load in loads:
+            load(k).wait()
         return carry
 
-    def side(step, carry):
-        for reduce, load in zip(reduces, loads):
-            load(7 - step).wait()
-            load(11 - step).wait()
-            reduce.side_x(3 - step)
-            reduce.side_y(3 - step)
-        return carry
-
-    def line(step, carry):
-        for reduce, load in zip(reduces, loads):
-            load(3 - step).wait()
-            reduce.line(3 - step)
-        return carry
-
-    lax.fori_loop(0, 4, corner, 0)
-    lax.fori_loop(0, 4, side, 0)
-    lax.fori_loop(0, 3, line, 0)
+    lax.fori_loop(0, 16, arrive, 0)
+    for kind, j in RETURN_ORDER:
+        for reduce in reduces:
+            getattr(reduce, kind)(*j)
     for number in reversed(range(count)):
-        reduce, load = reduces[number], loads[number]
-        load(0).wait()
+        reduce = reduces[number]
         mine = first_out if number == 0 else gathers[number - 1][0].block(0, 0)
 
         def put(at, total, mine=mine):
@@ -867,11 +1259,7 @@
         reduce.last(put)
         if number == 0:
             continue
-        gather = gathers[number - 1][0]
-        gather.copy("z", 1).start()
-        gather.line(0, True)
-        gather.copy("z", 2).start()
-        gather.copy("z", 3).start()
+        gathers[number - 1][0].begin()
 
     def pair_copy(number, q, j):
         gather, out, sem = gathers[number]
@@ -884,25 +1272,11 @@
             gathers[number][0].whole(q, j)
             pair_copy(number, q, j).start()
 
-    def spread(j, carry):
+    for kind, j, blocks in SPREAD_ORDER:
         for gather, _, _ in gathers:
-            gather.side_x(j)
-            gather.side_y(j)
-
-        @pl.when(j < 3)
-        def _():
-            for gather, _, _ in gathers:
-                gather.line(j + 1, False)
-
-        store(0, j)
-        store(1, j)
-        store(2, j)
-        for gather, _, _ in gathers:
-            gather.corner(j)
-        store(3, j)
-        return carry
-
-    lax.fori_loop(0, 4, spread, 0)
+            getattr(gather, kind)(*j)
+        for block in blocks:
+            store(*block)
 
     def drain(k, carry):
         for number in range(count - 1):
@@ -920,13 +1294,12 @@
     total = GRID[0] * GRID[1]
     shapes = []
     for part in parts:
-        width = part.shape[1]
-        shapes.append((part.shape[0] // total, width, width // 256 * 128))
+        shapes.append((part.shape[0] // total, part.shape[1]))
     scratch = []
-    for number, (rows, width, split) in enumerate(shapes):
+    for number, (rows, width) in enumerate(shapes):
         scratch += [
             pltpu.VMEM((16, rows, width), jnp.bfloat16),
-            *reduce_scratch(rows, width, split),
+            *reduce_scratch(rows, width),
             pltpu.SemaphoreType.DMA((2, N_SEM)),
             pltpu.SemaphoreType.DMA((16,)),
         ]
@@ -937,7 +1310,7 @@
                 pltpu.SemaphoreType.DMA((16,)),
             ]
     hbm = pl.BlockSpec(memory_space=pl.ANY)
-    rows, width, _ = shapes[0]
+    rows, width = shapes[0]
     return pl.pallas_call(
         functools.partial(sums_kernel, shapes),
         out_shape=(
@@ -987,44 +1360,82 @@
     )
     stream = tokens.astype(jnp.float32)
     upstream = cotangent.astype(jnp.float32)
-    after_attention, saved_parts = attention_forward(
-        stream, segments[0], value_ids[0], output_ids[0], shared
-    )
-    normed_low = layer_norm(after_attention, gain_feedforward).astype(jnp.bfloat16)
-    logits = jnp.dot(normed_low, expert_router, preferred_element_type=jnp.float32)
-    sigmoid_out = jax.nn.sigmoid(logits)
-    mask = expert_mask(ffn_ids[0], expert_count)
-    dense_gates = (sigmoid_out * mask).astype(jnp.bfloat16)
-    after_low = after_attention.astype(jnp.bfloat16)
     own_kernels = (lax.axis_size("dp"), lax.axis_size("expert")) == GRID
     if own_kernels:
-        model_width = tokens.shape[1]
+        length, model_width = tokens.shape
         gate_width = -(-expert_count // 128) * 128
-        me = lax.axis_index("dp") * lax.axis_size("expert") + lax.axis_index("expert")
-        owner = me * local_count + jnp.arange(local_count * expert_first.shape[2]) // expert_first.shape[2]
-        pick = (jnp.arange(gate_width)[:, None] == owner[None, :]).astype(jnp.bfloat16)
-        padded = jnp.pad(dense_gates, ((0, 0), (0, gate_width - expert_count)))
-        half = model_width // 2
-        packed = jnp.concatenate(
-            [cotangent[:, :half], after_low, padded, cotangent[:, half:]], axis=1
+        (
+            upstream_rows,
+            packed,
+            after_attention,
+            normed_attention,
+            normed_low,
+            queries,
+            key_rows,
+            projected,
+            values,
+            probability,
+            mixed,
+            gated_rows,
+            value_gates,
+            value_slope,
+            output_gates,
+            output_slope,
+            expert_slope,
+        ) = call_attention(
+            tokens,
+            cotangent,
+            gain_attention,
+            gain_feedforward,
+            shared[1:],
+            expert_router,
+            segments,
+            value_ids[0],
+            output_ids[0],
+            ffn_ids[0],
+            gate_width,
+        )
+        by_head = (length, HEADS, HEAD)
+        by_expert = (length, HEADS, ATT_EXP)
+        saved_parts = (
+            normed_attention,
+            queries.reshape(by_head),
+            key_rows.reshape(by_head),
+            value_slope.reshape(by_expert),
+            output_slope.reshape(by_expert),
+            value_gates.reshape(by_expert),
+            output_gates.reshape(by_expert),
+            tokens,
+            projected.reshape(length, HEADS, ATT_EXP, HEAD),
+            values.reshape(by_head),
+            probability,
+            probability.astype(jnp.bfloat16),
+            mixed.reshape(by_head),
+            gated_rows,
         )
         rows_sum, result, first_sum, second_sum = call_experts(
-            packed, expert_first, expert_second, pick
+            packed, upstream_rows, expert_first, expert_second
         )
         token_grad = rows_sum[:, :model_width]
         gate_back = rows_sum[:, model_width : model_width + expert_count]
     else:
+        after_attention, saved_parts = attention_forward(
+            stream, segments[0], value_ids[0], output_ids[0], shared
+        )
+        normed_low = layer_norm(after_attention, gain_feedforward).astype(jnp.bfloat16)
+        logits = jnp.dot(normed_low, expert_router, preferred_element_type=jnp.float32)
+        sigmoid_out = jax.nn.sigmoid(logits)
+        dense_gates = sigmoid_out * expert_mask(ffn_ids[0], expert_count)
+        expert_slope = dense_gates * (1.0 - sigmoid_out)
         result, token_grad, gate_back, first_sum, second_sum = expert_exchange(
-            after_low,
+            after_attention.astype(jnp.bfloat16),
             cotangent,
-            dense_gates,
+            dense_gates.astype(jnp.bfloat16),
             expert_first,
             expert_second,
             max(1, owner_total // 32),
         )
-    logit_grad = (
-        gate_back.astype(jnp.float32) * mask * sigmoid_out * (1.0 - sigmoid_out)
-    ).astype(jnp.bfloat16)
+    logit_grad = (gate_back.astype(jnp.float32) * expert_slope).astype(jnp.bfloat16)
     router_sum = jnp.einsum("sa,sb->ab", normed_low, logit_grad, preferred_element_type=jnp.float32)
     normed_grad = jnp.einsum(
         "sb,ab->sa", logit_grad, expert_router, preferred_element_type=jnp.float32

time: 433 us -> 415 us (0.958)
  Pallas kernels: 308 us -> 295 us
  matrix products: 39.5 us -> 29.4 us
  local copies, waits for them, and re-layouts: 43.5 us -> 52.6 us
    pallas_call x0 -> x1, Pallas kernels: none -> 50 us  [call_attention(): pl.pallas_call(attention_kernel, out_shape=tuple((jax.ShapeDtypeStruct(*s...]
    pallas_call x1, Pallas kernels: 139 us -> 101 us  [call_experts(): pl.pallas_call(functools.partial(expert_kernel, model_width, local_count)...]
    pallas_call x1, Pallas kernels: 170 us -> 144 us  [call_sums(): pl.pallas_call(functools.partial(sums_kernel, shapes), out_shape=(jax.Sha...]
    dot_general x9 -> x0, matrix products: 12.3 us -> none  [the longest x1 4.63 us: attention_forward(): jnp.dot(stream_low, value_weight, preferred_element_type=jnp.float32)]
    pallas_call x0 -> x3, local copies, waits for them, and re-layouts: none -> 4.61 us  [call_attention(): pl.pallas_call(attention_kernel, out_shape=tuple((jax.ShapeDtypeStruct(*s...]
    unnamed x133 -> x54, local copies, waits for them, and re-layouts: 8.78 us -> 10.4 us
where the time goes in v3:
time: 415 us; the launch traced here: 413 us
  Pallas kernels  295 us (71%)
  local copies, waits for them, and re-layouts  52.6 us (13%)
  other arithmetic  35.3 us (9%)
  matrix products  29.4 us (7%)
    pallas_call x1, Pallas kernels, call_sums(): pl.pallas_call(functools.partial(sums_kernel, shapes), out_shape=(jax.Sha...  144 us
    pallas_call x1, Pallas kernels, call_experts(): pl.pallas_call(functools.partial(expert_kernel, model_width, local_count)...  101 us
    pallas_call x1, Pallas kernels, call_attention(): pl.pallas_call(attention_kernel, out_shape=tuple((jax.ShapeDtypeStruct(*s...  50 us
    convert_element_type x4, other arithmetic, body(): summed.append(low[:, start:start + part.shape[1]].astype(jnp.float32))  14.8 us
    concatenate x1, local copies, waits for them, and re-layouts, body(): low = jnp.concatenate([part.astype(jnp.bfloat16) for part in parts], axis=1)  11.5 us
    unnamed x54, local copies, waits for them, and re-layouts  10.4 us

profile of v3, /device:TPU:1, one launch (start us, length us, event | category | flops | bytes accessed | tf_op | source)
XLA Modules:
  0.0 413.4 jit_solution(3385127055201340256)
XLA Ops:
  0.6 1.1 convert_reduce_fusion
  2.2 1.4 copy.88.value_ids_ref
  3.6 1.4 copy.89.output_ids_ref
  5.1 1.4 copy.84
  6.5 1.7 copy.85.value_router_ref
  8.2 1.7 copy.86.output_router_ref
  9.8 1.8 copy.87.expert_router_ref
  11.6 50.0 %attention.1 = (bf16[4096,1024]{1,0:T(8,128)(2,1)}, bf16[128,1152]{1,0:T(8,128)(2,1)}, f32[128,1024]{1,0:T(8,128)}, bf16[128,1024]{1,0:T(8,128)(2,1)}, bf16[128,...) custom-call(bf16[128,1024]{1,0:T(8,128)(2,1)} %tokens_ref.1, ...), custom_call_target="tpu_custom_call" | custom-call | tf_op jit(solution)/shard_map/attention/pallas_call | solution.py:940
  61.6 1.2 reduce_sum.128
  62.7 1.2 multiply_reduce_fusion.5
  64.0 0.9 copy.90
  64.9 0.9 copy.100
  66.5 1.7 copy.120
  68.1 1.7 copy.121
  69.8 1.8 copy.122
  71.6 2.8 copy.102
  74.4 100.7 %experts.1 = (f32[128,1152]{1,0:T(8,128)}, bf16[4096,1024]{1,0:T(8,128)(2,1)}, f32[384,1024]{1,0:T(8,128)}, f32[384,1024]{1,0:T(8,128)}) custom-call(bf16[128,1152]{1,0:T(8,128)(2,1)} %get-tuple-element.38.packed_ref, bf16[4096,1024]{1,0:T(8,128)(2,1)} %get-tuple-element.39.upstream_ref, bf16[3,1024,128]{2,1,0:T(8,128)(2,1)} %first_in.1, ...), custom_call_target="tpu_custom_call" | custom-call | tf_op jit(solution)/shard_map/experts/pallas_call | solution.py:1165
  175.1 0.9 multiply_convert_fusion.4
  176.3 3.0 copy.111
  181.8 4.4 %fusion.1 = f32[128,2560]{1,0:T(8,128)S(1)} fusion(bf16[2560,1024]{1,0:T(8,128)(2,1)} %output_ref.1, f32[128,1024]{1,0:T(8,128)S(1)} %add_add_fusion.2), kind=kOutput, calls=%fused_computation.5 | convolution fusion | flops 671875072 | bytes 7077888 | tf_op jit(solution)/shard_map/sb,ab->sa/dot_general | solution.py:139
  186.2 1.5 copy.91
  187.7 1.6 multiply_reduce_fusion
  190.7 1.5 multiply_reduce_fusion.1
  192.3 1.1 fusion.5
  193.4 1.8 fusion.4
  196.0 0.9 multiply_convert_fusion.2
  198.0 1.7 copy.106
  200.5 1.0 fusion.29
  201.5 1.0 fusion.30
  202.5 1.8 fusion.28
  204.3 1.2 fusion.15
  205.6 1.0 fusion.26
  206.6 5.2 %convolution_add_fusion.1 = f32[128,1024]{1,0:T(8,128)} fusion(bf16[128,2560]{0,1:T(8,128)(2,1)S(1)} %bitcast.74, bf16[1024,2560]{1,0:T(8,128)(2,1)} %value_ref.1, f32[128,1024]{1,0:T(8,128)S(1)} %add_add_fusion.2, f32[128]{0:T(128)S(1)} %negate_multiply_fusion, f32[128]{0:T(128)S(1)} %get-tuple-element.119, f32[128]{0:T(128)} %broadcast_multiply_fusion, ...), kind=kOutput, calls=%fused_computation.15 | convolution fusion | flops 672399360 | bytes 7739392 | tf_op jit(solution)/shard_map/sb,ab->sa/dot_general | solution.py:210
  213.2 1.4 convolution_convert_fusion.4
  214.7 3.9 convolution_convert_fusion.refs_2_
  218.5 3.9 fusion
  222.5 11.5 %concatenate.3 = bf16[1024,3722]{1,0:T(8,128)(2,1)} concatenate(bf16[1024,512]{1,0:T(8,128)(2,1)} %convolution_convert_fusion.4, bf16[1024,512]{1,0:T(8,128)(2,1)S(1)} %convolution_convert_fusion.3, bf16[1024,2560]{1,0:T(8,128)(2,1)} %fusion, bf16[1024,20]{1,0:T(8,128)(2,1)S(1)} %copy-done.10, bf16[1024,20]{1,0:T(8,128)(2,1)} %copy.107, bf16[1024,96]{1,0:T(8,128)(2,1)S(1)} %copy-done.8, ...), dimensions={1} | concatenate | bytes 15245312 | tf_op jit(solution)/shard_map/concatenate | solution.py:1458
  234.0 7.0 %pad.4.refs_1_ = bf16[1024,3840]{1,0:T(8,128)(2,1)} pad(bf16[1024,3722]{1,0:T(8,128)(2,1)} %concatenate.3, bf16[]{:T(256)} %constant.20.clone.1), padding=0_0x0_118 | pad | bytes 15486978 | tf_op jit(solution)/shard_map/jit(_pad)/pad | solution.py:1459
  241.0 144.5 %sums.1 = (f32[128,1024]{1,0:T(8,128)}, bf16[1024,3840]{1,0:T(8,128)(2,1)}, bf16[2560,1024]{1,0:T(8,128)(2,1)}) custom-call(bf16[4096,1024]{1,0:T(8,128)(2,1)} %get-tuple-element.40.refs_0_, bf16[1024,3840]{1,0:T(8,128)(2,1)} %pad.4.refs_1_, bf16[2560,1024]{1,0:T(8,128)(2,1)} %convolution_convert_fusion.refs_2_), custom_call_target="tpu_custom_call" | custom-call | tf_op jit(solution)/shard_map/sums/pallas_call | solution.py:1314
  385.5 1.8 add_convert_fusion
  387.3 2.1 convert_reduce_fusion.1
  389.4 1.2 slice_convert_fusion.3
  390.6 0.9 copy.114
  391.5 1.2 slice_convert_fusion.4
  394.4 4.3 %slice_convert_fusion.1 = (f32[1024,512]{1,0:T(8,128)}, f32[1024,512]{1,0:T(8,128)}) fusion(bf16[1024,3840]{1,0:T(8,128)(2,1)} %get-tuple-element.57), kind=kLoop, calls=%fused_computation.26 | loop fusion | flops 1048576 | bytes 6291456 | tf_op jit(solution)/shard_map/convert_element_type | solution.py:1468
  398.7 8.1 %slice_convert_fusion = f32[1024,2560]{1,0:T(8,128)} fusion(bf16[1024,3840]{1,0:T(8,128)(2,1)} %get-tuple-element.57), kind=kLoop, calls=%fused_computation.2 | loop fusion | flops 2621440 | bytes 15728640 | tf_op jit(solution)/shard_map/convert_element_type | solution.py:1468
  406.8 5.4 %convert_element_type.184 = f32[2560,1024]{1,0:T(8,128)} convert(bf16[2560,1024]{1,0:T(8,128)(2,1)S(1)} %bitcast.79) | non-fusion elementwise | flops 2621440 | bytes 15728640 | tf_op jit(solution)/shard_map/convert_element_type | solution.py:1477
  412.2 1.1 copy.131
  (76 shorter events, 11.1 us)
Async XLA Ops:
  74.3 100.7 %copy-start.18 = (f32[128,96]{1,0:T(8,128)S(1)}, f32[128,96]{1,0:T(8,128)}, u32[]{:S(2)}) copy-start(f32[128,96]{1,0:T(8,128)} %get-tuple-element.46) | copy-start | bytes 147460
  74.3 101.7 %copy-start.15 = (bf16[128,1024]{1,0:T(8,128)(2,1)S(1)}, bf16[128,1024]{1,0:T(8,128)(2,1)}, u32[]{:S(2)}) copy-start(bf16[128,1024]{1,0:T(8,128)(2,1)} %get-tuple-element.54) | copy-start | bytes 786436
  74.4 105.8 %copy-start = (f32[128,1024]{1,0:T(8,128)S(1)}, f32[128,1024]{1,0:T(8,128)}, u32[]{:S(2)}) copy-start(f32[128,1024]{1,0:T(8,128)} %get-tuple-element.37) | copy-start | bytes 1572868
  74.4 105.8 %copy-start.13 = (bf16[1024,96]{0,1:T(8,128)(2,1)S(1)}, bf16[1024,96]{0,1:T(8,128)(2,1)}, u32[]{:S(2)}) copy-start(bf16[1024,96]{0,1:T(8,128)(2,1)} %param.27) | copy-start | bytes 589828
  74.4 105.8 %copy-start.20 = (f32[1024]{0:T(1024)S(1)}, f32[1024]{0:T(1024)}, u32[]{:S(2)}) copy-start(f32[1024]{0:T(1024)} %param.20) | copy-start | bytes 12292
  175.0 5.7 %copy-start.12 = (bf16[128,1024]{1,0:T(8,128)(2,1)S(1)}, bf16[128,1024]{1,0:T(8,128)(2,1)}, u32[]{:S(2)}) copy-start(bf16[128,1024]{1,0:T(8,128)(2,1)} %cotangent_ref.1) | copy-start | bytes 786436
  175.1 5.7 %copy-start.14 = (f32[128,1152]{1,0:T(8,128)S(1)}, f32[128,1152]{1,0:T(8,128)}, u32[]{:S(2)}) copy-start(f32[128,1152]{1,0:T(8,128)} %get-tuple-element.45) | copy-start | bytes 1769476
  180.9 6.8 %copy-start.11 = (f32[128,512]{0,1:T(8,128)S(1)}, f32[128,512]{0,1:T(8,128)}, u32[]{:S(2)}) copy-start(f32[128,512]{0,1:T(8,128)} %copy.122) | copy-start | bytes 786436
  181.8 7.6 %copy-start.4 = (f32[4,128,128]{2,1,0:T(8,128)S(1)}, f32[4,128,128]{2,1,0:T(8,128)}, u32[]{:S(2)}) copy-start(f32[4,128,128]{2,1,0:T(8,128)} %get-tuple-element.43) | copy-start | bytes 786436
  181.8 7.6 %copy-start.16 = (bf16[128,512]{1,0:T(8,128)(2,1)S(1)}, bf16[128,512]{1,0:T(8,128)(2,1)}, u32[]{:S(2)}) copy-start(bf16[128,512]{1,0:T(8,128)(2,1)} %get-tuple-element.47) | copy-start | bytes 393220
  181.8 8.9 %copy-start.17 = (f32[128,4,5]{0,2,1:T(8,128)S(1)}, f32[128,4,5]{0,2,1:T(8,128)}, u32[]{:S(2)}) copy-start(f32[128,4,5]{0,2,1:T(8,128)} %mul.179) | copy-start | bytes 30724
  187.7 9.2 %copy-start.2 = (bf16[128,1024]{1,0:T(8,128)(2,1)S(1)}, bf16[128,1024]{1,0:T(8,128)(2,1)}, u32[]{:S(2)}) copy-start(bf16[128,1024]{1,0:T(8,128)(2,1)} %get-tuple-element.41) | copy-start | bytes 786436
  189.2 15.1 %copy-start.1 = (bf16[128,1024]{1,0:T(8,128)(2,1)S(1)}, bf16[128,1024]{1,0:T(8,128)(2,1)}, u32[]{:S(2)}) copy-start(bf16[128,1024]{1,0:T(8,128)(2,1)} %tokens_ref.1) | copy-start | bytes 786436
  189.3 15.1 %copy-start.3 = (bf16[1024,512]{1,0:T(8,128)(2,1)S(1)}, bf16[1024,512]{1,0:T(8,128)(2,1)}, u32[]{:S(2)}) copy-start(bf16[1024,512]{1,0:T(8,128)(2,1)} %key_ref.1) | copy-start | bytes 3145732
  189.3 15.1 %copy-start.19 = (f32[1024]{0:T(1024)S(1)}, f32[1024]{0:T(1024)}, u32[]{:S(2)}) copy-start(f32[1024]{0:T(1024)} %param.19) | copy-start | bytes 12292
  205.6 7.7 %copy-start.7 = (bf16[4,128,128]{2,1,0:T(8,128)(2,1)S(1)}, bf16[4,128,128]{2,1,0:T(8,128)(2,1)}, u32[]{:S(2)}) copy-start(bf16[4,128,128]{2,1,0:T(8,128)(2,1)} %fusion.4) | copy-start | bytes 393220
  206.6 8.0 %copy-start.5 = (bf16[128,2560]{1,0:T(8,128)(2,1)S(1)}, bf16[128,2560]{1,0:T(8,128)(2,1)}, u32[]{:S(2)}) copy-start(bf16[128,2560]{1,0:T(8,128)(2,1)} %get-tuple-element.55) | copy-start | bytes 1966084
  218.5 3.9 copy-start.8
  218.5 3.9 copy-start.9
  218.5 3.9 copy-start.10
  394.4 12.4 %slice-start = ((s8[5242880]{0:T(1024)(128)(4,1)}), s8[4194304]{0:T(1024)(128)(4,1)S(1)}, s32[]{:S(2)}) async-start(s8[5242880]{0:T(1024)(128)(4,1)} %bitcast.78), calls=%async_computation | async-start | bytes 8388608
  398.7 8.1 %slice-start.1 = ((s8[5242880]{0:T(1024)(128)(4,1)}), s8[1048576]{0:T(1024)(128)(4,1)S(1)}, s32[]{:S(2)}) async-start(s8[5242880]{0:T(1024)(128)(4,1)} %bitcast.78), calls=%async_computation.1 | async-start | bytes 2097152
  406.8 5.4 %copy-start.6 = (f32[384,1024]{1,0:T(8,128)S(1)}, f32[384,1024]{1,0:T(8,128)}, u32[]{:S(2)}) copy-start(f32[384,1024]{1,0:T(8,128)} %get-tuple-element.60) | copy-start | bytes 4718596

commit v4 on v3

--- a/solution.py
+++ b/solution.py
@@ -496,9 +496,11 @@
 
 
 class Reduce:
-    def __init__(self, place, own, other, boxes, sems):
-        self.place, self.own, self.other = place, own, other
+    def __init__(self, place, own, other, boxes, sems, held=None):
+        self.place, self.other = place, other
         self.other_in, self.a_in, self.b_in, self.x_in, self.y_in = boxes[:5]
+        self.own = own or (lambda k: self.other_in.at[k])
+        self.extra = held or (lambda k: self.other_in.at[k])
         self.z_in = boxes[5:]
         self.rows, self.width = self.other_in.shape[1:]
         self.d_end, self.split, self.c_start = cut_columns(self.width)
@@ -592,30 +594,30 @@
     def corner(self, j):
         k = 12 + j
         self.copy("core", k).wait_recv()
-        self.add(k, slice(None), [lambda at: self.other_in[k, at, :]])
+        self.add(k, slice(None), [lambda at: self.extra(k)[at, :]])
         self.copy("a", k).start()
         self.copy("b", k).start()
 
     def side_x(self, j):
         k, split = 4 + j, self.split
         self.copy("core", k).wait_recv()
-        self.add(k, slice(0, split), [lambda at: self.other_in[k, at, :split]])
+        self.add(k, slice(0, split), [lambda at: self.extra(k)[at, :split]])
         self.copy("a", k).wait_recv()
         self.add(
             k,
             slice(split, None),
-            [lambda at: self.other_in[k, at, split:], lambda at: self.a_in[j, at, :]],
+            [lambda at: self.extra(k)[at, split:], lambda at: self.a_in[j, at, :]],
         )
 
     def side_y(self, j):
         k, split = 8 + j, self.split
         self.copy("core", k).wait_recv()
-        self.add(k, slice(split, None), [lambda at: self.other_in[k, at, split:]])
+        self.add(k, slice(split, None), [lambda at: self.extra(k)[at, split:]])
         self.copy("b", k).wait_recv()
         self.add(
             k,
             slice(0, split),
-            [lambda at: self.other_in[k, at, :split], lambda at: self.b_in[j, at, :]],
+            [lambda at: self.extra(k)[at, :split], lambda at: self.b_in[j, at, :]],
         )
 
     def sides(self, j):
@@ -639,13 +641,13 @@
         self.copy("x", j).wait_recv()
         self.copy("y", j).wait_recv()
         d_end, c_start = self.d_end, self.c_start
-        boxes = (self.other_in, self.x_in, self.y_in)
+        boxes = (self.extra(j), self.x_in.at[j], self.y_in.at[j])
         for columns, used in (
             (slice(0, d_end), boxes[:2]),
             (slice(d_end, c_start), boxes),
             (slice(c_start, None), (boxes[0], boxes[2])),
         ):
-            self.add(j, columns, [lambda at, box=box: box[j, at, columns] for box in used])
+            self.add(j, columns, [lambda at, box=box: box[at, columns] for box in used])
         self.z_give(0, j)
 
     def last(self, put):
@@ -659,8 +661,8 @@
             def step(number, carry):
                 at = pl.ds(pl.multiple_of(number * 16, 16), 16)
                 total = own[at, :].astype(jnp.float32)
-                for box in (self.other_in, self.x_in, self.y_in, self.z_in[0]):
-                    total = total + box[0, at, :].astype(jnp.float32)
+                for box in (self.extra(0), self.x_in.at[0], self.y_in.at[0], self.z_in[0].at[0]):
+                    total = total + box[at, :].astype(jnp.float32)
                 if middle:
                     total = total + self.z_in[0][2, at, :].astype(jnp.float32)
                 put(at, total)
@@ -695,34 +697,6 @@
         lax.fori_loop(1, 4, outer, 0)
         self.copy("x0", 4).wait_send()
         self.copy("y0", 8).wait_send()
-
-
-RETURN_ORDER = (
-    ("corner", (3,)),
-    ("corner", (2,)),
-    ("corner", (1,)),
-    ("sides", (3,)),
-    ("corner", (0,)),
-    ("sides", (2,)),
-    ("sides", (1,)),
-    ("line", (3,)),
-    ("sides_last", ()),
-    ("line", (2,)),
-    ("line", (1,)),
-)
-SPREAD_ORDER = (
-    ("line", (1,), [(0, 0)]),
-    ("sides_first", (), [(0, 1)]),
-    ("line", (2,), [(1, 0), (2, 0)]),
-    ("line", (3,), [(0, 2)]),
-    ("corner", (0,), [(0, 3)]),
-    ("sides", (1,), [(3, 0)]),
-    ("sides", (2,), [(1, 1), (2, 1)]),
-    ("sides", (3,), [(1, 2), (2, 2)]),
-    ("corner", (1,), [(1, 3), (2, 3)]),
-    ("corner", (2,), [(3, 1)]),
-    ("corner", (3,), [(3, 2), (3, 3)]),
-)
 
 
 def reduce_scratch(rows, width):
@@ -756,21 +730,30 @@
     average = jnp.mean(stream, axis=-1, keepdims=True)
     centred = stream - average
     variance = jnp.mean(centred * centred, axis=-1, keepdims=True)
-    return centred, lax.rsqrt(variance + 1e-05)
+    scale = lax.rsqrt(variance + 1e-05)
+    return centred * scale, scale
+
+
+def norm_pull(normed_grad, unit, scale, gain):
+    inner = normed_grad * gain
+    mean = jnp.mean(inner, axis=-1, keepdims=True)
+    along = jnp.mean(inner * unit, axis=-1, keepdims=True)
+    gain_grad = jnp.sum(normed_grad * unit, axis=0, keepdims=True)
+    return scale * (inner - mean - unit * along), gain_grad
 
 
 def mm_nt(left, right):
     return lax.dot_general(left, right, (((1,), (1,)), ((), ())), preferred_element_type=jnp.float32)
 
 
-def picked_mask(ids, groups, per_group, group_size, width):
-    column = lax.broadcasted_iota(jnp.int32, (ids.shape[0], width), 1)
-    mask = jnp.zeros((ids.shape[0], width), jnp.float32)
-    for group in range(groups):
-        for number in range(per_group):
-            at = group * per_group + number
-            mask = jnp.where(column == ids[:, at : at + 1] + group * group_size, 1.0, mask)
-    return mask
+OUTPUT_LANE = 32
+
+
+def join_routers(joined, value_router_ref, output_router_ref):
+    count = value_router_ref.shape[0]
+    joined[...] = jnp.zeros_like(joined)
+    joined[:count, :] = value_router_ref[...]
+    joined[OUTPUT_LANE : OUTPUT_LANE + count, :] = output_router_ref[...]
 
 
 def attention_kernel(
@@ -778,10 +761,10 @@
     cotangent_ref,
     gain_attention_ref,
     gain_feedforward_ref,
-    query_ref,
-    key_ref,
-    value_ref,
-    output_ref,
+    query_in,
+    key_in,
+    value_in,
+    output_in,
     value_router_ref,
     output_router_ref,
     expert_router_ref,
@@ -801,46 +784,79 @@
     probability_out,
     mixed_out,
     gated_out,
-    value_gates_out,
-    value_slope_out,
-    output_gates_out,
-    output_slope_out,
+    gates_out,
+    slopes_out,
     expert_slope_out,
+    query_ref,
+    key_ref,
+    value_ref,
+    output_ref,
+    routers,
+    all_ids,
     own_sem,
+    weight_sems,
     gather_sems,
 ):
     place = Place()
     length, model_width = tokens_ref.shape
-    expert_count = expert_router_ref.shape[1]
-    router_width = value_router_ref.shape[1]
-    enter(place)
+    expert_count = expert_router_ref.shape[0]
+    loads = [
+        pltpu.make_async_copy(src, dst, weight_sems.at[number])
+        for number, (src, dst) in enumerate(
+            (
+                (query_in, query_ref),
+                (key_in, key_ref),
+                (value_in, value_ref),
+                (output_in, output_ref),
+            )
+        )
+    ]
     gather = Gather(place, upstream_out, length, gather_sems)
     own_copy = pltpu.make_async_copy(cotangent_ref, gather.block(0, 0), own_sem)
     own_copy.start()
+    for load in loads:
+        load.start()
+    enter(place)
     own_copy.wait()
     gather.begin()
 
+    join_routers(routers, value_router_ref, output_router_ref)
+    top = value_ids_ref.shape[1]
+    all_ids[...] = jnp.zeros_like(all_ids)
+    for head in range(HEADS):
+        at = head * top
+        all_ids[at : at + top, :] = value_ids_ref[head].astype(jnp.float32) + float(head * ATT_EXP)
+        all_ids[16 + at : 16 + at + top, :] = output_ids_ref[head].astype(jnp.float32) + float(
+            OUTPUT_LANE + head * ATT_EXP
+        )
+    ffn_top = ffn_ids_ref.shape[0]
+    all_ids[32 : 32 + ffn_top, :] = ffn_ids_ref[...].astype(jnp.float32)
+    ids = all_ids[...].T
+    lane = lax.broadcasted_iota(jnp.int32, (length, gates_out.shape[1]), 1).astype(jnp.float32)
+
+    def named(columns):
+        mask = jnp.zeros(lane.shape, jnp.float32)
+        for at in columns:
+            mask = jnp.where(lane == ids[:, at : at + 1], 1.0, mask)
+        return mask
+
     stream_low = tokens_ref[...]
     stream = stream_low.astype(jnp.float32)
-    centred, scale = norm_parts(stream)
-    normed = (centred * scale * gain_attention_ref[...]).astype(jnp.bfloat16)
+    unit, _ = norm_parts(stream)
+    normed = (unit * gain_attention_ref[...]).astype(jnp.bfloat16)
     normed_out[...] = normed
+    sig = jax.nn.sigmoid(mm_nt(normed, routers[...]))
+    gates = named([*range(HEADS * top), *range(16, 16 + HEADS * top)]) * sig
+    gates_out[...] = gates
+    slopes_out[...] = gates * (1.0 - sig)
+    loads[0].wait()
     queries_out[...] = mm(normed, query_ref[...]).astype(jnp.bfloat16)
+    loads[1].wait()
     keys_out[...] = mm(normed, key_ref[...]).astype(jnp.bfloat16)
-    value_sig = jax.nn.sigmoid(mm(normed, value_router_ref[...]))
-    output_sig = jax.nn.sigmoid(mm(normed, output_router_ref[...]))
-    picks = value_ids_ref.shape[1] // HEADS
-    value_mask = picked_mask(value_ids_ref[...], HEADS, picks, ATT_EXP, router_width)
-    output_mask = picked_mask(output_ids_ref[...], HEADS, picks, ATT_EXP, router_width)
-    value_gates = value_mask * value_sig
-    output_gates = output_mask * output_sig
-    value_gates_out[...] = value_gates
-    output_gates_out[...] = output_gates
-    value_slope_out[...] = value_gates * (1.0 - value_sig)
-    output_slope_out[...] = output_gates * (1.0 - output_sig)
     gather.line(1)
     gather.sides_first()
     gather.line(2)
+    loads[2].wait()
     head_width = ATT_EXP * HEAD
     for head in range(HEADS):
         columns = slice(head * head_width, (head + 1) * head_width)
@@ -848,7 +864,7 @@
         total = jnp.zeros((length, HEAD), jnp.float32)
         for e in range(ATT_EXP):
             at = head * ATT_EXP + e
-            total = total + value_gates[:, at : at + 1] * projected_out[:, at * HEAD : (at + 1) * HEAD]
+            total = total + gates[:, at : at + 1] * projected_out[:, at * HEAD : (at + 1) * HEAD]
         values_out[:, head * HEAD : (head + 1) * HEAD] = total.astype(jnp.bfloat16)
     gather.line(3)
     documents = jnp.broadcast_to(segments_ref[...].astype(jnp.float32), (length, length))
@@ -866,23 +882,23 @@
         mixed_out[:, columns] = mixed
         for e in range(ATT_EXP):
             at = head * ATT_EXP + e
-            gated_out[:, at * HEAD : (at + 1) * HEAD] = (
-                output_gates[:, at : at + 1] * mixed
-            ).astype(jnp.bfloat16)
+            gate = gates[:, OUTPUT_LANE + at : OUTPUT_LANE + at + 1]
+            gated_out[:, at * HEAD : (at + 1) * HEAD] = (gate * mixed).astype(jnp.bfloat16)
+    gather.corner(0)
+    loads[3].wait()
     after = stream + mm(gated_out[...], output_ref[...])
     after_out[...] = after
     packed_out[:, :model_width] = after.astype(jnp.bfloat16)
-    centred, scale = norm_parts(after)
-    normed_ffn = (centred * scale * gain_feedforward_ref[...]).astype(jnp.bfloat16)
+    unit, _ = norm_parts(after)
+    normed_ffn = (unit * gain_feedforward_ref[...]).astype(jnp.bfloat16)
     normed_ffn_out[...] = normed_ffn
-    expert_sig = jax.nn.sigmoid(mm(normed_ffn, expert_router_ref[...]))
-    expert_mask_ = picked_mask(ffn_ids_ref[...], 1, ffn_ids_ref.shape[1], 0, expert_count)
-    expert_gates = expert_mask_ * expert_sig
+    expert_sig = jax.nn.sigmoid(mm_nt(normed_ffn, expert_router_ref[...]))
+    expert_gates = named(range(32, 32 + ffn_top))[:, :expert_count] * expert_sig
     gate_width = packed_out.shape[1] - model_width
     packed_out[:, model_width:] = jnp.zeros((length, gate_width), jnp.bfloat16)
     packed_out[:, model_width : model_width + expert_count] = expert_gates.astype(jnp.bfloat16)
-    expert_slope_out[...] = expert_gates * (1.0 - expert_sig)
-    gather.corner(0)
+    expert_slope_out[...] = jnp.zeros((length, gate_width), jnp.float32)
+    expert_slope_out[:, :expert_count] = expert_gates * (1.0 - expert_sig)
     for j in (1, 2, 3):
         gather.sides(j)
     for j in (1, 2, 3):
@@ -899,10 +915,9 @@
 def call_attention(
     tokens,
     cotangent,
-    gain_attention,
-    gain_feedforward,
-    shared_weights,
-    expert_router,
+    gains,
+    weights,
+    routers,
     segments,
     value_ids,
     output_ids,
@@ -911,10 +926,8 @@
 ):
     length, model_width = tokens.shape
     total = GRID[0] * GRID[1] * length
-    expert_count = expert_router.shape[1]
-    wide = shared_weights[3].shape[0]
+    wide = weights[3].shape[0]
     narrow = HEADS * HEAD
-    router_width = HEADS * ATT_EXP
     low, full = jnp.bfloat16, jnp.float32
     shapes = (
         ((total, model_width), low),
@@ -929,20 +942,25 @@
         ((HEADS, length, length), full),
         ((length, narrow), full),
         ((length, wide), low),
-        ((length, router_width), full),
-        ((length, router_width), full),
-        ((length, router_width), full),
-        ((length, router_width), full),
-        ((length, expert_count), full),
+        ((length, 128), full),
+        ((length, 128), full),
+        ((length, gate_width), full),
     )
     vmem = pl.BlockSpec(memory_space=pltpu.VMEM)
     hbm = pl.BlockSpec(memory_space=pl.ANY)
     return pl.pallas_call(
         attention_kernel,
         out_shape=tuple(jax.ShapeDtypeStruct(*shape) for shape in shapes),
-        in_specs=[vmem] * 15,
+        in_specs=[vmem] * 4 + [hbm] * 4 + [vmem] * 7,
         out_specs=(hbm, *([vmem] * (len(shapes) - 1))),
-        scratch_shapes=[pltpu.SemaphoreType.DMA, pltpu.SemaphoreType.DMA((2, N_SEM))],
+        scratch_shapes=[
+            *(pltpu.VMEM(weight.shape, low) for weight in weights),
+            pltpu.VMEM((128, model_width), low),
+            pltpu.VMEM((128, length), full),
+            pltpu.SemaphoreType.DMA,
+            pltpu.SemaphoreType.DMA((4,)),
+            pltpu.SemaphoreType.DMA((2, N_SEM)),
+        ],
         compiler_params=pltpu.CompilerParams(
             collective_id=2, has_side_effects=True, vmem_limit_bytes=62 * 2**20
         ),
@@ -950,15 +968,439 @@
     )(
         tokens,
         cotangent,
-        gain_attention[None],
-        gain_feedforward[None],
-        *shared_weights,
-        expert_router,
+        *gains,
+        *weights,
+        *routers,
         segments,
-        value_ids.reshape(length, -1),
-        output_ids.reshape(length, -1),
-        ffn_ids,
-    )
+        value_ids.transpose(1, 2, 0),
+        output_ids.transpose(1, 2, 0),
+        ffn_ids.T,
+    )
+
+
+HELD = 6
+HELD_ORDER = (15, 14, 13, 7, 11, 12, 6, 10, 5, 9, 3, 4, 8, 2, 1, 0)
+GAIN_LANE = 64
+
+
+def backward_kernel(
+    rows_ref,
+    tokens_ref,
+    cotangent_ref,
+    gain_attention_ref,
+    gain_feedforward_ref,
+    value_router_ref,
+    output_router_ref,
+    expert_router_ref,
+    after_ref,
+    normed_ref,
+    normed_ffn_ref,
+    queries_ref,
+    keys_ref,
+    projected_ref,
+    values_ref,
+    probability_ref,
+    mixed_ref,
+    gated_ref,
+    gates_ref,
+    slopes_ref,
+    expert_slope_ref,
+    query_in,
+    key_in,
+    value_in,
+    output_in,
+    result_in,
+    block_out,
+    stream_out,
+    low_out,
+    output_low_out,
+    query_ref,
+    key_ref,
+    value_ref,
+    output_ref,
+    routers,
+    expert_router,
+    after_grad,
+    after_low,
+    gated_grad,
+    projected_grad,
+    both_grad,
+    held,
+    low_part,
+    output_part,
+    low_own,
+    output_own,
+    weight_sems,
+    held_sems,
+    own_sems,
+    *refs,
+):
+    place = Place()
+    length, model_width = tokens_ref.shape
+    wide = value_ref.shape[1]
+    narrow = query_ref.shape[1]
+    expert_count = expert_router_ref.shape[0]
+    low_rows, output_rows = low_own.shape[0], output_own.shape[0]
+    low_type = jnp.bfloat16
+
+    def held_copy(number):
+        k = HELD_ORDER[number]
+        start = (2 * place.chip(k // 4, k % 4) + place.core) * length
+        return pltpu.make_async_copy(
+            result_in.at[pl.ds(pl.multiple_of(start, length), length)],
+            held.at[number % HELD],
+            held_sems.at[number % HELD],
+        )
+
+    def other_rows(ref, rows):
+        def get(k):
+            start = (2 * place.chip(k // 4, k % 4) + 1 - place.core) * rows
+            return ref.at[pl.ds(pl.multiple_of(start, rows), rows)]
+
+        return get
+
+    def own_rows(ref, rows):
+        def get(k):
+            start = (2 * place.chip(k // 4, k % 4) + place.core) * rows
+            return ref.at[pl.ds(pl.multiple_of(start, rows), rows)]
+
+        return get
+
+    slots = {k: number % HELD for number, k in enumerate(HELD_ORDER)}
+    results = Reduce(
+        place,
+        None,
+        other_rows(result_in, length),
+        refs[0:8],
+        refs[8],
+        lambda k: held.at[slots[k]],
+    )
+    outputs = Reduce(
+        place,
+        own_rows(output_part, output_rows),
+        other_rows(output_part, output_rows),
+        refs[9:17],
+        refs[17],
+    )
+    lows = Reduce(
+        place,
+        own_rows(low_part, low_rows),
+        other_rows(low_part, low_rows),
+        refs[18:26],
+        refs[26],
+    )
+    spread_outputs = Gather(place, output_low_out, output_rows, refs[27])
+    spread_lows = Gather(place, low_out, low_rows, refs[28])
+    weights = ((output_in, output_ref), (query_in, query_ref), (key_in, key_ref), (value_in, value_ref))
+    loads = [
+        pltpu.make_async_copy(src, dst, weight_sems.at[number])
+        for number, (src, dst) in enumerate(weights)
+    ]
+
+    def hand_over(reduce):
+        def step(number, carry):
+            reduce.copy("core", 15 - number).start()
+            return carry
+
+        lax.fori_loop(0, 16, step, 0)
+
+    fetched = [0]
+
+    def result_event(kind, *j):
+        used = {"corner": 1, "sides": 2, "line": 1, "sides_last": 2, "last": 1}[kind]
+        start = fetched[0]
+        for number in range(start, start + used):
+            held_copy(number).wait()
+        if kind == "last":
+
+            def put(at, total):
+                block_out[at, :] = (after_ref[at, :] + total).astype(low_type)
+
+            results.last(put)
+        else:
+            getattr(results, kind)(*j)
+        for number in range(start + HELD, start + HELD + used):
+            if number < len(HELD_ORDER):
+                held_copy(number).start()
+        fetched[0] = start + used
+
+    def send_around(reduce, gather, own, own_sem):
+        def put(at, total):
+            own[at, :] = total.astype(low_type)
+
+        reduce.last(put)
+        copy = pltpu.make_async_copy(own, gather.block(0, 0), own_sem)
+        copy.start()
+        copy.wait()
+        gather.begin()
+
+    for number in range(HELD):
+        held_copy(number).start()
+    for load in loads:
+        load.start()
+    enter(place)
+    hand_over(results)
+    result_event("corner", 3)
+    result_event("corner", 2)
+    result_event("corner", 1)
+
+    join_routers(routers, value_router_ref, output_router_ref)
+    expert_router[...] = jnp.zeros_like(expert_router)
+    expert_router[:expert_count, :] = expert_router_ref[...]
+    logit_grad = (rows_ref[:, model_width:] * expert_slope_ref[...]).astype(low_type)
+    unit, scale = norm_parts(after_ref[...])
+    through, gain_feedforward_grad = norm_pull(
+        mm(logit_grad, expert_router[...]), unit, scale, gain_feedforward_ref[...]
+    )
+    after_grad[...] = cotangent_ref[...].astype(jnp.float32) + rows_ref[:, :model_width] + through
+    after_low[...] = after_grad[...].astype(low_type)
+    expert_column = wide + 2 * narrow + 128
+    low_part[:, expert_column:] = mm_tn(normed_ffn_ref[...], logit_grad).astype(low_type)
+    tile = 256
+
+    def output_tile(number, carry):
+        at = pl.ds(pl.multiple_of(number * tile, tile), tile)
+        output_part[at, :] = mm_tn(gated_ref[:, at], after_low[...]).astype(low_type)
+        return carry
+
+    lax.fori_loop(0, wide // tile, output_tile, 0)
+    hand_over(outputs)
+    result_event("sides", 3)
+    result_event("corner", 0)
+    loads[0].wait()
+
+    def gated_tile(number, carry):
+        at = pl.ds(pl.multiple_of(number * tile, tile), tile)
+        gated_grad[:, at] = mm_nt(after_low[...], output_ref[at, :]).astype(low_type)
+        return carry
+
+    lax.fori_loop(0, wide // tile, gated_tile, 0)
+    outputs.corner(3)
+    result_event("sides", 2)
+    outputs.corner(2)
+    outputs.corner(1)
+
+    lane = lax.broadcasted_iota(jnp.int32, (length, 128), 1)
+    gate_grads = jnp.zeros((length, 128), jnp.float32)
+    inverse = 1.0 / math.sqrt(HEAD)
+    for head in range(HEADS):
+        columns = slice(head * HEAD, (head + 1) * HEAD)
+        mixed = mixed_ref[:, columns]
+        mixed_grad = jnp.zeros((length, HEAD), jnp.float32)
+        for e in range(ATT_EXP):
+            at = head * ATT_EXP + e
+            part = gated_grad[:, at * HEAD : (at + 1) * HEAD].astype(jnp.float32)
+            lane_at = OUTPUT_LANE + at
+            mixed_grad = mixed_grad + gates_ref[:, lane_at : lane_at + 1] * part
+            gate_grads = jnp.where(
+                lane == lane_at, jnp.sum(part * mixed, axis=1, keepdims=True), gate_grads
+            )
+        mixed_grad = mixed_grad.astype(low_type)
+        probability = probability_ref[head]
+        prob_grad = mm_nt(mixed_grad, values_ref[:, columns])
+        inner = jnp.sum(probability * prob_grad, axis=-1, keepdims=True)
+        score_grad = (probability * (prob_grad - inner)).astype(low_type)
+        both_grad[:, columns] = (mm(score_grad, keys_ref[:, columns]) * inverse).astype(low_type)
+        both_grad[:, narrow + head * HEAD : narrow + (head + 1) * HEAD] = (
+            mm_tn(score_grad, queries_ref[:, columns]) * inverse
+        ).astype(low_type)
+        values_grad = mm_tn(probability.astype(low_type), mixed_grad)
+        values_grad = values_grad.astype(low_type).astype(jnp.float32)
+        for e in range(ATT_EXP):
+            at = head * ATT_EXP + e
+            wide_at = slice(at * HEAD, (at + 1) * HEAD)
+            projected_grad[:, wide_at] = (gates_ref[:, at : at + 1] * values_grad).astype(low_type)
+            gate_grad = jnp.sum(values_grad * projected_ref[:, wide_at], axis=1, keepdims=True)
+            gate_grads = jnp.where(lane == at, gate_grad, gate_grads)
+    router_grad = (gate_grads * slopes_ref[...]).astype(low_type)
+    result_event("sides", 1)
+    outputs.sides(3)
+    result_event("line", 3)
+    outputs.corner(0)
+
+    def value_tile(number, carry):
+        at = pl.ds(pl.multiple_of(number * tile, tile), tile)
+        to = pl.ds(pl.multiple_of(2 * narrow + number * tile, tile), tile)
+        low_part[:, to] = mm_tn(tokens_ref[...], projected_grad[:, at]).astype(low_type)
+        return carry
+
+    def both_tile(number, carry):
+        at = pl.ds(pl.multiple_of(number * tile, tile), tile)
+        low_part[:, at] = mm_tn(normed_ref[...], both_grad[:, at]).astype(low_type)
+        return carry
+
+    lax.fori_loop(0, wide // tile, value_tile, 0)
+    lax.fori_loop(0, 2 * narrow // tile, both_tile, 0)
+    loads[1].wait()
+    loads[2].wait()
+    normed_grad = mm_nt(both_grad[:, :narrow], query_ref[...])
+    normed_grad = normed_grad + mm_nt(both_grad[:, narrow:], key_ref[...])
+    normed_grad = normed_grad + mm(router_grad, routers[...])
+    unit, scale = norm_parts(tokens_ref[...].astype(jnp.float32))
+    through, gain_attention_grad = norm_pull(normed_grad, unit, scale, gain_attention_ref[...])
+    stream_out[...] = after_grad[...] + through
+    gain_columns = [
+        jnp.broadcast_to(grad, (128, model_width)).T
+        for grad in (gain_attention_grad, gain_feedforward_grad)
+    ]
+    small = mm_tn(normed_ref[...], router_grad)
+    small_lane = lax.broadcasted_iota(jnp.int32, (model_width, 128), 1)
+    small = jnp.where(small_lane == GAIN_LANE, gain_columns[0], small)
+    small = jnp.where(small_lane == GAIN_LANE + 1, gain_columns[1], small)
+    small_column = wide + 2 * narrow
+    low_part[:, small_column:expert_column] = small.astype(low_type)
+    hand_over(lows)
+    result_event("sides_last")
+    outputs.sides(2)
+    result_event("line", 2)
+    outputs.sides(1)
+    result_event("line", 1)
+    lows.corner(3)
+    outputs.line(3)
+    lows.corner(2)
+    result_event("last")
+    lows.corner(1)
+    outputs.sides_last()
+    lows.sides(3)
+    outputs.line(2)
+    lows.corner(0)
+    outputs.line(1)
+    lows.sides(2)
+    send_around(outputs, spread_outputs, output_own, own_sems.at[0])
+    loads[3].wait()
+    stream_out[...] += mm_nt(projected_grad[...], value_ref[...])
+    lows.sides(1)
+    spread_outputs.line(1)
+    lows.line(3)
+    spread_outputs.sides_first()
+    lows.sides_last()
+    spread_outputs.line(2)
+    lows.line(2)
+    spread_outputs.line(3)
+    lows.line(1)
+    spread_outputs.corner(0)
+    send_around(lows, spread_lows, low_own, own_sems.at[1])
+    for j in (1, 2, 3):
+        spread_outputs.sides(j)
+    spread_lows.line(1)
+    spread_lows.sides_first()
+    spread_lows.line(2)
+    for j in (1, 2, 3):
+        spread_outputs.corner(j)
+    spread_lows.line(3)
+    spread_lows.corner(0)
+    for j in (1, 2, 3):
+        spread_lows.sides(j)
+    for j in (1, 2, 3):
+        spread_lows.corner(j)
+
+    def arrived(k, carry):
+        spread_outputs.whole(k // 4, k % 4)
+        spread_lows.whole(k // 4, k % 4)
+        return carry
+
+    lax.fori_loop(0, 16, arrived, 0)
+    for reduce in (results, outputs, lows):
+        reduce.finish()
+    spread_outputs.finish()
+    spread_lows.finish()
+
+
+def call_backward(rows, tokens, cotangent, gains, routers, saved, weights, result):
+    length, model_width = tokens.shape
+    total = GRID[0] * GRID[1]
+    wide, narrow = weights[2].shape[1], weights[0].shape[1]
+    low_width = wide + 2 * narrow + 256
+    low_rows, output_rows = model_width // total, wide // total
+    low, full = jnp.bfloat16, jnp.float32
+    vmem = pl.BlockSpec(memory_space=pltpu.VMEM)
+    hbm = pl.BlockSpec(memory_space=pl.ANY)
+    sems = pltpu.SemaphoreType.DMA((2, N_SEM))
+    return pl.pallas_call(
+        backward_kernel,
+        out_shape=(
+            jax.ShapeDtypeStruct((length, model_width), low),
+            jax.ShapeDtypeStruct((length, model_width), full),
+            jax.ShapeDtypeStruct((model_width, low_width), low),
+            jax.ShapeDtypeStruct((wide, model_width), low),
+        ),
+        in_specs=[vmem] * 21 + [hbm] * 5,
+        out_specs=(vmem, vmem, hbm, hbm),
+        scratch_shapes=[
+            *(pltpu.VMEM(weight.shape, low) for weight in weights),
+            pltpu.VMEM((128, model_width), low),
+            pltpu.VMEM((128, model_width), low),
+            pltpu.VMEM((length, model_width), full),
+            pltpu.VMEM((length, model_width), low),
+            pltpu.VMEM((length, wide), low),
+            pltpu.VMEM((length, wide), low),
+            pltpu.VMEM((length, 2 * narrow), low),
+            pltpu.VMEM((HELD, length, model_width), low),
+            pltpu.VMEM((model_width, low_width), low),
+            pltpu.VMEM((wide, model_width), low),
+            pltpu.VMEM((low_rows, low_width), low),
+            pltpu.VMEM((output_rows, model_width), low),
+            pltpu.SemaphoreType.DMA((4,)),
+            pltpu.SemaphoreType.DMA((HELD,)),
+            pltpu.SemaphoreType.DMA((2,)),
+            *reduce_scratch(length, model_width),
+            sems,
+            *reduce_scratch(output_rows, model_width),
+            sems,
+            *reduce_scratch(low_rows, low_width),
+            sems,
+            sems,
+            sems,
+        ],
+        compiler_params=pltpu.CompilerParams(
+            collective_id=1, has_side_effects=True, vmem_limit_bytes=63 * 2**20
+        ),
+        name="backward",
+    )(rows, tokens, cotangent, *gains, *routers, *saved, *weights, result)
+
+
+def widen_kernel(low_ref, output_low_ref, query, key, value, output, small, expert):
+    full = jnp.float32
+    narrow, wide = query.shape[1], value.shape[1]
+    query[...] = low_ref[:, :narrow].astype(full)
+    key[...] = low_ref[:, narrow : 2 * narrow].astype(full)
+    value[...] = low_ref[:, 2 * narrow : 2 * narrow + wide].astype(full)
+    output[...] = output_low_ref[...].astype(full)
+    start = 2 * narrow + wide
+    small[...] = low_ref[:, start : start + 128].astype(full).T
+    expert[...] = low_ref[:, start + 128 :].astype(full).T
+
+
+def call_widen(low, output_low, narrow):
+    model_width, low_width = low.shape
+    wide = output_low.shape[0]
+    steps = model_width // 128
+    full = jnp.float32
+    rows = lambda height, width: pl.BlockSpec((height, width), lambda i: (i, 0))
+    columns = pl.BlockSpec((128, 128), lambda i: (0, i))
+    return pl.pallas_call(
+        widen_kernel,
+        grid=(steps,),
+        out_shape=(
+            jax.ShapeDtypeStruct((model_width, narrow), full),
+            jax.ShapeDtypeStruct((model_width, narrow), full),
+            jax.ShapeDtypeStruct((model_width, wide), full),
+            jax.ShapeDtypeStruct((wide, model_width), full),
+            jax.ShapeDtypeStruct((128, model_width), full),
+            jax.ShapeDtypeStruct((128, model_width), full),
+        ),
+        in_specs=[rows(128, low_width), rows(wide // steps, model_width)],
+        out_specs=(
+            rows(128, narrow),
+            rows(128, narrow),
+            rows(128, wide),
+            rows(wide // steps, model_width),
+            columns,
+            columns,
+        ),
+        compiler_params=pltpu.CompilerParams(vmem_limit_bytes=40 * 2**20),
+        name="widen",
+    )(low, output_low)
 
 
 def expert_kernel(
@@ -1197,137 +1639,7 @@
     return rows_sum, result, first_sum, second_sum.reshape(expert_second.shape)
 
 
-def sums_kernel(shapes, *refs):
-    count = len(shapes)
-    ins, refs = refs[:count], refs[count:]
-    first_out, outs, refs = refs[0], refs[1:count], refs[count:]
-    place = Place()
-    enter(place)
-    reduces, gathers, loads = [], [], []
-    for number, (rows, width) in enumerate(shapes):
-        held, refs = refs[0], refs[1:]
-        boxes, refs = refs[:8], refs[8:]
-        sems, load_sem, refs = refs[0], refs[1], refs[2:]
-
-        def source(k, core, rows=rows, ref=ins[number]):
-            start = (2 * place.chip(k // 4, k % 4) + core) * rows
-            return ref.at[pl.ds(pl.multiple_of(start, rows), rows)]
-
-        reduces.append(
-            Reduce(
-                place,
-                lambda k, held=held: held.at[k],
-                lambda k, source=source: source(k, 1 - place.core),
-                boxes,
-                sems,
-            )
-        )
-        loads.append(
-            lambda k, source=source, held=held, sem=load_sem: pltpu.make_async_copy(
-                source(k, place.core), held.at[k], sem.at[k]
-            )
-        )
-        if number:
-            buf, gather_sems, out_sem, refs = refs[0], refs[1], refs[2], refs[3:]
-            gathers.append((Gather(place, buf, rows, gather_sems), outs[number - 1], out_sem))
-
-    def begin(step, carry):
-        k = 15 - step
-        for reduce, load in zip(reduces, loads):
-            load(k).start()
-            reduce.copy("core", k).start()
-        return carry
-
-    lax.fori_loop(0, 16, begin, 0)
-
-    def arrive(k, carry):
-        for load in loads:
-            load(k).wait()
-        return carry
-
-    lax.fori_loop(0, 16, arrive, 0)
-    for kind, j in RETURN_ORDER:
-        for reduce in reduces:
-            getattr(reduce, kind)(*j)
-    for number in reversed(range(count)):
-        reduce = reduces[number]
-        mine = first_out if number == 0 else gathers[number - 1][0].block(0, 0)
-
-        def put(at, total, mine=mine):
-            mine[at, :] = total.astype(mine.dtype)
-
-        reduce.last(put)
-        if number == 0:
-            continue
-        gathers[number - 1][0].begin()
-
-    def pair_copy(number, q, j):
-        gather, out, sem = gathers[number]
-        rows = 2 * gather.rows
-        at = pl.ds(pl.multiple_of(place.chip(q, j) * rows, rows), rows)
-        return pltpu.make_async_copy(gather.buf.at[at], out.at[at], sem.at[4 * q + j])
-
-    def store(q, j):
-        for number in range(count - 1):
-            gathers[number][0].whole(q, j)
-            pair_copy(number, q, j).start()
-
-    for kind, j, blocks in SPREAD_ORDER:
-        for gather, _, _ in gathers:
-            getattr(gather, kind)(*j)
-        for block in blocks:
-            store(*block)
-
-    def drain(k, carry):
-        for number in range(count - 1):
-            pair_copy(number, k // 4, k % 4).wait()
-        return carry
-
-    lax.fori_loop(0, 16, drain, 0)
-    for reduce in reduces:
-        reduce.finish()
-    for gather, _, _ in gathers:
-        gather.finish()
-
-
-def call_sums(parts):
-    total = GRID[0] * GRID[1]
-    shapes = []
-    for part in parts:
-        shapes.append((part.shape[0] // total, part.shape[1]))
-    scratch = []
-    for number, (rows, width) in enumerate(shapes):
-        scratch += [
-            pltpu.VMEM((16, rows, width), jnp.bfloat16),
-            *reduce_scratch(rows, width),
-            pltpu.SemaphoreType.DMA((2, N_SEM)),
-            pltpu.SemaphoreType.DMA((16,)),
-        ]
-        if number:
-            scratch += [
-                pltpu.VMEM((total * rows, width), jnp.bfloat16),
-                pltpu.SemaphoreType.DMA((2, N_SEM)),
-                pltpu.SemaphoreType.DMA((16,)),
-            ]
-    hbm = pl.BlockSpec(memory_space=pl.ANY)
-    rows, width = shapes[0]
-    return pl.pallas_call(
-        functools.partial(sums_kernel, shapes),
-        out_shape=(
-            jax.ShapeDtypeStruct((rows, width), jnp.float32),
-            *(jax.ShapeDtypeStruct(part.shape, jnp.bfloat16) for part in parts[1:]),
-        ),
-        in_specs=[hbm] * len(parts),
-        out_specs=(pl.BlockSpec(memory_space=pltpu.VMEM), *([hbm] * (len(parts) - 1))),
-        scratch_shapes=scratch,
-        compiler_params=pltpu.CompilerParams(
-            collective_id=1, has_side_effects=True, vmem_limit_bytes=62 * 2**20
-        ),
-        name="sums",
-    )(*parts)
-
-
-def body(
+def general_body(
     tokens,
     cotangent,
     gain_attention,
@@ -1360,81 +1672,22 @@
     )
     stream = tokens.astype(jnp.float32)
     upstream = cotangent.astype(jnp.float32)
-    own_kernels = (lax.axis_size("dp"), lax.axis_size("expert")) == GRID
-    if own_kernels:
-        length, model_width = tokens.shape
-        gate_width = -(-expert_count // 128) * 128
-        (
-            upstream_rows,
-            packed,
-            after_attention,
-            normed_attention,
-            normed_low,
-            queries,
-            key_rows,
-            projected,
-            values,
-            probability,
-            mixed,
-            gated_rows,
-            value_gates,
-            value_slope,
-            output_gates,
-            output_slope,
-            expert_slope,
-        ) = call_attention(
-            tokens,
-            cotangent,
-            gain_attention,
-            gain_feedforward,
-            shared[1:],
-            expert_router,
-            segments,
-            value_ids[0],
-            output_ids[0],
-            ffn_ids[0],
-            gate_width,
-        )
-        by_head = (length, HEADS, HEAD)
-        by_expert = (length, HEADS, ATT_EXP)
-        saved_parts = (
-            normed_attention,
-            queries.reshape(by_head),
-            key_rows.reshape(by_head),
-            value_slope.reshape(by_expert),
-            output_slope.reshape(by_expert),
-            value_gates.reshape(by_expert),
-            output_gates.reshape(by_expert),
-            tokens,
-            projected.reshape(length, HEADS, ATT_EXP, HEAD),
-            values.reshape(by_head),
-            probability,
-            probability.astype(jnp.bfloat16),
-            mixed.reshape(by_head),
-            gated_rows,
-        )
-        rows_sum, result, first_sum, second_sum = call_experts(
-            packed, upstream_rows, expert_first, expert_second
-        )
-        token_grad = rows_sum[:, :model_width]
-        gate_back = rows_sum[:, model_width : model_width + expert_count]
-    else:
-        after_attention, saved_parts = attention_forward(
-            stream, segments[0], value_ids[0], output_ids[0], shared
-        )
-        normed_low = layer_norm(after_attention, gain_feedforward).astype(jnp.bfloat16)
-        logits = jnp.dot(normed_low, expert_router, preferred_element_type=jnp.float32)
-        sigmoid_out = jax.nn.sigmoid(logits)
-        dense_gates = sigmoid_out * expert_mask(ffn_ids[0], expert_count)
-        expert_slope = dense_gates * (1.0 - sigmoid_out)
-        result, token_grad, gate_back, first_sum, second_sum = expert_exchange(
-            after_attention.astype(jnp.bfloat16),
-            cotangent,
-            dense_gates.astype(jnp.bfloat16),
-            expert_first,
-            expert_second,
-            max(1, owner_total // 32),
-        )
+    after_attention, saved_parts = attention_forward(
+        stream, segments[0], value_ids[0], output_ids[0], shared
+    )
+    normed_low = layer_norm(after_attention, gain_feedforward).astype(jnp.bfloat16)
+    logits = jnp.dot(normed_low, expert_router, preferred_element_type=jnp.float32)
+    sigmoid_out = jax.nn.sigmoid(logits)
+    dense_gates = sigmoid_out * expert_mask(ffn_ids[0], expert_count)
+    expert_slope = dense_gates * (1.0 - sigmoid_out)
+    result, token_grad, gate_back, first_sum, second_sum = expert_exchange(
+        after_attention.astype(jnp.bfloat16),
+        cotangent,
+        dense_gates.astype(jnp.bfloat16),
+        expert_first,
+        expert_second,
+        max(1, owner_total // 32),
+    )
     logit_grad = (gate_back.astype(jnp.float32) * expert_slope).astype(jnp.bfloat16)
     router_sum = jnp.einsum("sa,sb->ab", normed_low, logit_grad, preferred_element_type=jnp.float32)
     normed_grad = jnp.einsum(
@@ -1458,10 +1711,7 @@
     low = jnp.concatenate([part.astype(jnp.bfloat16) for part in parts], axis=1)
     low = jnp.pad(low, ((0, 0), (0, -low.shape[1] % 256)))
     output_low = output_part.astype(jnp.bfloat16)
-    if own_kernels:
-        result, low, output_low = call_sums([result, low, output_low])
-    else:
-        low, output_low = lax.psum((low, output_low), BOTH)
+    low, output_low = lax.psum((low, output_low), BOTH)
     block_output = (after_attention + result.astype(jnp.float32)).astype(jnp.bfloat16)
     summed, start = [], 0
     for part in parts:
@@ -1486,6 +1736,75 @@
         first_sum,
         second_sum,
     )
+
+
+def kernel_body(
+    tokens,
+    cotangent,
+    gain_attention,
+    gain_feedforward,
+    query_weight,
+    key_weight,
+    value_weight,
+    output_weight,
+    value_router,
+    output_router,
+    expert_router,
+    expert_first,
+    expert_second,
+    segments,
+    value_ids,
+    output_ids,
+    ffn_ids,
+):
+    expert_count = expert_router.shape[1]
+    gate_width = -(-expert_count // 128) * 128
+    gains = (gain_attention[None], gain_feedforward[None])
+    weights = (query_weight, key_weight, value_weight, output_weight)
+    routers = (value_router.T, output_router.T, expert_router.T)
+    upstream_rows, packed, *saved = call_attention(
+        tokens,
+        cotangent,
+        gains,
+        weights,
+        routers,
+        segments,
+        value_ids[0],
+        output_ids[0],
+        ffn_ids[0],
+        gate_width,
+    )
+    rows_sum, result, first_sum, second_sum = call_experts(
+        packed, upstream_rows, expert_first, expert_second
+    )
+    block_output, stream_grad, low, output_low = call_backward(
+        rows_sum, tokens, cotangent, gains, routers, saved, weights, result
+    )
+    query_sum, key_sum, value_sum, output_sum, small, expert_small = call_widen(
+        low, output_low, query_weight.shape[1]
+    )
+    router_width = value_router.shape[1]
+    return (
+        block_output,
+        stream_grad,
+        small[GAIN_LANE],
+        small[GAIN_LANE + 1],
+        query_sum,
+        key_sum,
+        value_sum,
+        output_sum,
+        small[:router_width].T,
+        small[OUTPUT_LANE : OUTPUT_LANE + router_width].T,
+        expert_small[:expert_count].T,
+        first_sum,
+        second_sum,
+    )
+
+
+def body(*args):
+    if (lax.axis_size("dp"), lax.axis_size("expert")) == GRID:
+        return kernel_body(*args)
+    return general_body(*args)
 
 
 def solution(mesh):

time: 415 us -> 320 us (0.77)
  local copies, waits for them, and re-layouts: 52.6 us -> 13.5 us
  other arithmetic: 35.3 us -> 0 us
  matrix products: 29.4 us -> 0 us
  Pallas kernels: 295 us -> 304 us
    dot_general x18 -> x0, matrix products: 29.4 us -> none  [the longest x1 5.22 us: attention_backward(): jnp.einsum('sb,ab->sa', projected_grad, value_weight, preferred_element_t...]
    convert_element_type x9 -> x0, other arithmetic: 24.7 us -> none  [the longest x4 14.8 us: body(): summed.append(low[:, start:start + part.shape[1]].astype(jnp.float32))]
    pallas_call x1 -> x2, Pallas kernels: 144 us -> 159 us  [the longest x1 150 us: call_backward(): pl.pallas_call(backward_kernel, out_shape=(jax.ShapeDtypeStruct((length,...]
    concatenate x1 -> x0, local copies, waits for them, and re-layouts: 11.5 us -> none  [body(): low = jnp.concatenate([part.astype(jnp.bfloat16) for part in parts], axis=1)]
    reduce_sum x7 -> x0, other arithmetic: 7.84 us -> none  [the longest x2 2.22 us: layer_norm(): average = jnp.mean(stream, axis=-1, keepdims=True)]
    pad x1 -> x0, local copies, waits for them, and re-layouts: 7.01 us -> none  [body(): low = jnp.pad(low, ((0, 0), (0, -low.shape[1] % 256)))]
    convert_element_type x6 -> x0, local copies, waits for them, and re-layouts: 6.64 us -> none  [the longest x5 5.18 us: body(): low = jnp.concatenate([part.astype(jnp.bfloat16) for part in parts], axis=1)]
    pallas_call x1, Pallas kernels: 50 us -> 45.2 us  [call_attention(): pl.pallas_call(attention_kernel, out_shape=tuple((jax.ShapeDtypeStruct(*s...]
where the time goes in v4:
time: 320 us; the launch traced here: 318 us
  Pallas kernels  304 us (95%)
  local copies, waits for them, and re-layouts  13.5 us (4%)
    pallas_call x1, Pallas kernels, call_backward(): pl.pallas_call(backward_kernel, out_shape=(jax.ShapeDtypeStruct((length,...  150 us
    pallas_call x1, Pallas kernels, call_experts(): pl.pallas_call(functools.partial(expert_kernel, model_width, local_count)...  100 us
    pallas_call x1, Pallas kernels, call_attention(): pl.pallas_call(attention_kernel, out_shape=tuple((jax.ShapeDtypeStruct(*s...  45.2 us
    pallas_call x1, Pallas kernels, call_widen(): pl.pallas_call(widen_kernel, grid=(steps,), out_shape=(jax.ShapeDtypeStru...  8.54 us
    unnamed x13, local copies, waits for them, and re-layouts  8.37 us

profile of v4, /device:TPU:1, one launch (start us, length us, event | category | flops | bytes accessed | tf_op | source)
XLA Modules:
  0.0 318.3 jit_solution(10221033736745578624)
XLA Ops:
  0.6 45.2 %attention.1 = (bf16[4096,1024]{1,0:T(8,128)(2,1)}, bf16[128,1152]{1,0:T(8,128)(2,1)}, f32[128,1024]{1,0:T(8,128)}, bf16[128,1024]{1,0:T(8,128)(2,1)}, bf16[128,...) custom-call(bf16[128,1024]{1,0:T(8,128)(2,1)} %tokens_ref.3, ...), custom_call_target="tpu_custom_call" | custom-call | tf_op jit(solution)/shard_map/attention/pallas_call | solution.py:951
  45.8 100.0 %experts.1 = (f32[128,1152]{1,0:T(8,128)}, bf16[4096,1024]{1,0:T(8,128)(2,1)}, f32[384,1024]{1,0:T(8,128)}, f32[384,1024]{1,0:T(8,128)}) custom-call(bf16[128,1152]{1,0:T(8,128)(2,1)} %get-tuple-element.42.packed_ref, bf16[4096,1024]{1,0:T(8,128)(2,1)} %get-tuple-element.43.upstream_ref, bf16[3,1024,128]{2,1,0:T(8,128)(2,1)} %first_in.1, ...), custom_call_target="tpu_custom_call" | custom-call | tf_op jit(solution)/shard_map/experts/pallas_call | solution.py:1607
  145.9 150.4 %backward.1 = (bf16[128,1024]{1,0:T(8,128)(2,1)}, f32[128,1024]{1,0:T(8,128)}, bf16[1024,3840]{1,0:T(8,128)(2,1)}, bf16[2560,1024]{1,0:T(8,128)(2,1)}) custom-call(f32[128,1152]{1,0:T(8,128)} %get-tuple-element.44.rows_ref, bf16[128,1024]{1,0:T(8,128)(2,1)} %tokens_ref.3, bf16[128,1024]{1,0:T(8,128)(2,1)} %cotangent_ref.3, f32[1,1024]{1,0:T(1,128)} %bitcast.37, ...), custom_call_target="tpu_custom_call" | custom-call | tf_op jit(solution)/shard_map/backward/pallas_call | solution.py:1319
  296.3 3.0 copy.30
  299.3 0.0 copy-start
  299.3 3.2 %copy-done = bf16[1024,3840]{1,0:T(8,128)(2,1)S(1)} copy-done((bf16[1024,3840]{1,0:T(8,128)(2,1)S(1)}, bf16[1024,3840]{1,0:T(8,128)(2,1)}, u32[]{:S(2)}) %copy-start) | copy-done | bytes 7864344
  302.6 0.0 copy-start.1
  302.6 2.5 copy-done.1
  305.1 0.0 copy-start.4
  305.1 0.0 copy-start.3
  305.1 0.0 copy-start.2
  305.1 8.5 %widen.1 = (f32[1024,512]{1,0:T(8,128)}, f32[1024,512]{1,0:T(8,128)}, f32[1024,2560]{1,0:T(8,128)}, f32[2560,1024]{1,0:T(8,128)}, f32[128,1024]{1,0:T(8,128)S(1)}, /*index=5*/f32[128,1024]{1,0:T(8,128)S(1)}) custom-call(bf16[1024,3840]{1,0:T(8,128)(2,1)S(1)} %copy-done, bf16[2560,1024]{1,0:T(8,128)(2,1)S(1)} %copy-done.1), custom_call_target="tpu_custom_call" | custom-call | tf_op jit(solution)/shard_map/widen/pallas_call | solution.py:1381
  313.6 0.6 fusion
  314.2 0.7 slice_bitcast_fusion.1
  314.9 0.8 slice_bitcast_fusion
  315.7 0.0 copy-done.4
  315.7 0.7 copy.34
  316.4 0.0 copy-done.3
  316.4 0.8 copy.35
  317.2 0.0 copy-done.2
  317.2 1.1 copy.36
Async XLA Ops:
  299.3 3.2 %copy-start = (bf16[1024,3840]{1,0:T(8,128)(2,1)S(1)}, bf16[1024,3840]{1,0:T(8,128)(2,1)}, u32[]{:S(2)}) copy-start(bf16[1024,3840]{1,0:T(8,128)(2,1)} %get-tuple-element.61.low_ref) | copy-start | bytes 23592964
  302.6 2.5 copy-start.1
  305.1 10.6 %copy-start.4 = (bf16[128,1024]{1,0:T(8,128)(2,1)S(1)}, bf16[128,1024]{1,0:T(8,128)(2,1)}, u32[]{:S(2)}) copy-start(bf16[128,1024]{1,0:T(8,128)(2,1)} %get-tuple-element.88) | copy-start | bytes 786436
  305.1 11.3 %copy-start.3 = (f32[128,1024]{1,0:T(8,128)S(1)}, f32[128,1024]{1,0:T(8,128)}, u32[]{:S(2)}) copy-start(f32[128,1024]{1,0:T(8,128)} %get-tuple-element.89) | copy-start | bytes 1572868
  305.1 12.1 %copy-start.2 = (f32[384,1024]{1,0:T(8,128)S(1)}, f32[384,1024]{1,0:T(8,128)}, u32[]{:S(2)}) copy-start(f32[384,1024]{1,0:T(8,128)} %get-tuple-element.70) | copy-start | bytes 4718596

commit v5 on v4

--- a/solution.py
+++ b/solution.py
@@ -296,6 +296,7 @@
 MESH = pl.DeviceIdType.MESH
 GRID = (4, 8)
 N_SEM = 47
+VMEM_LIMIT = 63 * 2**20
 
 
 class Place:
@@ -354,7 +355,7 @@
     tiles = width // 128
     split = tiles // 2
     outer = max(1, tiles * 3 // 10)
-    return outer * 128, split * 128, (tiles - outer) * 128
+    return (outer + tiles % 2) * 128, split * 128, (tiles - outer) * 128
 
 
 class Gather:
@@ -754,228 +755,6 @@
     joined[...] = jnp.zeros_like(joined)
     joined[:count, :] = value_router_ref[...]
     joined[OUTPUT_LANE : OUTPUT_LANE + count, :] = output_router_ref[...]
-
-
-def attention_kernel(
-    tokens_ref,
-    cotangent_ref,
-    gain_attention_ref,
-    gain_feedforward_ref,
-    query_in,
-    key_in,
-    value_in,
-    output_in,
-    value_router_ref,
-    output_router_ref,
-    expert_router_ref,
-    segments_ref,
-    value_ids_ref,
-    output_ids_ref,
-    ffn_ids_ref,
-    upstream_out,
-    packed_out,
-    after_out,
-    normed_out,
-    normed_ffn_out,
-    queries_out,
-    keys_out,
-    projected_out,
-    values_out,
-    probability_out,
-    mixed_out,
-    gated_out,
-    gates_out,
-    slopes_out,
-    expert_slope_out,
-    query_ref,
-    key_ref,
-    value_ref,
-    output_ref,
-    routers,
-    all_ids,
-    own_sem,
-    weight_sems,
-    gather_sems,
-):
-    place = Place()
-    length, model_width = tokens_ref.shape
-    expert_count = expert_router_ref.shape[0]
-    loads = [
-        pltpu.make_async_copy(src, dst, weight_sems.at[number])
-        for number, (src, dst) in enumerate(
-            (
-                (query_in, query_ref),
-                (key_in, key_ref),
-                (value_in, value_ref),
-                (output_in, output_ref),
-            )
-        )
-    ]
-    gather = Gather(place, upstream_out, length, gather_sems)
-    own_copy = pltpu.make_async_copy(cotangent_ref, gather.block(0, 0), own_sem)
-    own_copy.start()
-    for load in loads:
-        load.start()
-    enter(place)
-    own_copy.wait()
-    gather.begin()
-
-    join_routers(routers, value_router_ref, output_router_ref)
-    top = value_ids_ref.shape[1]
-    all_ids[...] = jnp.zeros_like(all_ids)
-    for head in range(HEADS):
-        at = head * top
-        all_ids[at : at + top, :] = value_ids_ref[head].astype(jnp.float32) + float(head * ATT_EXP)
-        all_ids[16 + at : 16 + at + top, :] = output_ids_ref[head].astype(jnp.float32) + float(
-            OUTPUT_LANE + head * ATT_EXP
-        )
-    ffn_top = ffn_ids_ref.shape[0]
-    all_ids[32 : 32 + ffn_top, :] = ffn_ids_ref[...].astype(jnp.float32)
-    ids = all_ids[...].T
-    lane = lax.broadcasted_iota(jnp.int32, (length, gates_out.shape[1]), 1).astype(jnp.float32)
-
-    def named(columns):
-        mask = jnp.zeros(lane.shape, jnp.float32)
-        for at in columns:
-            mask = jnp.where(lane == ids[:, at : at + 1], 1.0, mask)
-        return mask
-
-    stream_low = tokens_ref[...]
-    stream = stream_low.astype(jnp.float32)
-    unit, _ = norm_parts(stream)
-    normed = (unit * gain_attention_ref[...]).astype(jnp.bfloat16)
-    normed_out[...] = normed
-    sig = jax.nn.sigmoid(mm_nt(normed, routers[...]))
-    gates = named([*range(HEADS * top), *range(16, 16 + HEADS * top)]) * sig
-    gates_out[...] = gates
-    slopes_out[...] = gates * (1.0 - sig)
-    loads[0].wait()
-    queries_out[...] = mm(normed, query_ref[...]).astype(jnp.bfloat16)
-    loads[1].wait()
-    keys_out[...] = mm(normed, key_ref[...]).astype(jnp.bfloat16)
-    gather.line(1)
-    gather.sides_first()
-    gather.line(2)
-    loads[2].wait()
-    head_width = ATT_EXP * HEAD
-    for head in range(HEADS):
-        columns = slice(head * head_width, (head + 1) * head_width)
-        projected_out[:, columns] = mm(stream_low, value_ref[:, columns])
-        total = jnp.zeros((length, HEAD), jnp.float32)
-        for e in range(ATT_EXP):
-            at = head * ATT_EXP + e
-            total = total + gates[:, at : at + 1] * projected_out[:, at * HEAD : (at + 1) * HEAD]
-        values_out[:, head * HEAD : (head + 1) * HEAD] = total.astype(jnp.bfloat16)
-    gather.line(3)
-    documents = jnp.broadcast_to(segments_ref[...].astype(jnp.float32), (length, length))
-    row = lax.broadcasted_iota(jnp.int32, (length, length), 0)
-    column = lax.broadcasted_iota(jnp.int32, (length, length), 1)
-    allowed = (documents == documents.T) & (row >= column)
-    for head in range(HEADS):
-        columns = slice(head * HEAD, (head + 1) * HEAD)
-        scores = mm_nt(queries_out[:, columns], keys_out[:, columns]) * (1.0 / math.sqrt(HEAD))
-        scores = jnp.where(allowed, scores, NEG_FILL)
-        exponent = jnp.exp(scores - jnp.max(scores, axis=-1, keepdims=True))
-        probability = exponent / jnp.sum(exponent, axis=-1, keepdims=True)
-        probability_out[head] = probability
-        mixed = mm(probability.astype(jnp.bfloat16), values_out[:, columns])
-        mixed_out[:, columns] = mixed
-        for e in range(ATT_EXP):
-            at = head * ATT_EXP + e
-            gate = gates[:, OUTPUT_LANE + at : OUTPUT_LANE + at + 1]
-            gated_out[:, at * HEAD : (at + 1) * HEAD] = (gate * mixed).astype(jnp.bfloat16)
-    gather.corner(0)
-    loads[3].wait()
-    after = stream + mm(gated_out[...], output_ref[...])
-    after_out[...] = after
-    packed_out[:, :model_width] = after.astype(jnp.bfloat16)
-    unit, _ = norm_parts(after)
-    normed_ffn = (unit * gain_feedforward_ref[...]).astype(jnp.bfloat16)
-    normed_ffn_out[...] = normed_ffn
-    expert_sig = jax.nn.sigmoid(mm_nt(normed_ffn, expert_router_ref[...]))
-    expert_gates = named(range(32, 32 + ffn_top))[:, :expert_count] * expert_sig
-    gate_width = packed_out.shape[1] - model_width
-    packed_out[:, model_width:] = jnp.zeros((length, gate_width), jnp.bfloat16)
-    packed_out[:, model_width : model_width + expert_count] = expert_gates.astype(jnp.bfloat16)
-    expert_slope_out[...] = jnp.zeros((length, gate_width), jnp.float32)
-    expert_slope_out[:, :expert_count] = expert_gates * (1.0 - expert_sig)
-    for j in (1, 2, 3):
-        gather.sides(j)
-    for j in (1, 2, 3):
-        gather.corner(j)
-
-    def arrived(k, carry):
-        gather.whole(k // 4, k % 4)
-        return carry
-
-    lax.fori_loop(0, 16, arrived, 0)
-    gather.finish()
-
-
-def call_attention(
-    tokens,
-    cotangent,
-    gains,
-    weights,
-    routers,
-    segments,
-    value_ids,
-    output_ids,
-    ffn_ids,
-    gate_width,
-):
-    length, model_width = tokens.shape
-    total = GRID[0] * GRID[1] * length
-    wide = weights[3].shape[0]
-    narrow = HEADS * HEAD
-    low, full = jnp.bfloat16, jnp.float32
-    shapes = (
-        ((total, model_width), low),
-        ((length, model_width + gate_width), low),
-        ((length, model_width), full),
-        ((length, model_width), low),
-        ((length, model_width), low),
-        ((length, narrow), low),
-        ((length, narrow), low),
-        ((length, wide), full),
-        ((length, narrow), low),
-        ((HEADS, length, length), full),
-        ((length, narrow), full),
-        ((length, wide), low),
-        ((length, 128), full),
-        ((length, 128), full),
-        ((length, gate_width), full),
-    )
-    vmem = pl.BlockSpec(memory_space=pltpu.VMEM)
-    hbm = pl.BlockSpec(memory_space=pl.ANY)
-    return pl.pallas_call(
-        attention_kernel,
-        out_shape=tuple(jax.ShapeDtypeStruct(*shape) for shape in shapes),
-        in_specs=[vmem] * 4 + [hbm] * 4 + [vmem] * 7,
-        out_specs=(hbm, *([vmem] * (len(shapes) - 1))),
-        scratch_shapes=[
-            *(pltpu.VMEM(weight.shape, low) for weight in weights),
-            pltpu.VMEM((128, model_width), low),
-            pltpu.VMEM((128, length), full),
-            pltpu.SemaphoreType.DMA,
-            pltpu.SemaphoreType.DMA((4,)),
-            pltpu.SemaphoreType.DMA((2, N_SEM)),
-        ],
-        compiler_params=pltpu.CompilerParams(
-            collective_id=2, has_side_effects=True, vmem_limit_bytes=62 * 2**20
-        ),
-        name="attention",
-    )(
-        tokens,
-        cotangent,
-        *gains,
-        *weights,
-        *routers,
-        segments,
-        value_ids.transpose(1, 2, 0),
-        output_ids.transpose(1, 2, 0),
-        ffn_ids.T,
-    )
 
 
 HELD = 6
@@ -1353,13 +1132,33 @@
             sems,
         ],
         compiler_params=pltpu.CompilerParams(
-            collective_id=1, has_side_effects=True, vmem_limit_bytes=63 * 2**20
+            collective_id=1, has_side_effects=True, vmem_limit_bytes=VMEM_LIMIT
         ),
         name="backward",
     )(rows, tokens, cotangent, *gains, *routers, *saved, *weights, result)
 
 
-def widen_kernel(low_ref, output_low_ref, query, key, value, output, small, expert):
+def widen_kernel(
+    low_ref,
+    output_low_ref,
+    first_ref,
+    second_ref,
+    block_ref,
+    stream_ref,
+    query,
+    key,
+    value,
+    output,
+    value_router,
+    output_router,
+    expert_router,
+    gain_attention,
+    gain_feedforward,
+    first,
+    second,
+    block,
+    stream,
+):
     full = jnp.float32
     narrow, wide = query.shape[1], value.shape[1]
     query[...] = low_ref[:, :narrow].astype(full)
@@ -1367,94 +1166,368 @@
     value[...] = low_ref[:, 2 * narrow : 2 * narrow + wide].astype(full)
     output[...] = output_low_ref[...].astype(full)
     start = 2 * narrow + wide
-    small[...] = low_ref[:, start : start + 128].astype(full).T
-    expert[...] = low_ref[:, start + 128 :].astype(full).T
-
-
-def call_widen(low, output_low, narrow):
+    small = low_ref[:, start : start + 128].astype(full).T
+    count = value_router.shape[0]
+    value_router[...] = small[:count]
+    output_router[...] = small[OUTPUT_LANE : OUTPUT_LANE + count]
+    gain_attention[...] = small[GAIN_LANE : GAIN_LANE + 1]
+    gain_feedforward[...] = small[GAIN_LANE + 1 : GAIN_LANE + 2]
+    expert_router[...] = low_ref[:, start + 128 :].astype(full).T[: expert_router.shape[0]]
+    hidden_width = second.shape[1]
+    for e in range(first.shape[0]):
+        rows = slice(e * hidden_width, (e + 1) * hidden_width)
+        first[e] = first_ref[rows, :].T
+        second[e] = second_ref[rows, :]
+    block[...] = block_ref[...]
+    stream[...] = stream_ref[...]
+
+
+def call_widen(low, output_low, first_sum, second_sum, block_output, stream_grad, narrow, expert_count, local_count):
     model_width, low_width = low.shape
     wide = output_low.shape[0]
+    hidden = first_sum.shape[0]
+    hidden_width = hidden // local_count
+    length = block_output.shape[0]
     steps = model_width // 128
     full = jnp.float32
+    router_width = HEADS * ATT_EXP
     rows = lambda height, width: pl.BlockSpec((height, width), lambda i: (i, 0))
-    columns = pl.BlockSpec((128, 128), lambda i: (0, i))
+    columns = lambda height: pl.BlockSpec((height, 128), lambda i: (0, i))
+    first_spec = pl.BlockSpec((local_count, 128, hidden_width), lambda i: (0, i, 0))
+    second_spec = pl.BlockSpec((local_count, hidden_width, 128), lambda i: (0, 0, i))
+    shape = lambda *dims, kind=full: jax.ShapeDtypeStruct(dims, kind)
     return pl.pallas_call(
         widen_kernel,
         grid=(steps,),
         out_shape=(
-            jax.ShapeDtypeStruct((model_width, narrow), full),
-            jax.ShapeDtypeStruct((model_width, narrow), full),
-            jax.ShapeDtypeStruct((model_width, wide), full),
-            jax.ShapeDtypeStruct((wide, model_width), full),
-            jax.ShapeDtypeStruct((128, model_width), full),
-            jax.ShapeDtypeStruct((128, model_width), full),
+            shape(model_width, narrow),
+            shape(model_width, narrow),
+            shape(model_width, wide),
+            shape(wide, model_width),
+            shape(router_width, model_width),
+            shape(router_width, model_width),
+            shape(expert_count, model_width),
+            shape(1, model_width),
+            shape(1, model_width),
+            shape(local_count, model_width, hidden_width),
+            shape(local_count, hidden_width, model_width),
+            shape(length, model_width, kind=block_output.dtype),
+            shape(length, model_width),
         ),
-        in_specs=[rows(128, low_width), rows(wide // steps, model_width)],
+        in_specs=[
+            rows(128, low_width),
+            rows(wide // steps, model_width),
+            columns(hidden),
+            columns(hidden),
+            rows(length // steps, model_width),
+            rows(length // steps, model_width),
+        ],
         out_specs=(
             rows(128, narrow),
             rows(128, narrow),
             rows(128, wide),
             rows(wide // steps, model_width),
-            columns,
-            columns,
+            columns(router_width),
+            columns(router_width),
+            columns(expert_count),
+            columns(1),
+            columns(1),
+            first_spec,
+            second_spec,
+            rows(length // steps, model_width),
+            rows(length // steps, model_width),
         ),
-        compiler_params=pltpu.CompilerParams(vmem_limit_bytes=40 * 2**20),
+        compiler_params=pltpu.CompilerParams(vmem_limit_bytes=VMEM_LIMIT),
         name="widen",
-    )(low, output_low)
-
-
-def expert_kernel(
-    model_width,
+    )(low, output_low, first_sum, second_sum, block_output, stream_grad)
+
+
+def run_events(events, sources):
+    for name, method, arguments, where in events:
+        action = functools.partial(getattr(sources[name], method), *arguments)
+        if where == "all":
+            action()
+        else:
+            pl.when(sources["place"].middle == (1 if where == "middle" else 0))(action)
+
+
+def ev(name, method, *arguments, where="all"):
+    return (name, method, arguments, where)
+
+
+AFTER_ATTENTION = (
+    ev("u", "line", 2, where="end"),
+    ev("u", "line", 3, where="middle"),
+    ev("u", "corner", 0),
+    ev("u", "sides", 1),
+)
+WALK = (
+    (0, 0, ()),
+    (
+        0,
+        1,
+        (
+            ev("u", "line", 3, where="end"),
+            ev("u", "sides", 2),
+            ev("u", "corner", 1),
+            ev("x", "line", 1),
+            ev("x", "sides_first"),
+            ev("x", "line", 2, where="middle"),
+        ),
+    ),
+    (1, 0, ()),
+    (2, 0, ()),
+    (
+        3,
+        0,
+        (
+            ev("x", "corner", 0),
+            ev("x", "line", 2, where="end"),
+            ev("x", "line", 3, where="middle"),
+            ev("u", "sides", 3),
+            ev("u", "corner", 2),
+        ),
+    ),
+    (0, 2, (ev("u", "corner", 3),)),
+    (0, 3, (ev("x", "line", 3, where="end"), ev("x", "sides", 1))),
+    (1, 1, ()),
+    (2, 1, (ev("r", "corner", 0),)),
+    (3, 1, (ev("x", "corner", 1), ev("x", "sides", 2))),
+    (1, 2, ()),
+    (2, 2, (ev("r", "corner", 1),)),
+    (3, 2, (ev("x", "corner", 2), ev("x", "sides", 3))),
+    (1, 3, ()),
+    (2, 3, (ev("r", "corner", 2),)),
+    (3, 3, (ev("x", "corner", 3),)),
+)
+GIVE_BACK = (
+    (ev("r", "corner", 3),),
+    (ev("r", "sides", 3),),
+    (ev("r", "sides", 2),),
+    (ev("r", "sides", 1),),
+    (ev("r", "line", 3),),
+    (ev("r", "sides_last"),),
+    (ev("r", "line", 2),),
+    (ev("r", "line", 1),),
+)
+
+
+def layer_kernel(
     local_count,
-    packed_ref,
-    upstream_ref,
+    tokens_ref,
+    cotangent_ref,
+    gain_attention_ref,
+    gain_feedforward_ref,
+    value_router_ref,
+    output_router_ref,
+    expert_router_ref,
+    segments_ref,
+    value_ids_ref,
+    output_ids_ref,
+    ffn_ids_ref,
     first_in,
-    second_in,
+    second_ref,
+    query_in,
+    key_in,
+    value_in,
+    output_in,
     rows_out,
-    result_out,
     first_out,
     second_out,
+    after_out,
+    normed_out,
+    normed_ffn_out,
+    queries_out,
+    keys_out,
+    projected_out,
+    values_out,
+    probability_out,
+    mixed_out,
+    gated_out,
+    gates_out,
+    slopes_out,
+    expert_slope_out,
+    result_out,
+    routers,
+    all_ids,
     gathered,
     upstream,
     first_ref,
     first_t_ref,
     second_t_ref,
-    gated_hidden,
-    pre_grads,
+    hidden_parts,
     partial,
-    *refs,
+    result_stage,
+    weight_sems,
+    upstream_sems,
+    gather_sems,
+    reduce_sems,
+    result_sems,
+    *boxes,
 ):
     place = Place()
-    length = packed_ref.shape[0]
+    length, model_width = tokens_ref.shape
     pair = 2 * length
-    gate_width = packed_ref.shape[1] - model_width
+    expert_count = expert_router_ref.shape[0]
+    width = gathered.shape[1]
+    gate_width = width - model_width
     hidden_width = first_ref.shape[1] // local_count
-    boxes, (result_stage, gather_sems, reduce_sems, result_sems, upstream_sem) = refs[:8], refs[8:]
-    upstream_copy = pltpu.make_async_copy(upstream_ref, upstream, upstream_sem)
-    upstream_copy.start()
+    narrow, wide = query_in.shape[1], value_in.shape[1]
+    mine = pl.ds(pl.multiple_of(place.me * length, length), length)
+
+    pieces = [
+        (start, min(wide, start + width), number)
+        for number, start in enumerate(range(0, wide, width), 1)
+    ]
+    value_refs = [
+        partial.at[number * model_width : (number + 1) * model_width, : end - start]
+        for start, end, number in pieces
+    ]
+    query_ref = partial.at[:model_width, :narrow]
+    key_ref = partial.at[:model_width, narrow : 2 * narrow]
+    hidden = first_ref.shape[1]
+    gated_hidden = hidden_parts.at[:, :hidden]
+    pre_grads = hidden_parts.at[:, hidden:]
+    main_columns, side_columns = 2 * hidden, model_width - 2 * hidden
+    last_rows = len(pieces) * model_width
+    output_parts = [
+        (0, wide, slice(0, main_columns), hidden_parts.at[:wide, :])
+    ]
+    for number, start in enumerate(range(0, wide, model_width), 1):
+        end = min(wide, start + model_width)
+        place_at = slice(number * side_columns, (number + 1) * side_columns)
+        ref = partial.at[last_rows : last_rows + end - start, place_at]
+        output_parts.append((start, end, slice(main_columns, None), ref))
+    loads = [
+        pltpu.make_async_copy(src, dst, weight_sems.at[number])
+        for number, (src, dst) in enumerate(
+            [
+                (query_in, query_ref),
+                (key_in, key_ref),
+                *(
+                    (value_in.at[:, start:end], ref)
+                    for (start, end, _), ref in zip(pieces, value_refs)
+                ),
+                *(
+                    (output_in.at[start:end, columns], ref)
+                    for start, end, columns, ref in output_parts
+                ),
+            ]
+        )
+    ]
+    for load in loads:
+        load.start()
+    upstream[mine, :] = cotangent_ref[...]
     enter(place)
+    gather_upstream = Gather(place, upstream, length, upstream_sems)
+    gather_upstream.begin()
+
+    join_routers(routers, value_router_ref, output_router_ref)
+    top = value_ids_ref.shape[1]
+    all_ids[...] = jnp.zeros_like(all_ids)
+    for head in range(HEADS):
+        at = head * top
+        all_ids[at : at + top, :] = value_ids_ref[head].astype(jnp.float32) + float(head * ATT_EXP)
+        all_ids[16 + at : 16 + at + top, :] = output_ids_ref[head].astype(jnp.float32) + float(
+            OUTPUT_LANE + head * ATT_EXP
+        )
+    ffn_top = ffn_ids_ref.shape[0]
+    all_ids[32 : 32 + ffn_top, :] = ffn_ids_ref[...].astype(jnp.float32)
+    ids = all_ids[...].T
+    lane = lax.broadcasted_iota(jnp.int32, (length, gates_out.shape[1]), 1).astype(jnp.float32)
+
+    def named(columns):
+        mask = jnp.zeros(lane.shape, jnp.float32)
+        for at in columns:
+            mask = jnp.where(lane == ids[:, at : at + 1], 1.0, mask)
+        return mask
+
+    stream_low = tokens_ref[...]
+    stream = stream_low.astype(jnp.float32)
+    unit, _ = norm_parts(stream)
+    normed = (unit * gain_attention_ref[...]).astype(jnp.bfloat16)
+    normed_out[...] = normed
+    sig = jax.nn.sigmoid(mm_nt(normed, routers[...]))
+    gates = named([*range(HEADS * top), *range(16, 16 + HEADS * top)]) * sig
+    gates_out[...] = gates
+    slopes_out[...] = gates * (1.0 - sig)
+    loads[0].wait()
+    queries_out[...] = mm(normed, query_ref[...]).astype(jnp.bfloat16)
+    loads[1].wait()
+    keys_out[...] = mm(normed, key_ref[...]).astype(jnp.bfloat16)
+    for (start, end, _), ref, load in zip(pieces, value_refs, loads[2:]):
+        load.wait()
+        projected_out[:, start:end] = mm(stream_low, ref[...])
+    for head in range(HEADS):
+        total = jnp.zeros((length, HEAD), jnp.float32)
+        for e in range(ATT_EXP):
+            at = head * ATT_EXP + e
+            total = total + gates[:, at : at + 1] * projected_out[:, at * HEAD : (at + 1) * HEAD]
+        values_out[:, head * HEAD : (head + 1) * HEAD] = total.astype(jnp.bfloat16)
+    documents = jnp.broadcast_to(segments_ref[...].astype(jnp.float32), (length, length))
+    row = lax.broadcasted_iota(jnp.int32, (length, length), 0)
+    column = lax.broadcasted_iota(jnp.int32, (length, length), 1)
+    allowed = (documents == documents.T) & (row >= column)
+    for head in range(HEADS):
+        columns = slice(head * HEAD, (head + 1) * HEAD)
+        scores = mm_nt(queries_out[:, columns], keys_out[:, columns]) * (1.0 / math.sqrt(HEAD))
+        scores = jnp.where(allowed, scores, NEG_FILL)
+        exponent = jnp.exp(scores - jnp.max(scores, axis=-1, keepdims=True))
+        probability = exponent / jnp.sum(exponent, axis=-1, keepdims=True)
+        probability_out[head] = probability
+        mixed = mm(probability.astype(jnp.bfloat16), values_out[:, columns])
+        mixed_out[:, columns] = mixed
+        for e in range(ATT_EXP):
+            at = head * ATT_EXP + e
+            gate = gates[:, OUTPUT_LANE + at : OUTPUT_LANE + at + 1]
+            gated_out[:, at * HEAD : (at + 1) * HEAD] = (gate * mixed).astype(jnp.bfloat16)
+    gather_upstream.line(1)
+    gather_upstream.sides_first()
+    place.if_middle(lambda: gather_upstream.line(2))
+    side = stream[:, main_columns:]
+    for (start, end, columns, ref), load in zip(output_parts, loads[2 + len(pieces) :]):
+        load.wait()
+        if start == 0 and end == wide:
+            after_out[:, columns] = stream[:, columns] + mm(gated_out[...], ref[...])
+        else:
+            side = side + mm(gated_out[:, start:end], ref[...])
+    after_out[:, main_columns:] = side
+    after = after_out[...]
+    gathered[mine, :model_width] = after.astype(jnp.bfloat16)
+    unit, _ = norm_parts(after)
+    normed_ffn = (unit * gain_feedforward_ref[...]).astype(jnp.bfloat16)
+    normed_ffn_out[...] = normed_ffn
+    expert_sig = jax.nn.sigmoid(mm_nt(normed_ffn, expert_router_ref[...]))
+    expert_gates = named(range(32, 32 + ffn_top))[:, :expert_count] * expert_sig
+    gathered[mine, model_width:] = jnp.zeros((length, gate_width), jnp.bfloat16)
+    gathered[mine, model_width : model_width + expert_count] = expert_gates.astype(jnp.bfloat16)
+    expert_slope_out[...] = jnp.zeros((length, gate_width), jnp.float32)
+    expert_slope_out[:, :expert_count] = expert_gates * (1.0 - expert_sig)
     gather = Gather(place, gathered, length, gather_sems)
-    gathered[pl.ds(pl.multiple_of(place.me * length, length), length), :] = packed_ref[...]
     gather.begin()
-    second_ref = second_in
+
     for e in range(local_count):
         columns = slice(e * hidden_width, (e + 1) * hidden_width)
         first_ref[:, columns] = first_in[e]
         first_t_ref[columns, :] = first_in[e].astype(jnp.float32).T.astype(jnp.bfloat16)
-        second_t_ref[:, columns] = second_in[columns, :].astype(jnp.float32).T.astype(jnp.bfloat16)
+        second_t_ref[:, columns] = second_ref[columns, :].astype(jnp.float32).T.astype(jnp.bfloat16)
     pick_row = lax.broadcasted_iota(jnp.int32, (gate_width, first_ref.shape[1]), 0)
     pick_column = lax.broadcasted_iota(jnp.int32, (gate_width, first_ref.shape[1]), 1)
     pick_gates = jnp.where(
         pick_row == place.me * local_count + pick_column // hidden_width, 1.0, 0.0
     ).astype(jnp.bfloat16)
 
-    def own(k):
-        return partial.at[k, pl.ds(pl.multiple_of(place.core * length, length), length)]
-
-    def other(k):
-        return partial.at[k, pl.ds(pl.multiple_of((1 - place.core) * length, length), length)]
-
-    reduce = Reduce(place, own, other, boxes, reduce_sems)
+    def share(k, core):
+        return partial.at[pl.ds(pl.multiple_of(k * pair + core * length, length), length)]
+
+    reduce = Reduce(
+        place,
+        lambda k: share(k, place.core),
+        lambda k: share(k, 1 - place.core),
+        boxes,
+        reduce_sems,
+    )
+    sources = {"place": place, "u": gather_upstream, "x": gather, "r": reduce}
 
     def result_copy(slot, chip):
         return pltpu.make_async_copy(
@@ -1481,7 +1554,8 @@
         gated_hidden[rows, :] = gated
         pre_grads[rows, :] = pre_grad
         k = 4 * q + j
-        partial[k, :, :model_width] = mm(pre_grad, first_t_ref[...]).astype(jnp.bfloat16)
+        to = pl.ds(pl.multiple_of(k * pair, pair), pair)
+        partial[to, :model_width] = mm(pre_grad, first_t_ref[...]).astype(jnp.bfloat16)
         product = hidden * back
         column = lax.broadcasted_iota(jnp.int32, (pair, gate_width), 1) - place.me * local_count
         gate_grad = jnp.zeros((pair, gate_width), jnp.float32)
@@ -1490,7 +1564,7 @@
                 product[:, e * hidden_width : (e + 1) * hidden_width], axis=1, keepdims=True
             )
             gate_grad = jnp.where(column == e, own_sum, gate_grad)
-        partial[k, :, model_width:] = gate_grad.astype(jnp.bfloat16)
+        partial[to, model_width:] = gate_grad.astype(jnp.bfloat16)
         reduce.copy("core", k).start()
         slot = step % 2
 
@@ -1501,29 +1575,7 @@
         result_stage[slot] = mm(gated, second_ref[...]).astype(jnp.bfloat16)
         result_copy(slot, chip).start()
 
-    upstream_copy.wait()
-
-    def arrive(actions):
-        for kind, j in actions:
-            if kind == "sides_first":
-                gather.sides_first()
-            elif kind == "line_middle":
-                place.if_middle(lambda: gather.line(j))
-            elif kind == "line_end":
-                pl.when(place.middle == 0)(lambda: gather.line(j))
-            else:
-                getattr(gather, kind)(j)
-
-    before = {
-        1: [("line", 1), ("sides_first", 0), ("line_middle", 2)],
-        4: [("corner", 0), ("line_end", 2), ("line_middle", 3)],
-        6: [("line_end", 3), ("sides", 1)],
-        9: [("corner", 1), ("sides", 2)],
-        12: [("corner", 2), ("sides", 3)],
-        15: [("corner", 3)],
-    }
-    order = [(0, 0), (0, 1), (1, 0), (2, 0), (3, 0), (0, 2), (0, 3), (1, 1)]
-    order += [(2, 1), (3, 1), (1, 2), (2, 2), (3, 2), (1, 3), (2, 3), (3, 3)]
+    run_events(AFTER_ATTENTION, sources)
 
     def pick(step, values):
         total = 0
@@ -1532,16 +1584,18 @@
         return total
 
     def walk(step, carry):
-        for number, actions in before.items():
-            pl.when(step == number)(functools.partial(arrive, actions))
-        q = pick(step, [pair_[0] for pair_ in order])
-        j = pick(step, [pair_[1] for pair_ in order])
+        for number, (_, _, events) in enumerate(WALK):
+            if events:
+                pl.when(step == number)(functools.partial(run_events, events, sources))
+        q = pick(step, [stop[0] for stop in WALK])
+        j = pick(step, [stop[1] for stop in WALK])
         gather.whole(q, j)
+        gather_upstream.whole(q, j)
         compute(step, q, j)
         return carry
 
     lax.fori_loop(0, 16, walk, 0)
-    piece = gathered.shape[0] // 8
+    piece = gathered.shape[0] // len(GIVE_BACK)
 
     def weight_piece(number):
         rows = pl.ds(pl.multiple_of(number * piece, piece), piece)
@@ -1558,33 +1612,13 @@
             second_out[...] += second
             first_out[...] += first
 
-    give_back = [
-        [("corner", 3), ("corner", 2)],
-        [("corner", 1), ("sides", 3)],
-        [("corner", 0)],
-        [("sides", 2)],
-        [("sides", 1)],
-        [("line", 3)],
-        [("sides_last", 0)],
-        [("line", 2)],
-    ]
-
     def give(step, carry):
-        for number, actions in enumerate(give_back):
-
-            @pl.when(step == number)
-            def _(actions=actions):
-                for kind, j in actions:
-                    if kind == "sides_last":
-                        reduce.sides_last()
-                    else:
-                        getattr(reduce, kind)(j)
-
+        for number, events in enumerate(GIVE_BACK):
+            pl.when(step == number)(functools.partial(run_events, events, sources))
         weight_piece(step)
         return carry
 
-    lax.fori_loop(0, len(give_back), give, 0)
-    reduce.line(1)
+    lax.fori_loop(0, len(GIVE_BACK), give, 0)
 
     def put(at, total):
         rows_out[at, :] = total
@@ -1592,51 +1626,96 @@
     reduce.last(put)
     for slot in range(2):
         result_copy(slot, 0).wait()
+    gather_upstream.finish()
     gather.finish()
     reduce.finish()
 
 
-def call_experts(packed, upstream, expert_first, expert_second):
-    local_count, model_width, hidden_width = expert_first.shape
-    wide = local_count * hidden_width
-    length, width = packed.shape
-    total = upstream.shape[0]
+def call_layer(
+    tokens,
+    cotangent,
+    gains,
+    weights,
+    routers,
+    segments,
+    value_ids,
+    output_ids,
+    ffn_ids,
+    expert_first,
+    expert_second,
+):
+    length, model_width = tokens.shape
+    local_count, _, hidden_width = expert_first.shape
+    hidden = local_count * hidden_width
+    expert_count = routers[2].shape[0]
+    gate_width = -(-expert_count // 128) * 128
+    width = model_width + gate_width
+    total = GRID[0] * GRID[1] * length
+    wide = weights[3].shape[0]
+    narrow = HEADS * HEAD
+    low, full = jnp.bfloat16, jnp.float32
+    shapes = (
+        ((length, width), full),
+        ((hidden, model_width), full),
+        ((hidden, model_width), full),
+        ((length, model_width), full),
+        ((length, model_width), low),
+        ((length, model_width), low),
+        ((length, narrow), low),
+        ((length, narrow), low),
+        ((length, wide), full),
+        ((length, narrow), low),
+        ((HEADS, length, length), full),
+        ((length, narrow), full),
+        ((length, wide), low),
+        ((length, 128), full),
+        ((length, 128), full),
+        ((length, gate_width), full),
+        ((total, model_width), low),
+    )
     vmem = pl.BlockSpec(memory_space=pltpu.VMEM)
     hbm = pl.BlockSpec(memory_space=pl.ANY)
-    low = jnp.bfloat16
-    rows_sum, result, first_sum, second_sum = pl.pallas_call(
-        functools.partial(expert_kernel, model_width, local_count),
-        out_shape=(
-            jax.ShapeDtypeStruct((length, width), jnp.float32),
-            jax.ShapeDtypeStruct((total, model_width), low),
-            jax.ShapeDtypeStruct((wide, model_width), jnp.float32),
-            jax.ShapeDtypeStruct((wide, model_width), jnp.float32),
-        ),
-        in_specs=[vmem, hbm, vmem, vmem],
-        out_specs=(vmem, hbm, vmem, vmem),
+    sems = pltpu.SemaphoreType.DMA((2, N_SEM))
+    return pl.pallas_call(
+        functools.partial(layer_kernel, local_count),
+        out_shape=tuple(jax.ShapeDtypeStruct(*shape) for shape in shapes),
+        in_specs=[vmem] * 13 + [hbm] * 4,
+        out_specs=(*([vmem] * (len(shapes) - 1)), hbm),
         scratch_shapes=[
+            pltpu.VMEM((128, model_width), low),
+            pltpu.VMEM((128, length), full),
             pltpu.VMEM((total, width), low),
             pltpu.VMEM((total, model_width), low),
-            pltpu.VMEM((model_width, wide), low),
-            pltpu.VMEM((wide, model_width), low),
-            pltpu.VMEM((model_width, wide), low),
-            pltpu.VMEM((total, wide), low),
-            pltpu.VMEM((total, wide), low),
-            pltpu.VMEM((16, 2 * length, width), low),
+            pltpu.VMEM((model_width, hidden), low),
+            pltpu.VMEM((hidden, model_width), low),
+            pltpu.VMEM((model_width, hidden), low),
+            pltpu.VMEM((total, 2 * hidden), low),
+            pltpu.VMEM((total, width), low),
+            pltpu.VMEM((2, 2 * length, model_width), low),
+            pltpu.SemaphoreType.DMA((3 + -(-wide // width) + -(-wide // model_width),)),
+            sems,
+            sems,
+            sems,
+            pltpu.SemaphoreType.DMA((2,)),
             *reduce_scratch(length, width),
-            pltpu.VMEM((2, 2 * length, model_width), low),
-            pltpu.SemaphoreType.DMA((2, N_SEM)),
-            pltpu.SemaphoreType.DMA((2, N_SEM)),
-            pltpu.SemaphoreType.DMA((2,)),
-            pltpu.SemaphoreType.DMA,
         ],
         compiler_params=pltpu.CompilerParams(
-            collective_id=0, has_side_effects=True, vmem_limit_bytes=62 * 2**20
+            collective_id=0, has_side_effects=True, vmem_limit_bytes=VMEM_LIMIT
         ),
-        name="experts",
-    )(packed, upstream, expert_first, expert_second.reshape(wide, model_width))
-    first_sum = first_sum.reshape(local_count, hidden_width, model_width).transpose(0, 2, 1)
-    return rows_sum, result, first_sum, second_sum.reshape(expert_second.shape)
+        name="layer",
+    )(
+        tokens,
+        cotangent,
+        *gains,
+        *routers,
+        segments,
+        value_ids.transpose(1, 2, 0),
+        output_ids.transpose(1, 2, 0),
+        ffn_ids.T,
+        expert_first,
+        expert_second.reshape(hidden, model_width),
+        *weights,
+    )
 
 
 def general_body(
@@ -1757,12 +1836,10 @@
     output_ids,
     ffn_ids,
 ):
-    expert_count = expert_router.shape[1]
-    gate_width = -(-expert_count // 128) * 128
     gains = (gain_attention[None], gain_feedforward[None])
     weights = (query_weight, key_weight, value_weight, output_weight)
     routers = (value_router.T, output_router.T, expert_router.T)
-    upstream_rows, packed, *saved = call_attention(
+    rows_sum, first_sum, second_sum, *saved, result = call_layer(
         tokens,
         cotangent,
         gains,
@@ -1772,30 +1849,49 @@
         value_ids[0],
         output_ids[0],
         ffn_ids[0],
-        gate_width,
-    )
-    rows_sum, result, first_sum, second_sum = call_experts(
-        packed, upstream_rows, expert_first, expert_second
+        expert_first,
+        expert_second,
     )
     block_output, stream_grad, low, output_low = call_backward(
         rows_sum, tokens, cotangent, gains, routers, saved, weights, result
     )
-    query_sum, key_sum, value_sum, output_sum, small, expert_small = call_widen(
-        low, output_low, query_weight.shape[1]
-    )
-    router_width = value_router.shape[1]
-    return (
-        block_output,
-        stream_grad,
-        small[GAIN_LANE],
-        small[GAIN_LANE + 1],
+    (
         query_sum,
         key_sum,
         value_sum,
         output_sum,
-        small[:router_width].T,
-        small[OUTPUT_LANE : OUTPUT_LANE + router_width].T,
-        expert_small[:expert_count].T,
+        value_router_sum,
+        output_router_sum,
+        expert_router_sum,
+        gain_attention_sum,
+        gain_feedforward_sum,
+        first_sum,
+        second_sum,
+        block_output,
+        stream_grad,
+    ) = call_widen(
+        low,
+        output_low,
+        first_sum,
+        second_sum,
+        block_output,
+        stream_grad,
+        query_weight.shape[1],
+        expert_router.shape[1],
+        expert_first.shape[0],
+    )
+    return (
+        block_output,
+        stream_grad,
+        gain_attention_sum[0],
+        gain_feedforward_sum[0],
+        query_sum,
+        key_sum,
+        value_sum,
+        output_sum,
+        value_router_sum.T,
+        output_router_sum.T,
+        expert_router_sum.T,
         first_sum,
         second_sum,
     )

time: 320 us -> 309 us (0.966)
  local copies, waits for them, and re-layouts: 13.5 us -> 0 us
  Pallas kernels: 304 us -> 308 us
    unnamed x13 -> x0, local copies, waits for them, and re-layouts: 8.37 us -> none
    pallas_call x1, Pallas kernels: 150 us -> 159 us  [call_backward(): pl.pallas_call(backward_kernel, out_shape=(jax.ShapeDtypeStruct((length,...]
    pallas_call x3 -> x2, Pallas kernels: 154 us -> 149 us  [the longest x1 132 us: call_layer(): pl.pallas_call(functools.partial(layer_kernel, local_count), out_shape=tu...]
where the time goes in v5:
time: 309 us
  Pallas kernels  308 us (100%)
    pallas_call x1, Pallas kernels, call_backward(): pl.pallas_call(backward_kernel, out_shape=(jax.ShapeDtypeStruct((length,...  159 us
    pallas_call x1, Pallas kernels, call_layer(): pl.pallas_call(functools.partial(layer_kernel, local_count), out_shape=tu...  132 us
    pallas_call x1, Pallas kernels, call_widen(): pl.pallas_call(widen_kernel, grid=(steps,), out_shape=(shape(model_width,...  17 us

profile of v5, /device:TPU:1, one launch (start us, length us, event | category | flops | bytes accessed | tf_op | source)
XLA Modules:
  0.0 308.7 jit_solution(5031077535274825419)
XLA Ops:
  0.6 132.2 %layer.1 = (f32[128,1152]{1,0:T(8,128)}, f32[384,1024]{1,0:T(8,128)}, f32[384,1024]{1,0:T(8,128)}, f32[128,1024]{1,0:T(8,128)}, bf16[128,1024]{1,0:T(8,128)(2,1)...) custom-call(bf16[128,1024]{1,0:T(8,128)(2,1)} %tokens_ref.3, ...), custom_call_target="tpu_custom_call" | custom-call | tf_op jit(solution)/shard_map/layer/pallas_call | solution.py:1679
  132.8 158.7 %backward.1 = (bf16[128,1024]{1,0:T(8,128)(2,1)}, f32[128,1024]{1,0:T(8,128)}, bf16[1024,3840]{1,0:T(8,128)(2,1)}, bf16[2560,1024]{1,0:T(8,128)(2,1)}) custom-call(f32[128,1152]{1,0:T(8,128)} %get-tuple-element.47.rows_ref, bf16[128,1024]{1,0:T(8,128)(2,1)} %tokens_ref.3, bf16[128,1024]{1,0:T(8,128)(2,1)} %cotangent_ref.3, f32[1,1024]{1,0:T(1,128)} %bitcast.28, ...), custom_call_target="tpu_custom_call" | custom-call | tf_op jit(solution)/shard_map/backward/pallas_call | solution.py:1098
  291.5 17.0 %widen.1 = (f32[1024,512]{1,0:T(8,128)}, f32[1024,512]{1,0:T(8,128)}, f32[1024,2560]{1,0:T(8,128)}, f32[2560,1024]{1,0:T(8,128)}, f32[20,1024]{1,0:T(8,128)}, /*...) custom-call(bf16[1024,3840]{1,0:T(8,128)(2,1)} %get-tuple-element.62, ...), custom_call_target="tpu_custom_call" | custom-call | tf_op jit(solution)/shard_map/widen/pallas_call | solution.py:1199
